TPU v7x, 1024 devices: a whole 8x8x8 slice. The times are simulated.
1024 devices in a mesh: dp: 8 (over y), tensor: 16 (over z, core), expert: 8 (over x).
Axes of the slice: x: 8, y: 8, z: 8, core: 2. Of those that a mesh axis runs over, the one named last changes fastest.
Arguments:
- grad_out: bfloat16 [8, 8, 256, 4096], P('dp', 'expert', 'tensor'), may hold values from -6 to 6
- routes: int32 [8, 8, 256, 8], P('dp', 'expert'), may hold values from 0 to 63, all different within a row; in each aligned block of 256 rows (0 to 255, 256 to 511, ..., all dimensions but the last counted through in order) at most 48 rows name the same one
- gates: bfloat16 [8, 8, 256, 8], P('dp', 'expert'), may hold values from 0.049804688 to 1
- hidden_saved: bfloat16 [8, 64, 384, 768], P('dp', 'expert'), may hold values from -4 to 4
- w_down: bfloat16 [64, 768, 4096], P('expert', None, 'tensor'), may hold values from -0.09375 to 0.09375
Outputs:
- grad_hidden: bfloat16 [8, 64, 384, 768], P('dp', 'expert', 'tensor')
- grad_gates: float32 [8, 64, 384], P('dp', 'expert', 'tensor')
- grad_weight: bfloat16 [64, 768, 4096], P('expert', 'dp', 'tensor')
Inputs may be any that keep to these rules, and one draw needn't show every extreme that they name: `routes`: within one column of 256 tokens each token names 8 different experts and no expert is named by more than 48 tokens; in every draw some expert is named by exactly 48 tokens of some column.
All inputs are finite; a program needn't handle non-finite values.
Results may differ from a plain program's by a relative error of at most 0.024.
Values may be sent and summed in bfloat16 or wider, within the bound.
No kernel may reach another device: no remote copies, remote signals or barrier semaphores. Data moves between devices by JAX's collectives and lax.ppermute only.
A program may use at most 128 MiB of HBM per device.

v0:
```python
import jax
import jax.numpy as jnp
from jax import lax
from jax.sharding import PartitionSpec as P


def slot_ranks(route_col, experts_all):
    onehot = (
        route_col[:, :, None] == jnp.arange(experts_all, dtype=jnp.int32)[None, None, :]
    ).astype(jnp.int32)
    named = jnp.sum(onehot, axis=1)
    before = jnp.cumsum(named, axis=0) - named
    return jnp.sum(onehot * before[:, None, :], axis=2)


def local(grad_out, routes, gates, hidden_saved, w_down):
    n_tensor = lax.axis_size("tensor")
    n_expert = lax.axis_size("expert")
    local_experts = w_down.shape[0]
    width_block = w_down.shape[2]
    slot_count = hidden_saved.shape[2]
    most_slots = slot_count // n_expert
    experts_all = local_experts * n_expert
    own_slots = slot_count // n_tensor
    choices_count = routes.shape[3]
    column = lax.all_to_all(grad_out[0, 0], "tensor", split_axis=1, concat_axis=0, tiled=True)
    route_col = routes[0, 0]
    gate_col = gates[0, 0]
    ranks = slot_ranks(route_col, experts_all)
    position = route_col * most_slots + ranks
    slot_ids = jnp.arange(experts_all * most_slots, dtype=jnp.int32)
    picker = jnp.zeros((route_col.shape[0], experts_all * most_slots), jnp.bfloat16)
    gate_sum = jnp.zeros((experts_all * most_slots,), jnp.float32)
    for choice_index in range(choices_count):
        onehot = (position[:, choice_index, None] == slot_ids[None, :]).astype(jnp.bfloat16)
        picker = picker + onehot
        gate_sum = gate_sum + jnp.dot(
            gate_col[:, choice_index], onehot, preferred_element_type=jnp.float32
        )
    gate_slots = gate_sum.astype(jnp.bfloat16)
    send_rows = jnp.einsum("cs,cd->sd", picker, column, preferred_element_type=jnp.float32).astype(
        jnp.bfloat16
    )
    send_rows = send_rows.reshape(n_expert, local_experts, most_slots, width_block)
    send_gates = gate_slots.reshape(n_expert, local_experts, most_slots)
    arrived, arrived_gates = (
        lax.all_to_all(send_rows, "expert", split_axis=0, concat_axis=0, tiled=True),
        lax.all_to_all(send_gates, "expert", split_axis=0, concat_axis=0, tiled=True),
    )
    slot_rows = arrived.transpose(1, 0, 2, 3).reshape(local_experts, slot_count, width_block)
    slot_gates = (
        arrived_gates.transpose(1, 0, 2).reshape(local_experts, slot_count).astype(jnp.float32)
    )
    hidden = hidden_saved[0]
    scaled = (slot_gates[:, :, None] * slot_rows).astype(jnp.bfloat16)
    summed = lax.psum_scatter(
        jnp.einsum("xsd,xfd->sxf", slot_rows, w_down, preferred_element_type=jnp.float32).astype(
            jnp.bfloat16
        ),
        "tensor",
        scatter_dimension=0,
        tiled=True,
    ).astype(jnp.float32)
    values = summed.transpose(1, 0, 2)
    first = lax.axis_index("tensor") * own_slots
    my_gates = lax.dynamic_slice_in_dim(slot_gates, first, own_slots, 1)
    my_hidden = lax.dynamic_slice_in_dim(hidden, first, own_slots, 1)
    grad_hidden = (my_gates[:, :, None] * values).astype(jnp.bfloat16)
    grad_gates = jnp.sum(my_hidden.astype(jnp.float32) * values, axis=2)
    grad_hidden, grad_gates = (grad_hidden[None], grad_gates[None])
    partial_grad = jnp.einsum("xsf,xsd->xfd", hidden, scaled, preferred_element_type=jnp.float32)
    partial_grad = lax.optimization_barrier(partial_grad.astype(jnp.bfloat16)).astype(jnp.float32)
    total = lax.psum_scatter(
        partial_grad.astype(jnp.bfloat16), "dp", scatter_dimension=1, tiled=True
    )
    return (grad_hidden, grad_gates, total)


def solution(mesh):
    in_specs = (
        P("dp", "expert", "tensor", None),
        P("dp", "expert", None, None),
        P("dp", "expert", None, None),
        P("dp", "expert", None, None),
        P("expert", None, "tensor"),
    )
    out_specs = (
        P("dp", "expert", "tensor", None),
        P("dp", "expert", "tensor"),
        P("expert", "dp", "tensor"),
    )
    return jax.shard_map(local, mesh=mesh, in_specs=in_specs, out_specs=out_specs, check_vma=False)
```

profile of v0, /device:TPU:1, one launch (start us, length us, event | category | flops | bytes accessed | tf_op | source)
XLA Modules:
  0.0 240.4 jit_solution(12002008524560301521)
XLA Ops:
  7.2 1.1 copy.53
  8.3 0.7 copy.41
  9.0 18.2 %all-to-all-start.1 = ((bf16[16,16,256]{2,0,1:T(8,128)(2,1)}), bf16[16,16,256]{2,0,1:T(8,128)(2,1)S(1)}, u32[]{:S(2)}, u32[]{:S(2)}) async-start(bf16[16,16,256]{2,0,1:T(8,128)(2,1)} %copy.41), calls=%async_computation.1 | async-start | bytes 262144 | tf_op jit(solution)/shard_map/all_to_all | solution.py:26
  27.2 0.8 convert_reduce_fusion
  28.0 0.6 reduce-window.6
  28.6 0.2 slice_reduce_fusion
  28.9 0.8 select_reduce_fusion
  29.7 0.7 multiply_add_fusion
  30.4 1.3 fusion.3
  31.7 1.3 fusion.15
  33.0 1.3 fusion.5
  34.4 0.6 fusion.7
  35.0 0.6 fusion.9
  35.7 0.6 fusion.11
  36.3 0.6 fusion.13
  36.9 0.6 fusion.17
  37.7 0.7 reshape.77
  38.4 6.5 %all-to-all-start = ((bf16[8,2,192]{2,1,0:T(2,128)(2,1)}), bf16[8,2,192]{2,1,0:T(2,128)(2,1)S(1)}, u32[]{:S(2)}, u32[]{:S(2)}) async-start(bf16[8,2,192]{2,1,0:T(2,128)(2,1)} %reshape.77), calls=%async_computation | async-start | bytes 16384 | tf_op jit(solution)/shard_map/all_to_all | solution.py:48
  44.9 4.7 %convolution_convert_fusion = bf16[3072,256]{1,0:T(8,128)(2,1)} fusion(bf16[256,256]{1,0:T(8,128)(2,1)S(1)} %bitcast.87, s32[256]{0:T(256)S(1)} %bitcast.102, s32[256]{0:T(256)S(1)} %bitcast.104, s32[256]{0:T(256)S(1)} %bitcast.106, s32[256]{0:T(256)S(1)} %bitcast.108, s32[256]{0:T(256)S(1)} %bitcast.110, s32[256]{0:T(256)S(1)} %bitcast.112, ...), kind=kOutput, calls=%fused_computation.3 | convolution fusion | flops 428605440 | bytes 1712128 | tf_op jit(solution)/shard_map/cs,cd->sd/dot_general | solution.py:41
  49.6 1.9 all-to-all-done
  51.5 4.7 %all-to-all-start.2 = ((bf16[8,8,48,256]{3,2,1,0:T(8,128)(2,1)}), bf16[8,8,48,256]{3,2,1,0:T(8,128)(2,1)}, u32[]{:S(2)}, u32[]{:S(2)}) async-start(bf16[8,8,48,256]{3,2,1,0:T(8,128)(2,1)} %bitcast.83), calls=%async_computation.2 | async-start | bytes 3145728 | tf_op jit(solution)/shard_map/all_to_all | solution.py:47
  56.5 38.1 %all-to-all-done.2 = bf16[8,8,48,256]{3,2,1,0:T(8,128)(2,1)} async-done(((bf16[8,8,48,256]{3,2,1,0:T(8,128)(2,1)}), bf16[8,8,48,256]{3,2,1,0:T(8,128)(2,1)}, u32[]{:S(2)}, u32[]{:S(2)}) %all-to-all-start.2) | async-done | bytes 1572896 | tf_op jit(solution)/shard_map/all_to_all | solution.py:47
  94.6 1.5 copy.42
  96.2 1.1 copy-done.1
  97.3 6.0 %convert_bitcast_fusion.1 = bf16[8,768,256]{1,2,0:T(8,128)(2,1)} fusion(bf16[1,8,384,768]{3,2,1,0:T(8,128)(2,1)} %param.8, bf16[8,384,256]{2,1,0:T(8,128)(2,1)S(1)} %bitcast.81, f32[8,384]{1,0:T(8,128)S(1)} %reshape.48), kind=kOutput, calls=%fused_computation.4 | convolution fusion | flops 1211891712 | bytes 9449472 | tf_op jit(solution)/shard_map/xsf,xsd->xfd/dot_general | solution.py:71
  103.3 5.1 %copy.44 = bf16[8,768,256]{2,0,1:T(8,128)(2,1)} copy(bf16[8,768,256]{1,2,0:T(8,128)(2,1)} %convert_bitcast_fusion.1) | data formatting | bytes 6291456 | tf_op jit(solution)/shard_map/optimization_barrier | solution.py:72
  108.5 2.8 %convert_bitcast_fusion = bf16[8,48,8,768]{3,2,1,0:T(8,128)(2,1)S(1)} fusion(bf16[8,384,256]{2,1,0:T(8,128)(2,1)} %bitcast.82, bf16[8,768,256]{2,1,0:T(8,128)(2,1)S(1)} %copy-done), kind=kOutput, calls=%fused_computation.2 | convolution fusion | flops 1210318848 | bytes 9437184 | tf_op jit(solution)/shard_map/xsd,xfd->sxf/dot_general | solution.py:57
  111.3 2.7 %copy.52 = bf16[8,48,8,768]{3,2,0,1:T(8,128)(2,1)} copy(bf16[8,48,8,768]{3,2,1,0:T(8,128)(2,1)S(1)} %convert_bitcast_fusion) | data formatting | bytes 9437184
  114.2 42.3 %reduce-scatter.5.cloned.1.call-done = bf16[8,96,256]{2,0,1:T(8,128)(2,1)} async-done(((bf16[8,768,256]{2,0,1:T(8,128)(2,1)}), bf16[8,96,256]{2,0,1:T(8,128)(2,1)}) %reduce-scatter.5.cloned.1.call-update) | async-done | bytes 393232 | tf_op jit(solution)/shard_map/reduce_scatter | solution.py:73
  156.5 1.8 copy.45
  158.3 72.7 %reduce-scatter.7.cloned.1.call-done = bf16[24,6144]{1,0:T(8,128)(2,1)} async-done(((bf16[384,6144]{1,0:T(8,128)(2,1)}), bf16[24,6144]{1,0:T(8,128)(2,1)}) %reduce-scatter.7.cloned.1.call-update) | async-done | bytes 294928
  231.0 2.5 %fusion.52 = (f32[8,24]{1,0:T(8,128)}, bf16[1,8,24,768]{3,2,1,0:T(8,128)(2,1)}) fusion(bf16[1,8,384,768]{3,2,1,0:T(8,128)(2,1)} %param.8, s32[]{:T(128)S(6)} %select_n.4, bf16[3,8,8,768]{3,2,1,0:T(8,128)(2,1)} %bitcast.85, f32[8,24]{1,0:T(8,128)S(1)} %constant_dynamic-slice_fusion), kind=kLoop, calls=%fused_computation.55 | loop fusion | flops 884544 | bytes 886276 | tf_op jit(solution)/shard_map/reduce_sum | solution.py:69
  (22 shorter events, 0.6 us)
Async XLA Ops:
  7.2 101.3 %copy-start = (bf16[8,768,256]{2,1,0:T(8,128)(2,1)S(1)}, bf16[8,768,256]{2,1,0:T(8,128)(2,1)}, u32[]{:S(2)}) copy-start(bf16[8,768,256]{2,1,0:T(8,128)(2,1)} %param.9) | copy-start | bytes 9437188
  7.2 27.2 %copy-start.2 = (bf16[1,1,256,8]{2,3,1,0:T(8,128)(2,1)S(1)}, bf16[1,1,256,8]{2,3,1,0:T(8,128)(2,1)}, u32[]{:S(2)}) copy-start(bf16[1,1,256,8]{2,3,1,0:T(8,128)(2,1)} %param.7) | copy-start | bytes 12292
  9.0 29.4 %all-to-all-start.1 = ((bf16[16,16,256]{2,0,1:T(8,128)(2,1)}), bf16[16,16,256]{2,0,1:T(8,128)(2,1)S(1)}, u32[]{:S(2)}, u32[]{:S(2)}) async-start(bf16[16,16,256]{2,0,1:T(8,128)(2,1)} %copy.41), calls=%async_computation.1 | async-start | bytes 262144 | tf_op jit(solution)/shard_map/all_to_all | solution.py:26
  38.4 13.1 %all-to-all-start = ((bf16[8,2,192]{2,1,0:T(2,128)(2,1)}), bf16[8,2,192]{2,1,0:T(2,128)(2,1)S(1)}, u32[]{:S(2)}, u32[]{:S(2)}) async-start(bf16[8,2,192]{2,1,0:T(2,128)(2,1)} %reshape.77), calls=%async_computation | async-start | bytes 16384 | tf_op jit(solution)/shard_map/all_to_all | solution.py:48
  51.5 43.1 %all-to-all-start.2 = ((bf16[8,8,48,256]{3,2,1,0:T(8,128)(2,1)}), bf16[8,8,48,256]{3,2,1,0:T(8,128)(2,1)}, u32[]{:S(2)}, u32[]{:S(2)}) async-start(bf16[8,8,48,256]{3,2,1,0:T(8,128)(2,1)} %bitcast.83), calls=%async_computation.2 | async-start | bytes 3145728 | tf_op jit(solution)/shard_map/all_to_all | solution.py:47
  56.2 100.2 %reduce-scatter.5.cloned.1.call-start = ((), (), s32[]{:S(2)}) async-start(), calls=%async_computation.5 | async-start | bytes 3538944 | tf_op jit(solution)/shard_map/reduce_scatter | solution.py:73
  96.2 1.1 copy-start.1
  108.4 122.6 %reduce-scatter.7.cloned.1.call-start = ((), (), s32[]{:S(2)}) async-start(), calls=%async_computation.6 | async-start | bytes 5013504
Sparse Core Ops, SparseCore 0:
  108.5 47.8 reduce-scatter.4
  159.9 71.0 reduce-scatter.6
where the time goes:
time: 243 us; the launch traced here: 240 us
  waiting for transfers between devices  155 us (64%)
  starting transfers between devices  29.5 us (12%)
  matrix products  20.7 us (9%)
  local copies, waits for them, and re-layouts  15.4 us (6%)
  between operations  14.1 us (6%)
  other arithmetic  5.52 us (2%)
    unnamed x3, waiting for transfers between devices  72.8 us
    reduce_scatter x1, waiting for transfers between devices, local(): lax.psum_scatter(partial_grad.astype(jnp.bfloat16), 'dp', scatter_dimensi...  42.3 us
    all_to_all x1, waiting for transfers between devices, local(): lax.all_to_all(send_rows, 'expert', split_axis=0, concat_axis=0, tiled=True)  38.1 us
    all_to_all x1, starting transfers between devices, local(): lax.all_to_all(grad_out[0, 0], 'tensor', split_axis=1, concat_axis=0, til...  18.2 us
    unnamed x11, local copies, waits for them, and re-layouts  7.58 us
    dot_general x8, matrix products, local(): jnp.dot(gate_col[:, choice_index], onehot, preferred_element_type=jnp.flo...  7.21 us
    all_to_all x1, starting transfers between devices, local(): lax.all_to_all(send_gates, 'expert', split_axis=0, concat_axis=0, tiled=T...  6.5 us
    dot_general x1, matrix products, local(): jnp.einsum('xsf,xsd->xfd', hidden, scaled, preferred_element_type=jnp.flo...  5.98 us
  transfers between devices with their start and end apart: 5, of which 4 were waited for; matrix products, arithmetic and copies ran while one was open for 10% of the time, Pallas kernels for 0%

commit v1 on v0

v1 whole, which is shorter than its diff:
```python
import functools

import jax
import jax.numpy as jnp
from jax import lax
from jax.experimental import pallas as pl
from jax.experimental.pallas import tpu as pltpu
from jax.sharding import PartitionSpec as P

BF = jnp.bfloat16
F32 = jnp.float32


def iota(shape, dim):
    return lax.broadcasted_iota(jnp.int32, shape, dim)


def tables(arr_ref, columns, first, experts, tokens, choices):
    expert_of = (first + iota((experts, tokens), 0)).astype(F32)
    named, gates = [], []
    for c in columns:
        meta = arr_ref[c, tokens : tokens + 2 * choices, :].astype(F32)
        hit_any = jnp.zeros((experts, tokens), F32)
        gate = jnp.zeros((experts, tokens), F32)
        for k in range(choices):
            hit = meta[k : k + 1, :] == expert_of
            hit_any = jnp.where(hit, 1.0, hit_any)
            gate = jnp.where(hit, meta[choices + k : choices + k + 1, :], gate)
        named.append(hit_any)
        gates.append(gate)
    named = jnp.concatenate(named, 0)
    before = (iota((tokens, tokens), 0) < iota((tokens, tokens), 1)).astype(F32).astype(BF)
    rank = jnp.dot(named.astype(BF), before, preferred_element_type=F32)
    table = jnp.where(named > 0, rank, -1.0)
    return [table[i * experts : (i + 1) * experts] for i in range(len(gates))], gates


def picker(table, gate, base, slots, experts, tokens):
    rank = (base + iota((slots, tokens), 0)).astype(F32)
    rows = []
    for x in range(experts):
        value = 1.0 if gate is None else gate[x : x + 1, :]
        rows.append(jnp.where(table[x : x + 1, :] == rank, value, 0.0))
    return jnp.concatenate(rows, 0)


def weight_kernel(place, arr_ref, hidden_ref, out_ref, scaled, *, dims):
    experts, columns, tokens, choices, most = dims
    step = pl.program_id(0)

    @pl.when(step == 0)
    def _():
        table, gates = tables(arr_ref, range(columns), place[0] * experts, experts, tokens, choices)
        for c in range(columns):
            pick = picker(table[c], gates[c], 0, most, experts, tokens).astype(BF)
            rows = jnp.dot(pick, arr_ref[c, :tokens, :], preferred_element_type=F32).astype(BF)
            for x in range(experts):
                scaled[x, c * most : (c + 1) * most, :] = rows[x * most : (x + 1) * most]

    part = lax.dot_general(
        hidden_ref[0], scaled[step], (((0,), (0,)), ((), ())), preferred_element_type=F32
    )
    out_ref[:, 0] = part.astype(BF).reshape(out_ref.shape[0], out_ref.shape[2], out_ref.shape[3])


def part_kernel(place, arr_ref, other_ref, w_ref, w_other_ref, out_ref, gate_ref, mine, theirs, *, dims):
    experts, columns, tokens, choices, most = dims
    half = most // 2
    step = pl.program_id(0)

    @pl.when(step == 0)
    def _():
        base = place[2] * half
        first = place[0] * experts
        table, _ = tables(arr_ref, range(columns), first, experts, tokens, choices)
        for c in range(columns):
            pick = picker(table[c], None, base, half, experts, tokens).astype(BF)
            for src, dst in ((arr_ref, mine), (other_ref, theirs)):
                rows = jnp.dot(pick, src[c, :tokens, :], preferred_element_type=F32)
                for x in range(experts):
                    dst[x, c * half : (c + 1) * half, :] = rows[x * half : (x + 1) * half]
        own, gates = tables(arr_ref, [place[1]], first, experts, tokens, choices)
        gate = picker(own[0], gates[0], base, half, experts, tokens)
        gate_ref[...] = jnp.broadcast_to(jnp.sum(gate, axis=1, keepdims=True), gate_ref.shape)

    dims_nt = (((1,), (1,)), ((), ()))
    part = lax.dot_general(mine[step].astype(BF), w_ref[0], dims_nt, preferred_element_type=F32)
    part = part + lax.dot_general(
        theirs[step].astype(BF), w_other_ref[0], dims_nt, preferred_element_type=F32
    )
    out_ref[:, 0] = part.astype(BF).reshape(columns, half, part.shape[1])


def finish_kernel(parts_ref, gate_ref, hidden_ref, grad_ref, gates_ref):
    sources, experts, half, width = parts_ref.shape
    values = parts_ref[0].astype(F32)
    for s in range(1, sources):
        values = values + parts_ref[s].astype(F32)
    gate = gate_ref[:, :1].reshape(experts, half, 1)
    grad_ref[...] = (gate * values).astype(BF)
    gates_ref[...] = jnp.sum(hidden_ref[...].astype(F32) * values, axis=2)


def local(grad_out, routes, gates, hidden_saved, w_down):
    n_tensor = lax.axis_size("tensor")
    n_expert = lax.axis_size("expert")
    n_dp = lax.axis_size("dp")
    chips = n_tensor // 2
    experts, width, block = w_down.shape
    slots = hidden_saved.shape[2]
    most = slots // n_expert
    half = most // 2
    tokens, choices = routes.shape[2:]
    own = grad_out.shape[2]
    dims = (experts, n_expert, tokens, choices, most)
    me = lax.axis_index("tensor")
    place = jnp.stack([lax.axis_index("expert"), me // 2, me % 2]).astype(jnp.int32)
    pair = [(i, i ^ 1) for i in range(n_tensor)]
    params = functools.partial(pltpu.CompilerParams, vmem_limit_bytes=32 * 1024 * 1024)

    w_other = lax.ppermute(w_down, "tensor", pair)
    first = me * (slots // n_tensor)
    my_hidden = lax.dynamic_slice_in_dim(hidden_saved[0], first, slots // n_tensor, 1)

    send = grad_out[0, 0].reshape(own, n_tensor, block).transpose(1, 0, 2)
    column = lax.all_to_all(send, "tensor", 0, 0, tiled=True).reshape(tokens, block)
    packed = jnp.concatenate([column, routes[0, 0].T.astype(BF), gates[0, 0].T], 0)
    packed = jnp.broadcast_to(packed[None], (n_expert,) + packed.shape)
    arr = lax.all_to_all(packed, "expert", 0, 0, tiled=True)
    other = lax.ppermute(arr, "tensor", pair)

    rows_all = arr.shape[1]
    whole = lambda *shape: pl.BlockSpec(shape, lambda x, p: (0,) * len(shape))
    per_expert = lambda *shape: pl.BlockSpec((1,) + shape, lambda x, p: (x, 0, 0))
    block_f = width // n_dp
    partial = pl.pallas_call(
        functools.partial(weight_kernel, dims=dims),
        out_shape=jax.ShapeDtypeStruct((n_dp, experts, block_f, block), BF),
        grid_spec=pltpu.PrefetchScalarGridSpec(
            num_scalar_prefetch=1,
            grid=(experts,),
            in_specs=[whole(n_expert, rows_all, block), per_expert(slots, width)],
            out_specs=pl.BlockSpec((n_dp, 1, block_f, block), lambda x, p: (0, x, 0, 0)),
            scratch_shapes=[pltpu.VMEM((experts, slots, block), BF)],
        ),
        compiler_params=params(),
        name="weight_part",
    )(place, arr, hidden_saved[0])
    total = lax.psum_scatter(partial, "dp", scatter_dimension=0, tiled=True)[0]

    arr_after, _ = lax.optimization_barrier((arr, partial))
    parts, gate_col = pl.pallas_call(
        functools.partial(part_kernel, dims=dims),
        out_shape=(
            jax.ShapeDtypeStruct((n_expert, experts, half, width), BF),
            jax.ShapeDtypeStruct((experts * half, 128), F32),
        ),
        grid_spec=pltpu.PrefetchScalarGridSpec(
            num_scalar_prefetch=1,
            grid=(experts,),
            in_specs=[
                whole(n_expert, rows_all, block),
                whole(n_expert, rows_all, block),
                per_expert(width, block),
                per_expert(width, block),
            ],
            out_specs=(
                pl.BlockSpec((n_expert, 1, half, width), lambda x, p: (0, x, 0, 0)),
                whole(experts * half, 128),
            ),
            scratch_shapes=[pltpu.VMEM((experts, slots // 2, block), F32)] * 2,
        ),
        compiler_params=params(),
        name="hidden_part",
    )(place, arr_after, other, w_down, w_other)
    same_core = [[2 * z + c for z in range(chips)] for c in range(2)]
    parts = lax.all_to_all(parts, "tensor", 0, 0, tiled=True, axis_index_groups=same_core)
    grad_hidden, grad_gates = pl.pallas_call(
        finish_kernel,
        out_shape=(
            jax.ShapeDtypeStruct((experts, half, width), BF),
            jax.ShapeDtypeStruct((experts, half), F32),
        ),
        in_specs=[pl.BlockSpec(memory_space=pltpu.VMEM)] * 3,
        out_specs=(pl.BlockSpec(memory_space=pltpu.VMEM),) * 2,
        compiler_params=params(),
        name="finish",
    )(parts, gate_col, my_hidden)
    return grad_hidden[None], grad_gates[None], total


def solution(mesh):
    in_specs = (
        P("dp", "expert", "tensor", None),
        P("dp", "expert", None, None),
        P("dp", "expert", None, None),
        P("dp", "expert", None, None),
        P("expert", None, "tensor"),
    )
    out_specs = (
        P("dp", "expert", "tensor", None),
        P("dp", "expert", "tensor"),
        P("expert", "dp", "tensor"),
    )
    return jax.shard_map(local, mesh=mesh, in_specs=in_specs, out_specs=out_specs, check_vma=False)
```

time: 243 us -> 170 us (0.70)
  waiting for transfers between devices: 155 us -> 95.8 us
  matrix products: 20.7 us -> 0 us
  Pallas kernels: 0 us -> 15.2 us
  local copies, waits for them, and re-layouts: 15.4 us -> 10 us
  other arithmetic: 5.52 us -> 1.47 us
  starting transfers between devices: 29.5 us -> 32.8 us
    unnamed x3 -> x1, waiting for transfers between devices: 72.8 us -> 0.02 us
    all_to_all x3, waiting for transfers between devices: 40 us -> 93.4 us  [the longest x1 56.3 us: local(): lax.all_to_all(parts, 'tensor', 0, 0, tiled=True, axis_index_groups=same_...]
    reduce_scatter x1, waiting for transfers between devices: 42.3 us -> 0.01 us  [local(): total = lax.psum_scatter(partial, 'dp', scatter_dimension=0, tiled=True)[0]]
    dot_general x11 -> x0, matrix products: 20.7 us -> none  [the longest x8 7.21 us: local(): jnp.dot(gate_col[:, choice_index], onehot, preferred_element_type=jnp.flo...]
    pallas_call x0 -> x3, Pallas kernels: none -> 15.2 us  [the longest x1 7.6 us: local(): pl.pallas_call(functools.partial(part_kernel, dims=dims), out_shape=(jax....]
    optimization_barrier x1 -> x0, local copies, waits for them, and re-layouts: 5.12 us -> none  [local(): lax.optimization_barrier(partial_grad.astype(jnp.bfloat16))]
    ppermute x0 -> x2, starting transfers between devices: none -> 4.32 us  [the longest x1 2.39 us: local(): other = lax.ppermute(arr, 'tensor', pair)]
    reduce_sum x3 -> x0, other arithmetic: 4.06 us -> none  [the longest x1 2.53 us: local(): grad_gates = jnp.sum(my_hidden.astype(jnp.float32) * values, axis=2)]
  transfers between devices with their start and end apart: 5 -> 6, of which waited for: 4 -> 4; matrix products, arithmetic and copies ran while one was open for 10% -> 1% of each run, Pallas kernels for 0% -> 9%
where the time goes in v1:
time: 170 us; the launch traced here: 169 us
  waiting for transfers between devices  95.8 us (56%)
  starting transfers between devices  32.8 us (19%)
  Pallas kernels  15.2 us (9%)
  between operations  14.1 us (8%)
  local copies, waits for them, and re-layouts  10 us (6%)
    all_to_all x1, waiting for transfers between devices, local(): lax.all_to_all(parts, 'tensor', 0, 0, tiled=True, axis_index_groups=same_...  56.3 us
    all_to_all x1, waiting for transfers between devices, local(): arr = lax.all_to_all(packed, 'expert', 0, 0, tiled=True)  28.6 us
    all_to_all x1, starting transfers between devices, local(): lax.all_to_all(send, 'tensor', 0, 0, tiled=True).reshape(tokens, block)  18.2 us
    all_to_all x1, waiting for transfers between devices, local(): lax.all_to_all(send, 'tensor', 0, 0, tiled=True).reshape(tokens, block)  8.47 us
    pallas_call x1, Pallas kernels, local(): pl.pallas_call(functools.partial(part_kernel, dims=dims), out_shape=(jax....  7.6 us
    unnamed x11, local copies, waits for them, and re-layouts  7.25 us
    all_to_all x1, starting transfers between devices, local(): arr = lax.all_to_all(packed, 'expert', 0, 0, tiled=True)  6.48 us
    pallas_call x1, Pallas kernels, local(): pl.pallas_call(functools.partial(weight_kernel, dims=dims), out_shape=jax...  6.38 us
  transfers between devices with their start and end apart: 6, of which 4 were waited for; matrix products, arithmetic and copies ran while one was open for 1% of the time, Pallas kernels for 9%

profile of v1, /device:TPU:1, one launch (start us, length us, event | category | flops | bytes accessed | tf_op | source)
XLA Modules:
  0.0 169.3 jit_solution(2146308333186573902)
XLA Ops:
  7.2 0.9 copy.10
  8.1 0.7 copy.9
  8.8 18.2 %all-to-all-start = ((bf16[16,16,256]{2,1,0:T(8,128)(2,1)}), bf16[16,16,256]{2,1,0:T(8,128)(2,1)S(1)}, u32[]{:S(2)}, u32[]{:S(2)}) async-start(bf16[16,16,256]{2,1,0:T(8,128)(2,1)} %copy.9), calls=%async_computation | async-start | bytes 262144 | tf_op jit(solution)/shard_map/all_to_all | solution.py:126
  27.0 0.7 convert_bitcast_fusion
  27.7 8.5 %all-to-all-done = bf16[16,16,256]{2,1,0:T(8,128)(2,1)S(1)} async-done(((bf16[16,16,256]{2,1,0:T(8,128)(2,1)}), bf16[16,16,256]{2,1,0:T(8,128)(2,1)S(1)}, u32[]{:S(2)}, u32[]{:S(2)}) %all-to-all-start) | async-done | bytes 131104 | tf_op jit(solution)/shard_map/all_to_all | solution.py:126
  36.2 0.7 pad_maximum_fusion
  36.9 1.1 broadcast_in_dim.12
  37.9 6.5 %all-to-all-start.1 = ((bf16[8,272,256]{2,1,0:T(8,128)(2,1)}), bf16[8,272,256]{2,1,0:T(8,128)(2,1)S(1)}, u32[]{:S(2)}, u32[]{:S(2)}) async-start(bf16[8,272,256]{2,1,0:T(8,128)(2,1)} %broadcast_in_dim.12), calls=%async_computation.1 | async-start | bytes 2228224 | tf_op jit(solution)/shard_map/all_to_all | solution.py:129
  44.4 0.0 reduce-scatter.2.cloned.1.call-start
  44.5 1.9 %collective-permute-start.1 = (bf16[8,768,256]{2,1,0:T(8,128)(2,1)}, bf16[8,768,256]{2,1,0:T(8,128)(2,1)}, u32[]{:S(2)}, u32[]{:S(2)}) collective-permute-start(bf16[8,768,256]{2,1,0:T(8,128)(2,1)} %w_ref.1), channel_id=1, source_target_pairs={{0,8},{8,0},{16,24},{24,16},{32,40},{40,32},{48,56},{56,48},{64,72... | collective-permute-start | bytes 9437192 | tf_op jit(solution)/shard_map/ppermute | solution.py:121
  46.4 0.1 pad_add_fusion.place
  46.5 28.6 %all-to-all-done.1.arr_ref = bf16[8,272,256]{2,1,0:T(8,128)(2,1)S(1)} async-done(((bf16[8,272,256]{2,1,0:T(8,128)(2,1)}), bf16[8,272,256]{2,1,0:T(8,128)(2,1)S(1)}, u32[]{:S(2)}, u32[]{:S(2)}) %all-to-all-start.1) | async-done | bytes 1114144 | tf_op jit(solution)/shard_map/all_to_all | solution.py:129
  75.1 0.0 copy-start
  75.1 2.3 %copy-done = bf16[1,8,384,768]{3,2,1,0:T(8,128)(2,1)S(1)} copy-done((bf16[1,8,384,768]{3,2,1,0:T(8,128)(2,1)S(1)}, bf16[1,8,384,768]{3,2,1,0:T(8,128)(2,1)}, u32[]{:S(2)}) %copy-start) | copy-done | bytes 4718616
  77.5 6.4 %weight_part.1 = bf16[8,8,96,256]{3,2,1,0:T(8,128)(2,1)} custom-call(s32[3]{0:T(128)S(1)} %pad_add_fusion.place, bf16[8,272,256]{2,1,0:T(8,128)(2,1)S(1)} %all-to-all-done.1.arr_ref, bf16[8,384,768]{2,1,0:T(8,128)(2,1)S(1)} %bitcast.23), custom_call_target="tpu_custom_call" | custom-call | tf_op jit(solution)/shard_map/weight_part/pallas_call | solution.py:136
  83.8 0.0 reduce-scatter.2.cloned.1.call-update
  83.9 2.4 %collective-permute-start = (bf16[8,272,256]{2,1,0:T(8,128)(2,1)S(1)}, bf16[8,272,256]{2,1,0:T(8,128)(2,1)S(1)}, u32[]{:S(2)}, u32[]{:S(2)}) collective-permute-start(bf16[8,272,256]{2,1,0:T(8,128)(2,1)S(1)} %all-to-all-done.1.arr_ref), channel_id=1, source_target_pairs={{0,8},{8,0},{16,24},{24,16},{32,40},{40,32},{48,56},{56,48},{64,72... | collective-permute-start | bytes 3342344 | tf_op jit(solution)/shard_map/ppermute | solution.py:130
  86.3 0.0 collective-permute-done.1.w_other_ref
  86.3 2.3 %collective-permute-done.other_ref = bf16[8,272,256]{2,1,0:T(8,128)(2,1)S(1)} collective-permute-done((bf16[8,272,256]{2,1,0:T(8,128)(2,1)S(1)}, bf16[8,272,256]{2,1,0:T(8,128)(2,1)S(1)}, u32[]{:S(2)}, u32[]{:S(2)}) %collective-permute-start) | collective-permute-done | bytes 1114144 | tf_op jit(solution)/shard_map/ppermute | solution.py:130
  88.6 0.0 copy-start.1
  88.6 1.9 %copy-done.1 = bf16[8,768,256]{2,1,0:T(8,128)(2,1)S(1)} copy-done((bf16[8,768,256]{2,1,0:T(8,128)(2,1)S(1)}, bf16[8,768,256]{2,1,0:T(8,128)(2,1)}, u32[]{:S(2)}) %copy-start.1) | copy-done | bytes 3145752
  90.5 7.6 %hidden_part.1 = (bf16[8,8,24,768]{3,2,1,0:T(8,128)(2,1)S(1)}, f32[192,128]{1,0:T(8,128)S(1)}) custom-call(s32[3]{0:T(128)S(1)} %pad_add_fusion.place, bf16[8,272,256]{2,1,0:T(8,128)(2,1)S(1)} %all-to-all-done.1.arr_ref, bf16[8,272,256]{2,1,0:T(8,128)(2,1)S(1)} %collective-permute-done.other_ref, bf16[8,768,256]{2,1,0:T(8,128)(2,1)S(1)} %copy-done.1, ...), custom_call_target="tpu_custom_call" | custom-call | tf_op jit(solution)/shard_map/hidden_part/pallas_call | solution.py:152
  98.1 0.0 copy-start.2
  98.1 1.4 copy-done.2
  99.6 0.0 copy-start.3
  99.6 0.6 copy-done.3
  100.2 0.0 copy-start.4
  100.2 3.7 %all-to-all-start.2 = ((bf16[8,8,24,768]{3,2,1,0:T(8,128)(2,1)}), bf16[8,8,24,768]{3,2,1,0:T(8,128)(2,1)S(1)}, u32[]{:S(2)}, u32[]{:S(2)}) async-start(bf16[8,8,24,768]{3,2,1,0:T(8,128)(2,1)} %copy-done.2), calls=%async_computation.2 | async-start | bytes 4718592 | tf_op jit(solution)/shard_map/all_to_all | solution.py:177
  104.0 1.0 dynamic-slice_bitcast_fusion.hidden_ref
  105.0 56.3 %all-to-all-done.2.parts_ref = bf16[8,8,24,768]{3,2,1,0:T(8,128)(2,1)S(1)} async-done(((bf16[8,8,24,768]{3,2,1,0:T(8,128)(2,1)}), bf16[8,8,24,768]{3,2,1,0:T(8,128)(2,1)S(1)}, u32[]{:S(2)}, u32[]{:S(2)}) %all-to-all-start.2) | async-done | bytes 2359328 | tf_op jit(solution)/shard_map/all_to_all | solution.py:177
  161.3 0.0 copy-done.4
  161.3 1.2 finish.1
  (1 shorter events, 0.0 us)
Async XLA Ops:
  8.8 27.4 %all-to-all-start = ((bf16[16,16,256]{2,1,0:T(8,128)(2,1)}), bf16[16,16,256]{2,1,0:T(8,128)(2,1)S(1)}, u32[]{:S(2)}, u32[]{:S(2)}) async-start(bf16[16,16,256]{2,1,0:T(8,128)(2,1)} %copy.9), calls=%async_computation | async-start | bytes 262144 | tf_op jit(solution)/shard_map/all_to_all | solution.py:126
  37.9 37.2 %all-to-all-start.1 = ((bf16[8,272,256]{2,1,0:T(8,128)(2,1)}), bf16[8,272,256]{2,1,0:T(8,128)(2,1)S(1)}, u32[]{:S(2)}, u32[]{:S(2)}) async-start(bf16[8,272,256]{2,1,0:T(8,128)(2,1)} %broadcast_in_dim.12), calls=%async_computation.1 | async-start | bytes 2228224 | tf_op jit(solution)/shard_map/all_to_all | solution.py:129
  44.4 118.0 %reduce-scatter.2.cloned.1.call-start = ((), (), s32[]{:S(2)}) async-start(), calls=%async_computation.4 | async-start | bytes 3538944 | tf_op jit(solution)/shard_map/reduce_scatter | solution.py:149
  44.5 41.8 %collective-permute-start.1 = (bf16[8,768,256]{2,1,0:T(8,128)(2,1)}, bf16[8,768,256]{2,1,0:T(8,128)(2,1)}, u32[]{:S(2)}, u32[]{:S(2)}) collective-permute-start(bf16[8,768,256]{2,1,0:T(8,128)(2,1)} %w_ref.1), channel_id=1, source_target_pairs={{0,8},{8,0},{16,24},{24,16},{32,40},{40,32},{48,56},{56,48},{64,72... | collective-permute-start | bytes 9437192 | tf_op jit(solution)/shard_map/ppermute | solution.py:121
  75.1 2.3 %copy-start = (bf16[1,8,384,768]{3,2,1,0:T(8,128)(2,1)S(1)}, bf16[1,8,384,768]{3,2,1,0:T(8,128)(2,1)}, u32[]{:S(2)}) copy-start(bf16[1,8,384,768]{3,2,1,0:T(8,128)(2,1)} %param.8) | copy-start | bytes 14155780
  83.9 4.8 %collective-permute-start = (bf16[8,272,256]{2,1,0:T(8,128)(2,1)S(1)}, bf16[8,272,256]{2,1,0:T(8,128)(2,1)S(1)}, u32[]{:S(2)}, u32[]{:S(2)}) collective-permute-start(bf16[8,272,256]{2,1,0:T(8,128)(2,1)S(1)} %all-to-all-done.1.arr_ref), channel_id=1, source_target_pairs={{0,8},{8,0},{16,24},{24,16},{32,40},{40,32},{48,56},{56,48},{64,72... | collective-permute-start | bytes 3342344 | tf_op jit(solution)/shard_map/ppermute | solution.py:130
  88.6 1.9 %copy-start.1 = (bf16[8,768,256]{2,1,0:T(8,128)(2,1)S(1)}, bf16[8,768,256]{2,1,0:T(8,128)(2,1)}, u32[]{:S(2)}) copy-start(bf16[8,768,256]{2,1,0:T(8,128)(2,1)} %w_ref.1) | copy-start | bytes 9437188
  98.1 1.5 copy-start.2
  99.6 0.6 copy-start.3
  100.2 61.1 %copy-start.4 = (f32[192,128]{1,0:T(8,128)S(1)}, f32[192,128]{1,0:T(8,128)}, u32[]{:S(2)}) copy-start(f32[192,128]{1,0:T(8,128)} %copy-done.3) | copy-start | bytes 294916
  100.2 61.1 %all-to-all-start.2 = ((bf16[8,8,24,768]{3,2,1,0:T(8,128)(2,1)}), bf16[8,8,24,768]{3,2,1,0:T(8,128)(2,1)S(1)}, u32[]{:S(2)}, u32[]{:S(2)}) async-start(bf16[8,8,24,768]{3,2,1,0:T(8,128)(2,1)} %copy-done.2), calls=%async_computation.2 | async-start | bytes 4718592 | tf_op jit(solution)/shard_map/all_to_all | solution.py:177
Sparse Core Ops, SparseCore 0:
  84.0 40.8 reduce-scatter.1

commit v2 on v1

--- a/solution.py
+++ b/solution.py
@@ -15,11 +15,13 @@
     return lax.broadcasted_iota(jnp.int32, shape, dim)
 
 
-def tables(arr_ref, columns, first, experts, tokens, choices):
+def tables(few_ref, columns, core, first, experts, tokens, choices):
     expert_of = (first + iota((experts, tokens), 0)).astype(F32)
+    head = few_ref.shape[1] - 2 * choices
+    n_columns = few_ref.shape[0] // 2
     named, gates = [], []
     for c in columns:
-        meta = arr_ref[c, tokens : tokens + 2 * choices, :].astype(F32)
+        meta = few_ref[core * n_columns + c, head:, :].astype(F32)
         hit_any = jnp.zeros((experts, tokens), F32)
         gate = jnp.zeros((experts, tokens), F32)
         for k in range(choices):
@@ -35,6 +37,12 @@
     return [table[i * experts : (i + 1) * experts] for i in range(len(gates))], gates
 
 
+def column_tokens(many_ref, few_ref, c, core, choices):
+    head = few_ref.shape[1] - 2 * choices
+    few = few_ref[core * (few_ref.shape[0] // 2) + c, :head, :]
+    return jnp.concatenate([many_ref[c], few], 0)
+
+
 def picker(table, gate, base, slots, experts, tokens):
     rank = (base + iota((slots, tokens), 0)).astype(F32)
     rows = []
@@ -44,16 +52,18 @@
     return jnp.concatenate(rows, 0)
 
 
-def weight_kernel(place, arr_ref, hidden_ref, out_ref, scaled, *, dims):
+def weight_kernel(place, many_ref, few_ref, hidden_ref, out_ref, scaled, *, dims):
     experts, columns, tokens, choices, most = dims
     step = pl.program_id(0)
 
     @pl.when(step == 0)
     def _():
-        table, gates = tables(arr_ref, range(columns), place[0] * experts, experts, tokens, choices)
+        first = place[0] * experts
+        table, gates = tables(few_ref, range(columns), place[2], first, experts, tokens, choices)
         for c in range(columns):
             pick = picker(table[c], gates[c], 0, most, experts, tokens).astype(BF)
-            rows = jnp.dot(pick, arr_ref[c, :tokens, :], preferred_element_type=F32).astype(BF)
+            column = column_tokens(many_ref, few_ref, c, place[2], choices)
+            rows = jnp.dot(pick, column, preferred_element_type=F32).astype(BF)
             for x in range(experts):
                 scaled[x, c * most : (c + 1) * most, :] = rows[x * most : (x + 1) * most]
 
@@ -63,23 +73,27 @@
     out_ref[:, 0] = part.astype(BF).reshape(out_ref.shape[0], out_ref.shape[2], out_ref.shape[3])
 
 
-def part_kernel(place, arr_ref, other_ref, w_ref, w_other_ref, out_ref, gate_ref, mine, theirs, *, dims):
+def part_kernel(
+    place, many_ref, other_ref, few_ref, w_ref, w_other_ref, out_ref, gate_ref, mine, theirs, *, dims
+):
     experts, columns, tokens, choices, most = dims
     half = most // 2
     step = pl.program_id(0)
 
     @pl.when(step == 0)
     def _():
-        base = place[2] * half
+        core = place[2]
+        base = core * half
         first = place[0] * experts
-        table, _ = tables(arr_ref, range(columns), first, experts, tokens, choices)
+        table, _ = tables(few_ref, range(columns), core, first, experts, tokens, choices)
         for c in range(columns):
             pick = picker(table[c], None, base, half, experts, tokens).astype(BF)
-            for src, dst in ((arr_ref, mine), (other_ref, theirs)):
-                rows = jnp.dot(pick, src[c, :tokens, :], preferred_element_type=F32)
+            for src, of_core, dst in ((many_ref, core, mine), (other_ref, 1 - core, theirs)):
+                column = column_tokens(src, few_ref, c, of_core, choices)
+                rows = jnp.dot(pick, column, preferred_element_type=F32)
                 for x in range(experts):
                     dst[x, c * half : (c + 1) * half, :] = rows[x * half : (x + 1) * half]
-        own, gates = tables(arr_ref, [place[1]], first, experts, tokens, choices)
+        own, gates = tables(few_ref, [place[1]], core, first, experts, tokens, choices)
         gate = picker(own[0], gates[0], base, half, experts, tokens)
         gate_ref[...] = jnp.broadcast_to(jnp.sum(gate, axis=1, keepdims=True), gate_ref.shape)
 
@@ -116,7 +130,10 @@
     me = lax.axis_index("tensor")
     place = jnp.stack([lax.axis_index("expert"), me // 2, me % 2]).astype(jnp.int32)
     pair = [(i, i ^ 1) for i in range(n_tensor)]
-    params = functools.partial(pltpu.CompilerParams, vmem_limit_bytes=32 * 1024 * 1024)
+    params = pltpu.CompilerParams(vmem_limit_bytes=60 * 1024 * 1024)
+
+    work = 2 * experts * slots * width * block + 2 * n_expert * slots * tokens * block
+    cost = pl.CostEstimate(flops=work, bytes_accessed=2 * w_down.size, transcendentals=0)
 
     w_other = lax.ppermute(w_down, "tensor", pair)
     first = me * (slots // n_tensor)
@@ -124,31 +141,22 @@
 
     send = grad_out[0, 0].reshape(own, n_tensor, block).transpose(1, 0, 2)
     column = lax.all_to_all(send, "tensor", 0, 0, tiled=True).reshape(tokens, block)
-    packed = jnp.concatenate([column, routes[0, 0].T.astype(BF), gates[0, 0].T], 0)
-    packed = jnp.broadcast_to(packed[None], (n_expert,) + packed.shape)
-    arr = lax.all_to_all(packed, "expert", 0, 0, tiled=True)
-    other = lax.ppermute(arr, "tensor", pair)
-
-    rows_all = arr.shape[1]
+    cut = tokens - own
+    few = jnp.concatenate([column[cut:], routes[0, 0].T.astype(BF), gates[0, 0].T], 0)
+    few = jnp.broadcast_to(few[None], (2 * n_expert,) + few.shape)
+    same_chip = [
+        [(2 * z + c) * n_expert + x for c in range(2) for x in range(n_expert)] for z in range(chips)
+    ]
+    few = lax.all_to_all(
+        few, ("tensor", "expert"), 0, 0, tiled=True, axis_index_groups=same_chip
+    )
+    many = lax.all_gather(column[:cut], "expert")
+    many, few = lax.optimization_barrier((many, few))
+    other = lax.ppermute(many, "tensor", pair)
+
     whole = lambda *shape: pl.BlockSpec(shape, lambda x, p: (0,) * len(shape))
     per_expert = lambda *shape: pl.BlockSpec((1,) + shape, lambda x, p: (x, 0, 0))
     block_f = width // n_dp
-    partial = pl.pallas_call(
-        functools.partial(weight_kernel, dims=dims),
-        out_shape=jax.ShapeDtypeStruct((n_dp, experts, block_f, block), BF),
-        grid_spec=pltpu.PrefetchScalarGridSpec(
-            num_scalar_prefetch=1,
-            grid=(experts,),
-            in_specs=[whole(n_expert, rows_all, block), per_expert(slots, width)],
-            out_specs=pl.BlockSpec((n_dp, 1, block_f, block), lambda x, p: (0, x, 0, 0)),
-            scratch_shapes=[pltpu.VMEM((experts, slots, block), BF)],
-        ),
-        compiler_params=params(),
-        name="weight_part",
-    )(place, arr, hidden_saved[0])
-    total = lax.psum_scatter(partial, "dp", scatter_dimension=0, tiled=True)[0]
-
-    arr_after, _ = lax.optimization_barrier((arr, partial))
     parts, gate_col = pl.pallas_call(
         functools.partial(part_kernel, dims=dims),
         out_shape=(
@@ -159,8 +167,9 @@
             num_scalar_prefetch=1,
             grid=(experts,),
             in_specs=[
-                whole(n_expert, rows_all, block),
-                whole(n_expert, rows_all, block),
+                whole(*many.shape),
+                whole(*many.shape),
+                whole(*few.shape),
                 per_expert(width, block),
                 per_expert(width, block),
             ],
@@ -170,9 +179,27 @@
             ),
             scratch_shapes=[pltpu.VMEM((experts, slots // 2, block), F32)] * 2,
         ),
-        compiler_params=params(),
+        compiler_params=params,
+        cost_estimate=cost,
         name="hidden_part",
-    )(place, arr_after, other, w_down, w_other)
+    )(place, many, other, few, w_down, w_other)
+
+    partial = pl.pallas_call(
+        functools.partial(weight_kernel, dims=dims),
+        out_shape=jax.ShapeDtypeStruct((n_dp, experts, block_f, block), BF),
+        grid_spec=pltpu.PrefetchScalarGridSpec(
+            num_scalar_prefetch=1,
+            grid=(experts,),
+            in_specs=[whole(*many.shape), whole(*few.shape), per_expert(slots, width)],
+            out_specs=pl.BlockSpec((n_dp, 1, block_f, block), lambda x, p: (0, x, 0, 0)),
+            scratch_shapes=[pltpu.VMEM((experts, slots, block), BF)],
+        ),
+        compiler_params=params,
+        cost_estimate=cost,
+        name="weight_part",
+    )(place, many, few, hidden_saved[0])
+    total = lax.psum_scatter(partial, "dp", scatter_dimension=0, tiled=True)[0]
+
     same_core = [[2 * z + c for z in range(chips)] for c in range(2)]
     parts = lax.all_to_all(parts, "tensor", 0, 0, tiled=True, axis_index_groups=same_core)
     grad_hidden, grad_gates = pl.pallas_call(
@@ -183,7 +210,7 @@
         ),
         in_specs=[pl.BlockSpec(memory_space=pltpu.VMEM)] * 3,
         out_specs=(pl.BlockSpec(memory_space=pltpu.VMEM),) * 2,
-        compiler_params=params(),
+        compiler_params=pltpu.CompilerParams(vmem_limit_bytes=32 * 1024 * 1024),
         name="finish",
     )(parts, gate_col, my_hidden)
     return grad_hidden[None], grad_gates[None], total

time: 170 us -> 175 us (1.029)
  waiting for transfers between devices: 95.8 us -> 64.9 us
  blocking collectives: 0 us -> 27.2 us
  starting transfers between devices: 32.8 us -> 38.8 us
  Pallas kernels: 15.2 us -> 21.1 us
  local copies, waits for them, and re-layouts: 10 us -> 6.21 us
    all_to_all x1, waiting for transfers between devices: 28.6 us -> 0.01 us  [local(): lax.all_to_all(few, ('tensor', 'expert'), 0, 0, tiled=True, axis_index_gr...]
    all_gather x0 -> x1, blocking collectives: none -> 27.2 us  [local(): many = lax.all_gather(column[:cut], 'expert')]
    ppermute x1, starting transfers between devices: 2.39 us -> 7.95 us  [local(): other = lax.ppermute(many, 'tensor', pair)]
    unnamed x11 -> x9, local copies, waits for them, and re-layouts: 7.25 us -> 3.78 us
    pallas_call x1, Pallas kernels: 6.38 us -> 9.62 us  [local(): pl.pallas_call(functools.partial(weight_kernel, dims=dims), out_shape=jax...]
    pallas_call x1, Pallas kernels: 7.6 us -> 10.4 us  [local(): pl.pallas_call(functools.partial(part_kernel, dims=dims), out_shape=(jax....]
    all_to_all x1, waiting for transfers between devices: 8.47 us -> 6.45 us  [local(): lax.all_to_all(send, 'tensor', 0, 0, tiled=True).reshape(tokens, block)]
  transfers between devices with their start and end apart: 6 -> 6, of which waited for: 4 -> 3; matrix products, arithmetic and copies ran while one was open for 1% -> 2% of each run, Pallas kernels for 9% -> 12%
where the time goes in v2:
time: 175 us; the launch traced here: 174 us
  waiting for transfers between devices  64.9 us (37%)
  starting transfers between devices  38.8 us (22%)
  blocking collectives  27.2 us (16%)
  Pallas kernels  21.1 us (12%)
  between operations  14.1 us (8%)
  local copies, waits for them, and re-layouts  6.21 us (4%)
  other arithmetic  1.95 us (1%)
    all_to_all x1, waiting for transfers between devices, local(): lax.all_to_all(parts, 'tensor', 0, 0, tiled=True, axis_index_groups=same_...  56.3 us
    all_gather x1, blocking collectives, local(): many = lax.all_gather(column[:cut], 'expert')  27.2 us
    all_to_all x1, starting transfers between devices, local(): lax.all_to_all(send, 'tensor', 0, 0, tiled=True).reshape(tokens, block)  18.2 us
    pallas_call x1, Pallas kernels, local(): pl.pallas_call(functools.partial(part_kernel, dims=dims), out_shape=(jax....  10.4 us
    pallas_call x1, Pallas kernels, local(): pl.pallas_call(functools.partial(weight_kernel, dims=dims), out_shape=jax...  9.62 us
    ppermute x1, starting transfers between devices, local(): other = lax.ppermute(many, 'tensor', pair)  7.95 us
    all_to_all x1, starting transfers between devices, local(): lax.all_to_all(few, ('tensor', 'expert'), 0, 0, tiled=True, axis_index_gr...  6.89 us
    all_to_all x1, waiting for transfers between devices, local(): lax.all_to_all(send, 'tensor', 0, 0, tiled=True).reshape(tokens, block)  6.45 us
  transfers between devices with their start and end apart: 6, of which 3 were waited for; matrix products, arithmetic and copies ran while one was open for 2% of the time, Pallas kernels for 12%

profile of v2, /device:TPU:1, one launch (start us, length us, event | category | flops | bytes accessed | tf_op | source)
XLA Modules:
  0.0 174.4 jit_solution(5237770444540301831)
XLA Ops:
  7.2 0.9 copy.10
  8.1 0.7 copy.12
  8.8 18.2 %all-to-all-start = ((bf16[16,16,256]{2,1,0:T(8,128)(2,1)}), bf16[16,16,256]{2,1,0:T(8,128)(2,1)S(1)}, u32[]{:S(2)}, u32[]{:S(2)}) async-start(bf16[16,16,256]{2,1,0:T(8,128)(2,1)} %bitcast.25), calls=%async_computation | async-start | bytes 262144 | tf_op jit(solution)/shard_map/all_to_all | solution.py:143
  27.0 2.0 %collective-permute-start.1 = (bf16[8,768,256]{2,1,0:T(8,128)(2,1)}, bf16[8,768,256]{2,1,0:T(8,128)(2,1)}, u32[]{:S(2)}, u32[]{:S(2)}) collective-permute-start(bf16[8,768,256]{2,1,0:T(8,128)(2,1)} %w_ref.1), channel_id=1, source_target_pairs={{0,8},{8,0},{16,24},{24,16},{32,40},{40,32},{48,56},{56,48},{64,72... | collective-permute-start | bytes 9437192 | tf_op jit(solution)/shard_map/ppermute | solution.py:138
  29.0 0.7 convert_bitcast_fusion
  29.7 6.4 %all-to-all-done = bf16[16,16,256]{2,1,0:T(8,128)(2,1)S(1)} async-done(((bf16[16,16,256]{2,1,0:T(8,128)(2,1)}), bf16[16,16,256]{2,1,0:T(8,128)(2,1)S(1)}, u32[]{:S(2)}, u32[]{:S(2)}) %all-to-all-start) | async-done | bytes 131104 | tf_op jit(solution)/shard_map/all_to_all | solution.py:143
  36.2 0.7 pad_maximum_fusion
  36.9 0.7 broadcast_in_dim.12
  37.6 6.9 %all-to-all-start.1 = ((bf16[16,32,256]{2,1,0:T(8,128)(2,1)}), bf16[16,32,256]{2,1,0:T(8,128)(2,1)S(1)}, u32[]{:S(2)}, u32[]{:S(2)}) async-start(bf16[16,32,256]{2,1,0:T(8,128)(2,1)} %broadcast_in_dim.12), calls=%async_computation.1 | async-start | bytes 524288 | tf_op jit(solution)/shard_map/all_to_all | solution.py:150
  44.5 0.0 reduce-scatter.2.cloned.1.call-start
  44.5 0.6 pad_add_fusion.place
  45.1 27.2 %all_gather.7.many_ref = bf16[8,240,256]{2,1,0:T(8,128)(2,1)} all-gather(bf16[1,240,256]{2,1,0:T(8,128)(2,1)S(1)} %bitcast.28), channel_id=1, replica_groups=mesh['dp'=8,'tensor'=16,'expert'=8] {'expert'}, dimensions={0}, use_global_device_ids=true | all-gather | bytes 1105920 | tf_op jit(solution)/shard_map/all_gather | solution.py:153
  72.3 0.0 all-to-all-done.1.few_ref
  72.3 0.0 copy-start.2
  72.3 0.7 copy-done.2
  73.0 9.6 %weight_part.1 = bf16[8,8,96,256]{3,2,1,0:T(8,128)(2,1)} custom-call(s32[3]{0:T(128)} %pad_add_fusion.place, bf16[8,240,256]{2,1,0:T(8,128)(2,1)} %all_gather.7.many_ref, bf16[16,32,256]{2,1,0:T(8,128)(2,1)} %copy-done.2, bf16[8,384,768]{2,1,0:T(8,128)(2,1)} %bitcast.26), custom_call_target="tpu_custom_call" | custom-call | flops 1610612736 | bytes 3145728 | tf_op jit(solution)/shard_map/weight_part/pallas_call | solution.py:187
  82.6 0.0 copy-start.1
  82.6 0.0 reduce-scatter.2.cloned.1.call-update
  82.6 1.2 copy-done.1
  83.8 8.0 %collective-permute-start = (bf16[8,240,256]{2,1,0:T(8,128)(2,1)S(1)}, bf16[8,240,256]{2,1,0:T(8,128)(2,1)S(1)}, u32[]{:S(2)}, u32[]{:S(2)}) collective-permute-start(bf16[8,240,256]{2,1,0:T(8,128)(2,1)S(1)} %copy-done.1), channel_id=1, source_target_pairs={{0,8},{8,0},{16,24},{24,16},{32,40},{40,32},{48,56},{56,48},{64,72... | collective-permute-start | bytes 2949128 | tf_op jit(solution)/shard_map/ppermute | solution.py:155
  91.8 2.2 %collective-permute-done.other_ref = bf16[8,240,256]{2,1,0:T(8,128)(2,1)S(1)} collective-permute-done((bf16[8,240,256]{2,1,0:T(8,128)(2,1)S(1)}, bf16[8,240,256]{2,1,0:T(8,128)(2,1)S(1)}, u32[]{:S(2)}, u32[]{:S(2)}) %collective-permute-start) | collective-permute-done | bytes 983072 | tf_op jit(solution)/shard_map/ppermute | solution.py:155
  93.9 0.0 copy-start.3
  93.9 0.0 collective-permute-done.1.w_other_ref
  94.0 1.0 copy-done.3
  94.9 10.4 %hidden_part.1 = (bf16[8,8,24,768]{3,2,1,0:T(8,128)(2,1)}, f32[192,128]{1,0:T(8,128)}) custom-call(s32[3]{0:T(128)} %pad_add_fusion.place, bf16[8,240,256]{2,1,0:T(8,128)(2,1)} %all_gather.7.many_ref, bf16[8,240,256]{2,1,0:T(8,128)(2,1)} %copy-done.3, bf16[16,32,256]{2,1,0:T(8,128)(2,1)} %copy-done.2, bf16[8,768,256]{2,1,0:T(8,128)(2,1)} %w_ref.1, ...), custom_call_target="tpu_custom_call" | custom-call | flops 1610612736 | bytes 3145728 | tf_op jit(solution)/shard_map/hidden_part/pallas_call | solution.py:160
  105.3 0.0 copy-start
  105.3 3.8 %all-to-all-start.2 = ((bf16[8,8,24,768]{3,2,1,0:T(8,128)(2,1)}), bf16[8,8,24,768]{3,2,1,0:T(8,128)(2,1)S(1)}, u32[]{:S(2)}, u32[]{:S(2)}) async-start(bf16[8,8,24,768]{3,2,1,0:T(8,128)(2,1)} %get-tuple-element.11), calls=%async_computation.2 | async-start | bytes 4718592 | tf_op jit(solution)/shard_map/all_to_all | solution.py:204
  109.0 1.0 dynamic-slice_bitcast_fusion.hidden_ref
  110.0 56.3 %all-to-all-done.2.parts_ref = bf16[8,8,24,768]{3,2,1,0:T(8,128)(2,1)S(1)} async-done(((bf16[8,8,24,768]{3,2,1,0:T(8,128)(2,1)}), bf16[8,8,24,768]{3,2,1,0:T(8,128)(2,1)S(1)}, u32[]{:S(2)}, u32[]{:S(2)}) %all-to-all-start.2) | async-done | bytes 2359328 | tf_op jit(solution)/shard_map/all_to_all | solution.py:204
  166.3 0.0 copy-done
  166.4 1.2 finish.1
  167.5 0.0 reduce-scatter.2.cloned.1.call-done
  (2 shorter events, 0.0 us)
Async XLA Ops:
  8.8 27.4 %all-to-all-start = ((bf16[16,16,256]{2,1,0:T(8,128)(2,1)}), bf16[16,16,256]{2,1,0:T(8,128)(2,1)S(1)}, u32[]{:S(2)}, u32[]{:S(2)}) async-start(bf16[16,16,256]{2,1,0:T(8,128)(2,1)} %bitcast.25), calls=%async_computation | async-start | bytes 262144 | tf_op jit(solution)/shard_map/all_to_all | solution.py:143
  27.0 67.0 %collective-permute-start.1 = (bf16[8,768,256]{2,1,0:T(8,128)(2,1)}, bf16[8,768,256]{2,1,0:T(8,128)(2,1)}, u32[]{:S(2)}, u32[]{:S(2)}) collective-permute-start(bf16[8,768,256]{2,1,0:T(8,128)(2,1)} %w_ref.1), channel_id=1, source_target_pairs={{0,8},{8,0},{16,24},{24,16},{32,40},{40,32},{48,56},{56,48},{64,72... | collective-permute-start | bytes 9437192 | tf_op jit(solution)/shard_map/ppermute | solution.py:138
  37.6 34.7 %all-to-all-start.1 = ((bf16[16,32,256]{2,1,0:T(8,128)(2,1)}), bf16[16,32,256]{2,1,0:T(8,128)(2,1)S(1)}, u32[]{:S(2)}, u32[]{:S(2)}) async-start(bf16[16,32,256]{2,1,0:T(8,128)(2,1)} %broadcast_in_dim.12), calls=%async_computation.1 | async-start | bytes 524288 | tf_op jit(solution)/shard_map/all_to_all | solution.py:150
  44.5 123.1 %reduce-scatter.2.cloned.1.call-start = ((), (), s32[]{:S(2)}) async-start(), calls=%async_computation.4 | async-start | bytes 3538944 | tf_op jit(solution)/shard_map/reduce_scatter | solution.py:201
  72.3 0.7 copy-start.2
  82.6 1.2 copy-start.1
  83.8 10.1 %collective-permute-start = (bf16[8,240,256]{2,1,0:T(8,128)(2,1)S(1)}, bf16[8,240,256]{2,1,0:T(8,128)(2,1)S(1)}, u32[]{:S(2)}, u32[]{:S(2)}) collective-permute-start(bf16[8,240,256]{2,1,0:T(8,128)(2,1)S(1)} %copy-done.1), channel_id=1, source_target_pairs={{0,8},{8,0},{16,24},{24,16},{32,40},{40,32},{48,56},{56,48},{64,72... | collective-permute-start | bytes 2949128 | tf_op jit(solution)/shard_map/ppermute | solution.py:155
  93.9 1.0 copy-start.3
  105.3 61.1 %copy-start = (f32[192,128]{1,0:T(8,128)S(1)}, f32[192,128]{1,0:T(8,128)}, u32[]{:S(2)}) copy-start(f32[192,128]{1,0:T(8,128)} %get-tuple-element.12.gate_ref) | copy-start | bytes 294916
  105.3 61.1 %all-to-all-start.2 = ((bf16[8,8,24,768]{3,2,1,0:T(8,128)(2,1)}), bf16[8,8,24,768]{3,2,1,0:T(8,128)(2,1)S(1)}, u32[]{:S(2)}, u32[]{:S(2)}) async-start(bf16[8,8,24,768]{3,2,1,0:T(8,128)(2,1)} %get-tuple-element.11), calls=%async_computation.2 | async-start | bytes 4718592 | tf_op jit(solution)/shard_map/all_to_all | solution.py:204
Sparse Core Ops, SparseCore 0:
  82.8 49.4 reduce-scatter.1

commit v3 on v1

v3 whole, which is shorter than its diff:
```python
import functools

import jax
import jax.numpy as jnp
from jax import lax
from jax.experimental import pallas as pl
from jax.experimental.pallas import tpu as pltpu
from jax.sharding import PartitionSpec as P

BF = jnp.bfloat16
F32 = jnp.float32


def iota(shape, dim):
    return lax.broadcasted_iota(jnp.int32, shape, dim)


def tables(meta_ref, columns, first, experts, tokens, choices):
    expert_of = (first + iota((experts, tokens), 0)).astype(F32)
    named, gates = [], []
    for c in range(columns):
        meta = meta_ref[c].astype(F32)
        hit_any = jnp.zeros((experts, tokens), F32)
        gate = jnp.zeros((experts, tokens), F32)
        for k in range(choices):
            hit = meta[k : k + 1, :] == expert_of
            hit_any = jnp.where(hit, 1.0, hit_any)
            gate = jnp.where(hit, meta[choices + k : choices + k + 1, :], gate)
        named.append(hit_any)
        gates.append(gate)
    named = jnp.concatenate(named, 0)
    before = (iota((tokens, tokens), 0) < iota((tokens, tokens), 1)).astype(F32).astype(BF)
    rank = jnp.dot(named.astype(BF), before, preferred_element_type=F32)
    table = jnp.where(named > 0, rank, -1.0)
    return [table[c * experts : (c + 1) * experts] for c in range(columns)], gates


def picker(table, gate, base, slots, experts, tokens):
    rank = (base + iota((slots, tokens), 0)).astype(F32)
    rows = []
    for x in range(experts):
        value = 1.0 if gate is None else gate[x : x + 1, :]
        rows.append(jnp.where(table[x : x + 1, :] == rank, value, 0.0))
    return jnp.concatenate(rows, 0)


def weight_kernel(place, tok_ref, meta_ref, hidden_ref, out_ref, hot_ref, gate_ref, scaled, *, dims):
    experts, columns, tokens, choices, most = dims
    half = most // 2
    step = pl.program_id(0)
    per = hidden_ref.shape[0]

    @pl.when(step == 0)
    def _():
        table, gates = tables(meta_ref, columns, place[0] * experts, experts, tokens, choices)
        for c in range(columns):
            pick = picker(table[c], gates[c], 0, most, experts, tokens).astype(BF)
            rows = jnp.dot(pick, tok_ref[c], preferred_element_type=F32).astype(BF)
            for x in range(experts):
                scaled[x, c * most : (c + 1) * most, :] = rows[x * most : (x + 1) * most]
            base = place[2] * half
            hot_ref[c] = picker(table[c], None, base, half, experts, tokens).astype(BF)

            @pl.when(place[1] == c)
            def _():
                gate = picker(table[c], gates[c], base, half, experts, tokens)
                gate_ref[...] = jnp.broadcast_to(
                    jnp.sum(gate, axis=1, keepdims=True), gate_ref.shape
                )

    for i in range(per):
        part = lax.dot_general(
            hidden_ref[i],
            scaled[step * per + i],
            (((0,), (0,)), ((), ())),
            preferred_element_type=F32,
        )
        n_dp, _, block_f, block = out_ref.shape
        out_ref[:, i] = part.astype(BF).reshape(n_dp, block_f, block)


def part_kernel(
    place, tok_ref, other_ref, hot_ref, w_ref, w_other_ref, keep_ref, near_ref, far_ref, mine, theirs
):
    columns, rows_half, _ = hot_ref.shape
    experts = mine.shape[0]
    half = rows_half // experts
    step = pl.program_id(0)
    per = w_ref.shape[0]

    @pl.when(step == 0)
    def _():
        for c in range(columns):
            for src, dst in ((tok_ref, mine), (other_ref, theirs)):
                rows = jnp.dot(hot_ref[c], src[c], preferred_element_type=F32)
                for x in range(experts):
                    dst[x, c * half : (c + 1) * half, :] = rows[x * half : (x + 1) * half]

    dims_nt = (((1,), (1,)), ((), ()))
    odd = place[1] % 2 == 1
    for i in range(per):
        x = step * per + i
        part = lax.dot_general(mine[x].astype(BF), w_ref[i], dims_nt, preferred_element_type=F32)
        part = part + lax.dot_general(
            theirs[x].astype(BF), w_other_ref[i], dims_nt, preferred_element_type=F32
        )
        part = part.reshape(columns // 2, 2, half, part.shape[1])
        keep_ref[:, i] = jnp.where(odd, part[:, 1], part[:, 0]).astype(BF)
        give = jnp.where(odd, part[:, 0], part[:, 1]).astype(BF)

        @pl.when(x < experts // 2)
        def _():
            near_ref[:, i] = give

        @pl.when(x >= experts // 2)
        def _():
            far_ref[:, i] = give


def add_kernel(keep_ref, near_ref, far_ref, out_ref):
    h = near_ref.shape[1]
    out_ref[:, :h] = (keep_ref[:, :h].astype(F32) + near_ref[...].astype(F32)).astype(BF)
    out_ref[:, h:] = (keep_ref[:, h:].astype(F32) + far_ref[...].astype(F32)).astype(BF)


def finish_kernel(parts_ref, gate_ref, hidden_ref, grad_ref, gates_ref):
    sources, experts, half, width = parts_ref.shape
    values = parts_ref[0].astype(F32)
    for s in range(1, sources):
        values = values + parts_ref[s].astype(F32)
    gate = gate_ref[:, :1].reshape(experts, half, 1)
    grad_ref[...] = (gate * values).astype(BF)
    gates_ref[...] = jnp.sum(hidden_ref[...].astype(F32) * values, axis=2)


def local(grad_out, routes, gates, hidden_saved, w_down):
    n_tensor = lax.axis_size("tensor")
    n_expert = lax.axis_size("expert")
    n_dp = lax.axis_size("dp")
    chips = n_tensor // 2
    experts, width, block = w_down.shape
    slots = hidden_saved.shape[2]
    most = slots // n_expert
    half = most // 2
    tokens, choices = routes.shape[2:]
    own = grad_out.shape[2]
    dims = (experts, n_expert, tokens, choices, most)
    me = lax.axis_index("tensor")
    place = jnp.stack([lax.axis_index("expert"), me // 2, me % 2]).astype(jnp.int32)
    pair = [(i, i ^ 1) for i in range(n_tensor)]
    params = pltpu.CompilerParams(vmem_limit_bytes=50 * 1024 * 1024)

    work = 2 * experts * slots * width * block + 2 * n_expert * slots * tokens * block
    cost = pl.CostEstimate(flops=work, bytes_accessed=2 * w_down.size, transcendentals=0)

    w_other = lax.ppermute(w_down, "tensor", pair)
    first = me * (slots // n_tensor)
    my_hidden = lax.dynamic_slice_in_dim(hidden_saved[0], first, slots // n_tensor, 1)

    meta = jnp.concatenate([routes[0, 0].T.astype(BF), gates[0, 0].T], 0)
    meta, w_other = lax.optimization_barrier((lax.all_gather(meta, "expert"), w_other))
    send = grad_out[0, 0].reshape(own, n_tensor, block).transpose(1, 0, 2)
    send = jnp.broadcast_to(send[None], (n_expert,) + send.shape)
    send = send.reshape(n_expert * n_tensor, own, block)
    tok = lax.all_to_all(send, ("expert", "tensor"), 0, 0, tiled=True)
    tok = tok.reshape(n_expert, tokens, block)
    other = lax.ppermute(tok, "tensor", pair)

    per = 2
    whole = lambda *shape: pl.BlockSpec(shape, lambda x, p: (0,) * len(shape))
    per_expert = lambda *shape: pl.BlockSpec((per,) + shape, lambda x, p: (x, 0, 0))
    block_f = width // n_dp
    partial, hot, gate_col = pl.pallas_call(
        functools.partial(weight_kernel, dims=dims),
        out_shape=(
            jax.ShapeDtypeStruct((n_dp, experts, block_f, block), BF),
            jax.ShapeDtypeStruct((n_expert, experts * half, tokens), BF),
            jax.ShapeDtypeStruct((experts * half, 128), F32),
        ),
        grid_spec=pltpu.PrefetchScalarGridSpec(
            num_scalar_prefetch=1,
            grid=(experts // per,),
            in_specs=[whole(*tok.shape), whole(*meta.shape), per_expert(slots, width)],
            out_specs=(
                pl.BlockSpec((n_dp, per, block_f, block), lambda x, p: (0, x, 0, 0)),
                whole(n_expert, experts * half, tokens),
                whole(experts * half, 128),
            ),
            scratch_shapes=[pltpu.VMEM((experts, slots, block), BF)],
        ),
        compiler_params=params,
        cost_estimate=cost,
        name="weight_part",
    )(place, tok, meta, hidden_saved[0])
    total = lax.psum_scatter(partial, "dp", scatter_dimension=0, tiled=True)[0]

    pairs, near_steps = chips // 2, experts // per // 2
    out_block = (pairs, per, half, width)
    keep, near, far = pl.pallas_call(
        part_kernel,
        out_shape=(
            jax.ShapeDtypeStruct((pairs, experts, half, width), BF),
            jax.ShapeDtypeStruct((pairs, experts // 2, half, width), BF),
            jax.ShapeDtypeStruct((pairs, experts // 2, half, width), BF),
        ),
        grid_spec=pltpu.PrefetchScalarGridSpec(
            num_scalar_prefetch=1,
            grid=(experts // per,),
            in_specs=[
                whole(*tok.shape),
                whole(*tok.shape),
                whole(*hot.shape),
                per_expert(width, block),
                per_expert(width, block),
            ],
            out_specs=(
                pl.BlockSpec(out_block, lambda x, p: (0, x, 0, 0)),
                pl.BlockSpec(out_block, lambda x, p: (0, jnp.minimum(x, near_steps - 1), 0, 0)),
                pl.BlockSpec(out_block, lambda x, p: (0, jnp.maximum(x - near_steps, 0), 0, 0)),
            ),
            scratch_shapes=[pltpu.VMEM((experts, slots // 2, block), F32)] * 2,
        ),
        compiler_params=params,
        cost_estimate=cost,
        name="hidden_part",
    )(place, tok, other, hot, w_down, w_other)

    def swap(shift):
        at = lambda z: (z ^ 1) if shift == 0 else ((((z + 1) % chips) ^ 1) - 1) % chips
        return [(2 * z + c, 2 * at(z) + c) for z in range(chips) for c in range(2)]

    near = lax.ppermute(near, "tensor", swap(0))
    far = lax.ppermute(far, "tensor", swap(1))
    row = lambda n: pl.BlockSpec((1, n, half, width), lambda m: (m, 0, 0, 0))
    parts = pl.pallas_call(
        add_kernel,
        out_shape=jax.ShapeDtypeStruct(keep.shape, BF),
        grid=(pairs,),
        in_specs=[row(experts), row(experts // 2), row(experts // 2)],
        out_specs=row(experts),
        compiler_params=params,
        name="pair_sum",
    )(keep, near, far)
    same_kind = [
        [2 * (2 * m + p) + c for m in range(pairs)] for p in range(2) for c in range(2)
    ]
    parts = lax.all_to_all(parts, "tensor", 0, 0, tiled=True, axis_index_groups=same_kind)
    grad_hidden, grad_gates = pl.pallas_call(
        finish_kernel,
        out_shape=(
            jax.ShapeDtypeStruct((experts, half, width), BF),
            jax.ShapeDtypeStruct((experts, half), F32),
        ),
        in_specs=[pl.BlockSpec(memory_space=pltpu.VMEM)] * 3,
        out_specs=(pl.BlockSpec(memory_space=pltpu.VMEM),) * 2,
        compiler_params=pltpu.CompilerParams(vmem_limit_bytes=32 * 1024 * 1024),
        name="finish",
    )(parts, gate_col, my_hidden)
    return grad_hidden[None], grad_gates[None], total


def solution(mesh):
    in_specs = (
        P("dp", "expert", "tensor", None),
        P("dp", "expert", None, None),
        P("dp", "expert", None, None),
        P("dp", "expert", None, None),
        P("expert", None, "tensor"),
    )
    out_specs = (
        P("dp", "expert", "tensor", None),
        P("dp", "expert", "tensor"),
        P("expert", "dp", "tensor"),
    )
    return jax.shard_map(local, mesh=mesh, in_specs=in_specs, out_specs=out_specs, check_vma=False)
```

time: 170 us -> 169 us (level)
  waiting for transfers between devices: 95.8 us -> 43.5 us
  blocking collectives: 0 us -> 39 us
  starting transfers between devices: 32.8 us -> 47.1 us
  local copies, waits for them, and re-layouts: 10 us -> 4.32 us
  Pallas kernels: 15.2 us -> 19 us
    all_gather x0 -> x1, blocking collectives: none -> 39 us  [local(): lax.all_gather(meta, 'expert')]
    all_to_all x2 -> x1, waiting for transfers between devices: 37.1 us -> 0.01 us  [local(): tok = lax.all_to_all(send, ('expert', 'tensor'), 0, 0, tiled=True)]
    all_to_all x1, waiting for transfers between devices: 56.3 us -> 28 us  [local(): lax.all_to_all(parts, 'tensor', 0, 0, tiled=True, axis_index_groups=same_...]
    all_to_all x2 -> x1, starting transfers between devices: 24.7 us -> 10.4 us  [local(): tok = lax.all_to_all(send, ('expert', 'tensor'), 0, 0, tiled=True)]
    ppermute x1, starting transfers between devices: 1.92 us -> 16.2 us  [local(): w_other = lax.ppermute(w_down, 'tensor', pair)]
    ppermute x1 -> x3, waiting for transfers between devices: 2.35 us -> 15.5 us  [the longest x1 8.99 us: local(): near = lax.ppermute(near, 'tensor', swap(0))]
    ppermute x1 -> x3, starting transfers between devices: 2.39 us -> 15.2 us  [the longest x1 7.71 us: local(): other = lax.ppermute(tok, 'tensor', pair)]
    unnamed x11 -> x7, local copies, waits for them, and re-layouts: 7.25 us -> 2.22 us
  transfers between devices with their start and end apart: 6 -> 7, of which waited for: 4 -> 4; matrix products, arithmetic and copies ran while one was open for 1% -> 2% of each run, Pallas kernels for 9% -> 6%
where the time goes in v3:
time: 169 us; the launch traced here: 167 us
  starting transfers between devices  47.1 us (28%)
  waiting for transfers between devices  43.5 us (26%)
  blocking collectives  39 us (23%)
  Pallas kernels  19 us (11%)
  between operations  14.2 us (8%)
  local copies, waits for them, and re-layouts  4.32 us (3%)
    all_gather x1, blocking collectives, local(): lax.all_gather(meta, 'expert')  39 us
    all_to_all x1, waiting for transfers between devices, local(): lax.all_to_all(parts, 'tensor', 0, 0, tiled=True, axis_index_groups=same_...  28 us
    ppermute x1, starting transfers between devices, local(): w_other = lax.ppermute(w_down, 'tensor', pair)  16.2 us
    all_to_all x1, starting transfers between devices, local(): tok = lax.all_to_all(send, ('expert', 'tensor'), 0, 0, tiled=True)  10.4 us
    ppermute x1, waiting for transfers between devices, local(): near = lax.ppermute(near, 'tensor', swap(0))  8.99 us
    pallas_call x1, Pallas kernels, local(): pl.pallas_call(functools.partial(weight_kernel, dims=dims), out_shape=(ja...  8.5 us
    pallas_call x1, Pallas kernels, local(): pl.pallas_call(part_kernel, out_shape=(jax.ShapeDtypeStruct((pairs, exper...  7.76 us
    ppermute x1, starting transfers between devices, local(): other = lax.ppermute(tok, 'tensor', pair)  7.71 us
  transfers between devices with their start and end apart: 7, of which 4 were waited for; matrix products, arithmetic and copies ran while one was open for 2% of the time, Pallas kernels for 6%

profile of v3, /device:TPU:1, one launch (start us, length us, event | category | flops | bytes accessed | tf_op | source)
XLA Modules:
  0.0 167.1 jit_solution(149451248573071871)
XLA Ops:
  7.2 0.0 copy-start.1
  7.2 0.0 copy-start.2
  7.2 16.2 %collective-permute-start.1 = (bf16[8,768,256]{2,1,0:T(8,128)(2,1)}, bf16[8,768,256]{2,1,0:T(8,128)(2,1)}, u32[]{:S(2)}, u32[]{:S(2)}) collective-permute-start(bf16[8,768,256]{2,1,0:T(8,128)(2,1)} %w_ref.1), channel_id=1, source_target_pairs={{0,8},{8,0},{16,24},{24,16},{32,40},{40,32},{48,56},{56,48},{64,72... | collective-permute-start | bytes 9437192 | tf_op jit(solution)/shard_map/ppermute | solution.py:156
  23.4 0.9 copy.9
  24.4 1.1 broadcast_in_dim.12
  25.4 10.4 %all-to-all-start = ((bf16[128,16,256]{2,1,0:T(8,128)(2,1)}), bf16[128,16,256]{2,1,0:T(8,128)(2,1)S(1)}, u32[]{:S(2)}, u32[]{:S(2)}) async-start(bf16[128,16,256]{2,1,0:T(8,128)(2,1)} %bitcast.4), calls=%async_computation | async-start | bytes 2097152 | tf_op jit(solution)/shard_map/all_to_all | solution.py:165
  35.9 0.0 reduce-scatter.2.cloned.1.call-start
  35.9 0.0 copy-done.1
  35.9 0.0 copy-done.2
  36.0 39.0 %all-gather = bf16[128,256]{1,0:T(8,128)(2,1)S(1)} all-gather(bf16[16,256]{1,0:T(8,128)(2,1)S(1)} %pad_maximum_fusion), channel_id=2, replica_groups=mesh['dp'=8,'tensor'=16,'expert'=8] {'expert'}, dimensions={0}, use_global_device_ids=true | all-gather | bytes 73728 | tf_op jit(solution)/shard_map/all_gather | solution.py:161
  75.0 0.1 pad_add_fusion.place
  75.1 0.0 collective-permute-done.1.w_other_ref
  75.1 0.0 all-to-all-done
  75.1 8.5 %weight_part.1 = (bf16[8,8,96,256]{3,2,1,0:T(8,128)(2,1)}, bf16[8,192,256]{2,1,0:T(8,128)(2,1)S(1)}, f32[192,128]{1,0:T(8,128)S(1)}) custom-call(s32[3]{0:T(128)S(1)} %pad_add_fusion.place, bf16[8,256,256]{2,1,0:T(8,128)(2,1)S(1)} %bitcast.25, bf16[8,16,256]{2,1,0:T(8,128)(2,1)S(1)} %bitcast.28, bf16[8,384,768]{2,1,0:T(8,128)(2,1)} %bitcast.31), custom_call_target="tpu_custom_call" | custom-call | flops 1610612736 | bytes 3145728 | tf_op jit(solution)/shard_map/weight_part/pallas_call | solution.py:173
  83.6 0.0 reduce-scatter.2.cloned.1.call-update
  83.6 7.7 %collective-permute-start = (bf16[8,256,256]{2,1,0:T(8,128)(2,1)S(1)}, bf16[8,256,256]{2,1,0:T(8,128)(2,1)S(1)}, u32[]{:S(2)}, u32[]{:S(2)}) collective-permute-start(bf16[8,256,256]{2,1,0:T(8,128)(2,1)S(1)} %bitcast.26), channel_id=1, source_target_pairs={{0,8},{8,0},{16,24},{24,16},{32,40},{40,32},{48,56},{56,48},{64,72... | collective-permute-start | bytes 3145736 | tf_op jit(solution)/shard_map/ppermute | solution.py:167
  91.3 2.3 %collective-permute-done.other_ref = bf16[8,256,256]{2,1,0:T(8,128)(2,1)S(1)} collective-permute-done((bf16[8,256,256]{2,1,0:T(8,128)(2,1)S(1)}, bf16[8,256,256]{2,1,0:T(8,128)(2,1)S(1)}, u32[]{:S(2)}, u32[]{:S(2)}) %collective-permute-start) | collective-permute-done | bytes 1048608 | tf_op jit(solution)/shard_map/ppermute | solution.py:167
  93.6 7.8 %hidden_part.1 = (bf16[4,8,24,768]{3,2,1,0:T(8,128)(2,1)}, bf16[4,4,24,768]{3,2,1,0:T(8,128)(2,1)S(1)}, bf16[4,4,24,768]{3,2,1,0:T(8,128)(2,1)S(1)}) custom-call(s32[3]{0:T(128)S(1)} %pad_add_fusion.place, bf16[8,256,256]{2,1,0:T(8,128)(2,1)S(1)} %bitcast.27, bf16[8,256,256]{2,1,0:T(8,128)(2,1)S(1)} %collective-permute-done.other_ref, ...), custom_call_target="tpu_custom_call" | custom-call | flops 1610612736 | bytes 3145728 | tf_op jit(solution)/shard_map/hidden_part/pallas_call | solution.py:199
  101.3 3.3 %collective-permute-start.2 = (bf16[4,4,24,768]{3,2,1,0:T(8,128)(2,1)S(1)}, bf16[4,4,24,768]{3,2,1,0:T(8,128)(2,1)S(1)}, u32[]{:S(2)}, u32[]{:S(2)}) collective-permute-start(bf16[4,4,24,768]{3,2,1,0:T(8,128)(2,1)S(1)} %get-tuple-element.17), channel_id=1, source_target_pairs={{0,16},{8,24},{16,0},{24,8},{32,48},{40,56},{48,32},{56,40},{64,80... | collective-permute-start | bytes 1769480 | tf_op jit(solution)/shard_map/ppermute | solution.py:232
  104.6 4.2 %collective-permute-start.3 = (bf16[4,4,24,768]{3,2,1,0:T(8,128)(2,1)S(1)}, bf16[4,4,24,768]{3,2,1,0:T(8,128)(2,1)S(1)}, u32[]{:S(2)}, u32[]{:S(2)}) collective-permute-start(bf16[4,4,24,768]{3,2,1,0:T(8,128)(2,1)S(1)} %get-tuple-element.18), channel_id=1, source_target_pairs={{0,112},{8,120},{16,32},{24,40},{32,16},{40,24},{48,64},{56,72},{6... | collective-permute-start | bytes 1769480 | tf_op jit(solution)/shard_map/ppermute | solution.py:233
  108.8 9.0 %collective-permute-done.2.near_ref = bf16[4,4,24,768]{3,2,1,0:T(8,128)(2,1)S(1)} collective-permute-done((bf16[4,4,24,768]{3,2,1,0:T(8,128)(2,1)S(1)}, bf16[4,4,24,768]{3,2,1,0:T(8,128)(2,1)S(1)}, u32[]{:S(2)}, u32[]{:S(2)}) %collective-permute-start.2) | collective-permute-done | bytes 589856 | tf_op jit(solution)/shard_map/ppermute | solution.py:232
  117.8 4.2 %collective-permute-done.3.far_ref = bf16[4,4,24,768]{3,2,1,0:T(8,128)(2,1)S(1)} collective-permute-done((bf16[4,4,24,768]{3,2,1,0:T(8,128)(2,1)S(1)}, bf16[4,4,24,768]{3,2,1,0:T(8,128)(2,1)S(1)}, u32[]{:S(2)}, u32[]{:S(2)}) %collective-permute-start.3) | collective-permute-done | bytes 589856 | tf_op jit(solution)/shard_map/ppermute | solution.py:233
  122.0 0.0 copy-start
  122.0 1.3 copy-done
  123.3 1.7 pair_sum.1
  125.0 5.3 %all-to-all-start.1 = ((bf16[4,8,24,768]{3,2,1,0:T(8,128)(2,1)}), bf16[4,8,24,768]{3,2,1,0:T(8,128)(2,1)S(1)}, u32[]{:S(2)}, u32[]{:S(2)}) async-start(bf16[4,8,24,768]{3,2,1,0:T(8,128)(2,1)} %pair_sum.1), calls=%async_computation.1 | async-start | bytes 2359296 | tf_op jit(solution)/shard_map/all_to_all | solution.py:247
  130.2 1.0 dynamic-slice_bitcast_fusion.hidden_ref
  131.2 28.0 %all-to-all-done.1.parts_ref = bf16[4,8,24,768]{3,2,1,0:T(8,128)(2,1)S(1)} async-done(((bf16[4,8,24,768]{3,2,1,0:T(8,128)(2,1)}), bf16[4,8,24,768]{3,2,1,0:T(8,128)(2,1)S(1)}, u32[]{:S(2)}, u32[]{:S(2)}) %all-to-all-start.1) | async-done | bytes 1179680 | tf_op jit(solution)/shard_map/all_to_all | solution.py:247
  159.2 1.0 finish.1
  160.2 0.0 reduce-scatter.2.cloned.1.call-done
  (3 shorter events, 0.1 us)
Async XLA Ops:
  7.2 28.8 %copy-start.1 = (s32[1,1,256,8]{2,3,1,0:T(8,128)S(1)}, s32[1,1,256,8]{2,3,1,0:T(8,128)}, u32[]{:S(2)}) copy-start(s32[1,1,256,8]{2,3,1,0:T(8,128)} %param.6) | copy-start | bytes 24580
  7.2 28.8 %copy-start.2 = (bf16[1,1,256,8]{2,3,1,0:T(8,128)(2,1)S(1)}, bf16[1,1,256,8]{2,3,1,0:T(8,128)(2,1)}, u32[]{:S(2)}) copy-start(bf16[1,1,256,8]{2,3,1,0:T(8,128)(2,1)} %param.7) | copy-start | bytes 12292
  7.2 67.9 %collective-permute-start.1 = (bf16[8,768,256]{2,1,0:T(8,128)(2,1)}, bf16[8,768,256]{2,1,0:T(8,128)(2,1)}, u32[]{:S(2)}, u32[]{:S(2)}) collective-permute-start(bf16[8,768,256]{2,1,0:T(8,128)(2,1)} %w_ref.1), channel_id=1, source_target_pairs={{0,8},{8,0},{16,24},{24,16},{32,40},{40,32},{48,56},{56,48},{64,72... | collective-permute-start | bytes 9437192 | tf_op jit(solution)/shard_map/ppermute | solution.py:156
  25.4 49.6 %all-to-all-start = ((bf16[128,16,256]{2,1,0:T(8,128)(2,1)}), bf16[128,16,256]{2,1,0:T(8,128)(2,1)S(1)}, u32[]{:S(2)}, u32[]{:S(2)}) async-start(bf16[128,16,256]{2,1,0:T(8,128)(2,1)} %bitcast.4), calls=%async_computation | async-start | bytes 2097152 | tf_op jit(solution)/shard_map/all_to_all | solution.py:165
  35.9 124.4 %reduce-scatter.2.cloned.1.call-start = ((), (), s32[]{:S(2)}) async-start(), calls=%async_computation.3 | async-start | bytes 3538944 | tf_op jit(solution)/shard_map/reduce_scatter | solution.py:195
  83.6 10.0 %collective-permute-start = (bf16[8,256,256]{2,1,0:T(8,128)(2,1)S(1)}, bf16[8,256,256]{2,1,0:T(8,128)(2,1)S(1)}, u32[]{:S(2)}, u32[]{:S(2)}) collective-permute-start(bf16[8,256,256]{2,1,0:T(8,128)(2,1)S(1)} %bitcast.26), channel_id=1, source_target_pairs={{0,8},{8,0},{16,24},{24,16},{32,40},{40,32},{48,56},{56,48},{64,72... | collective-permute-start | bytes 3145736 | tf_op jit(solution)/shard_map/ppermute | solution.py:167
  101.3 16.5 %collective-permute-start.2 = (bf16[4,4,24,768]{3,2,1,0:T(8,128)(2,1)S(1)}, bf16[4,4,24,768]{3,2,1,0:T(8,128)(2,1)S(1)}, u32[]{:S(2)}, u32[]{:S(2)}) collective-permute-start(bf16[4,4,24,768]{3,2,1,0:T(8,128)(2,1)S(1)} %get-tuple-element.17), channel_id=1, source_target_pairs={{0,16},{8,24},{16,0},{24,8},{32,48},{40,56},{48,32},{56,40},{64,80... | collective-permute-start | bytes 1769480 | tf_op jit(solution)/shard_map/ppermute | solution.py:232
  104.6 17.5 %collective-permute-start.3 = (bf16[4,4,24,768]{3,2,1,0:T(8,128)(2,1)S(1)}, bf16[4,4,24,768]{3,2,1,0:T(8,128)(2,1)S(1)}, u32[]{:S(2)}, u32[]{:S(2)}) collective-permute-start(bf16[4,4,24,768]{3,2,1,0:T(8,128)(2,1)S(1)} %get-tuple-element.18), channel_id=1, source_target_pairs={{0,112},{8,120},{16,32},{24,40},{32,16},{40,24},{48,64},{56,72},{6... | collective-permute-start | bytes 1769480 | tf_op jit(solution)/shard_map/ppermute | solution.py:233
  122.0 1.3 copy-start
  125.0 34.2 %all-to-all-start.1 = ((bf16[4,8,24,768]{3,2,1,0:T(8,128)(2,1)}), bf16[4,8,24,768]{3,2,1,0:T(8,128)(2,1)S(1)}, u32[]{:S(2)}, u32[]{:S(2)}) async-start(bf16[4,8,24,768]{3,2,1,0:T(8,128)(2,1)} %pair_sum.1), calls=%async_computation.1 | async-start | bytes 2359296 | tf_op jit(solution)/shard_map/all_to_all | solution.py:247
Sparse Core Ops, SparseCore 0:
  83.7 54.2 reduce-scatter.1

commit v4 on v3

--- a/solution.py
+++ b/solution.py
@@ -44,29 +44,34 @@
     return jnp.concatenate(rows, 0)
 
 
-def weight_kernel(place, tok_ref, meta_ref, hidden_ref, out_ref, hot_ref, gate_ref, scaled, *, dims):
+def pick_kernel(place, meta_ref, scaled_hot_ref, hot_ref, gate_ref, *, dims):
     experts, columns, tokens, choices, most = dims
     half = most // 2
+    base = place[2] * half
+    table, gates = tables(meta_ref, columns, place[0] * experts, experts, tokens, choices)
+    for c in range(columns):
+        scaled_hot_ref[c] = picker(table[c], gates[c], 0, most, experts, tokens).astype(BF)
+        hot_ref[c] = picker(table[c], None, base, half, experts, tokens).astype(BF)
+
+        @pl.when(place[1] == c)
+        def _():
+            gate = picker(table[c], gates[c], base, half, experts, tokens)
+            gate_ref[...] = jnp.broadcast_to(jnp.sum(gate, axis=1, keepdims=True), gate_ref.shape)
+
+
+def weight_kernel(tok_ref, hot_ref, hidden_ref, out_ref, scaled):
+    experts = scaled.shape[0]
+    columns = tok_ref.shape[0]
+    most = scaled.shape[1] // columns
     step = pl.program_id(0)
     per = hidden_ref.shape[0]
 
     @pl.when(step == 0)
     def _():
-        table, gates = tables(meta_ref, columns, place[0] * experts, experts, tokens, choices)
         for c in range(columns):
-            pick = picker(table[c], gates[c], 0, most, experts, tokens).astype(BF)
-            rows = jnp.dot(pick, tok_ref[c], preferred_element_type=F32).astype(BF)
+            rows = jnp.dot(hot_ref[c], tok_ref[c], preferred_element_type=F32).astype(BF)
             for x in range(experts):
                 scaled[x, c * most : (c + 1) * most, :] = rows[x * most : (x + 1) * most]
-            base = place[2] * half
-            hot_ref[c] = picker(table[c], None, base, half, experts, tokens).astype(BF)
-
-            @pl.when(place[1] == c)
-            def _():
-                gate = picker(table[c], gates[c], base, half, experts, tokens)
-                gate_ref[...] = jnp.broadcast_to(
-                    jnp.sum(gate, axis=1, keepdims=True), gate_ref.shape
-                )
 
     for i in range(per):
         part = lax.dot_general(
@@ -158,44 +163,60 @@
     my_hidden = lax.dynamic_slice_in_dim(hidden_saved[0], first, slots // n_tensor, 1)
 
     meta = jnp.concatenate([routes[0, 0].T.astype(BF), gates[0, 0].T], 0)
-    meta, w_other = lax.optimization_barrier((lax.all_gather(meta, "expert"), w_other))
+    meta = jnp.broadcast_to(meta[None], (n_expert,) + meta.shape)
+    meta = lax.all_to_all(meta, "expert", 0, 0, tiled=True)
+    whole = lambda *shape: pl.BlockSpec(shape, lambda x, p: (0,) * len(shape))
+    scaled_hot, hot, gate_col = pl.pallas_call(
+        functools.partial(pick_kernel, dims=dims),
+        out_shape=(
+            jax.ShapeDtypeStruct((n_expert, experts * most, tokens), BF),
+            jax.ShapeDtypeStruct((n_expert, experts * half, tokens), BF),
+            jax.ShapeDtypeStruct((experts * half, 128), F32),
+        ),
+        grid_spec=pltpu.PrefetchScalarGridSpec(
+            num_scalar_prefetch=1,
+            grid=(1,),
+            in_specs=[whole(*meta.shape)],
+            out_specs=(
+                whole(n_expert, experts * most, tokens),
+                whole(n_expert, experts * half, tokens),
+                whole(experts * half, 128),
+            ),
+        ),
+        compiler_params=params,
+        cost_estimate=cost,
+        name="pick",
+    )(place, meta)
+    scaled_hot, w_other = lax.optimization_barrier((scaled_hot, w_other))
     send = grad_out[0, 0].reshape(own, n_tensor, block).transpose(1, 0, 2)
     send = jnp.broadcast_to(send[None], (n_expert,) + send.shape)
     send = send.reshape(n_expert * n_tensor, own, block)
+    send, _ = lax.optimization_barrier((send, meta))
     tok = lax.all_to_all(send, ("expert", "tensor"), 0, 0, tiled=True)
     tok = tok.reshape(n_expert, tokens, block)
     other = lax.ppermute(tok, "tensor", pair)
 
     per = 2
-    whole = lambda *shape: pl.BlockSpec(shape, lambda x, p: (0,) * len(shape))
-    per_expert = lambda *shape: pl.BlockSpec((per,) + shape, lambda x, p: (x, 0, 0))
+    whole = lambda *shape: pl.BlockSpec(shape, lambda x: (0,) * len(shape))
+    per_expert = lambda *shape: pl.BlockSpec((per,) + shape, lambda x: (x, 0, 0))
     block_f = width // n_dp
-    partial, hot, gate_col = pl.pallas_call(
-        functools.partial(weight_kernel, dims=dims),
-        out_shape=(
-            jax.ShapeDtypeStruct((n_dp, experts, block_f, block), BF),
-            jax.ShapeDtypeStruct((n_expert, experts * half, tokens), BF),
-            jax.ShapeDtypeStruct((experts * half, 128), F32),
-        ),
-        grid_spec=pltpu.PrefetchScalarGridSpec(
-            num_scalar_prefetch=1,
-            grid=(experts // per,),
-            in_specs=[whole(*tok.shape), whole(*meta.shape), per_expert(slots, width)],
-            out_specs=(
-                pl.BlockSpec((n_dp, per, block_f, block), lambda x, p: (0, x, 0, 0)),
-                whole(n_expert, experts * half, tokens),
-                whole(experts * half, 128),
-            ),
-            scratch_shapes=[pltpu.VMEM((experts, slots, block), BF)],
-        ),
+    partial = pl.pallas_call(
+        weight_kernel,
+        out_shape=jax.ShapeDtypeStruct((n_dp, experts, block_f, block), BF),
+        grid=(experts // per,),
+        in_specs=[whole(*tok.shape), whole(*scaled_hot.shape), per_expert(slots, width)],
+        out_specs=pl.BlockSpec((n_dp, per, block_f, block), lambda x: (0, x, 0, 0)),
+        scratch_shapes=[pltpu.VMEM((experts, slots, block), BF)],
         compiler_params=params,
         cost_estimate=cost,
         name="weight_part",
-    )(place, tok, meta, hidden_saved[0])
+    )(tok, scaled_hot, hidden_saved[0])
     total = lax.psum_scatter(partial, "dp", scatter_dimension=0, tiled=True)[0]
 
     pairs, near_steps = chips // 2, experts // per // 2
     out_block = (pairs, per, half, width)
+    whole_p = lambda *shape: pl.BlockSpec(shape, lambda x, p: (0,) * len(shape))
+    per_expert_p = lambda *shape: pl.BlockSpec((per,) + shape, lambda x, p: (x, 0, 0))
     keep, near, far = pl.pallas_call(
         part_kernel,
         out_shape=(
@@ -207,11 +228,11 @@
             num_scalar_prefetch=1,
             grid=(experts // per,),
             in_specs=[
-                whole(*tok.shape),
-                whole(*tok.shape),
-                whole(*hot.shape),
-                per_expert(width, block),
-                per_expert(width, block),
+                whole_p(*tok.shape),
+                whole_p(*tok.shape),
+                whole_p(*hot.shape),
+                per_expert_p(width, block),
+                per_expert_p(width, block),
             ],
             out_specs=(
                 pl.BlockSpec(out_block, lambda x, p: (0, x, 0, 0)),

time: 169 us -> 162 us (0.959)
  blocking collectives: 39 us -> 0 us
  waiting for transfers between devices: 43.5 us -> 78.8 us
  starting transfers between devices: 47.1 us -> 41.5 us
    all_gather x1 -> x0, blocking collectives: 39 us -> none  [local(): lax.all_gather(meta, 'expert')]
    all_to_all x1, waiting for transfers between devices: 0.01 us -> 28.2 us  [local(): tok = lax.all_to_all(send, ('expert', 'tensor'), 0, 0, tiled=True)]
    all_to_all x0 -> x1, waiting for transfers between devices: none -> 6.29 us  [local(): meta = lax.all_to_all(meta, 'expert', 0, 0, tiled=True)]
    ppermute x1, starting transfers between devices: 7.71 us -> 3.24 us  [local(): other = lax.ppermute(tok, 'tensor', pair)]
    all_to_all x0 -> x1, starting transfers between devices: none -> 3.35 us  [local(): meta = lax.all_to_all(meta, 'expert', 0, 0, tiled=True)]
    ppermute x1, waiting for transfers between devices: 8.99 us -> 11.5 us  [local(): near = lax.ppermute(near, 'tensor', swap(0))]
    ppermute x1, starting transfers between devices: 4.24 us -> 2.45 us  [local(): far = lax.ppermute(far, 'tensor', swap(1))]
    pallas_call x1 -> x2, Pallas kernels: 8.5 us -> 7.53 us  [the longest x1 6.29 us: local(): pl.pallas_call(weight_kernel, out_shape=jax.ShapeDtypeStruct((n_dp, exper...]
  transfers between devices with their start and end apart: 7 -> 8, of which waited for: 4 -> 6; matrix products, arithmetic and copies ran while one was open for 2% -> 3% of each run, Pallas kernels for 6% -> 7%
where the time goes in v4:
time: 162 us; the launch traced here: 160 us
  waiting for transfers between devices  78.8 us (49%)
  starting transfers between devices  41.5 us (26%)
  Pallas kernels  18 us (11%)
  between operations  14.1 us (9%)
  local copies, waits for them, and re-layouts  5.83 us (4%)
    all_to_all x1, waiting for transfers between devices, local(): tok = lax.all_to_all(send, ('expert', 'tensor'), 0, 0, tiled=True)  28.2 us
    all_to_all x1, waiting for transfers between devices, local(): lax.all_to_all(parts, 'tensor', 0, 0, tiled=True, axis_index_groups=same_...  27 us
    ppermute x1, starting transfers between devices, local(): w_other = lax.ppermute(w_down, 'tensor', pair)  16.1 us
    ppermute x1, waiting for transfers between devices, local(): near = lax.ppermute(near, 'tensor', swap(0))  11.5 us
    all_to_all x1, starting transfers between devices, local(): tok = lax.all_to_all(send, ('expert', 'tensor'), 0, 0, tiled=True)  9.91 us
    pallas_call x1, Pallas kernels, local(): pl.pallas_call(part_kernel, out_shape=(jax.ShapeDtypeStruct((pairs, exper...  7.78 us
    all_to_all x1, waiting for transfers between devices, local(): meta = lax.all_to_all(meta, 'expert', 0, 0, tiled=True)  6.29 us
    pallas_call x1, Pallas kernels, local(): pl.pallas_call(weight_kernel, out_shape=jax.ShapeDtypeStruct((n_dp, exper...  6.29 us
  transfers between devices with their start and end apart: 8, of which 6 were waited for; matrix products, arithmetic and copies ran while one was open for 3% of the time, Pallas kernels for 7%

profile of v4, /device:TPU:1, one launch (start us, length us, event | category | flops | bytes accessed | tf_op | source)
XLA Modules:
  0.0 159.7 jit_solution(1308860835552397578)
XLA Ops:
  7.2 16.1 %collective-permute-start.1 = (bf16[8,768,256]{2,1,0:T(8,128)(2,1)}, bf16[8,768,256]{2,1,0:T(8,128)(2,1)}, u32[]{:S(2)}, u32[]{:S(2)}) collective-permute-start(bf16[8,768,256]{2,1,0:T(8,128)(2,1)} %w_ref.1), channel_id=1, source_target_pairs={{0,8},{8,0},{16,24},{24,16},{32,40},{40,32},{48,56},{56,48},{64,72... | collective-permute-start | bytes 9437192 | tf_op jit(solution)/shard_map/ppermute | solution.py:161
  23.2 0.7 convert_bitcast_fusion
  23.9 0.7 pad_maximum_fusion
  24.6 0.6 broadcast_in_dim.9
  25.3 3.4 %all-to-all-start = ((bf16[8,16,256]{2,1,0:T(8,128)(2,1)}), bf16[8,16,256]{2,1,0:T(8,128)(2,1)S(1)}, u32[]{:S(2)}, u32[]{:S(2)}) async-start(bf16[8,16,256]{2,1,0:T(8,128)(2,1)} %broadcast_in_dim.9), calls=%async_computation | async-start | bytes 131072 | tf_op jit(solution)/shard_map/all_to_all | solution.py:167
  28.6 0.9 copy.9
  29.6 6.3 %all-to-all-done.meta_ref = bf16[8,16,256]{2,1,0:T(8,128)(2,1)S(1)} async-done(((bf16[8,16,256]{2,1,0:T(8,128)(2,1)}), bf16[8,16,256]{2,1,0:T(8,128)(2,1)S(1)}, u32[]{:S(2)}, u32[]{:S(2)}) %all-to-all-start) | async-done | bytes 65568 | tf_op jit(solution)/shard_map/all_to_all | solution.py:167
  35.9 0.0 copy-start.1
  35.9 1.1 broadcast_in_dim.8
  37.0 0.0 copy-done.1
  37.0 9.9 %all-to-all-start.1 = ((bf16[128,16,256]{2,1,0:T(8,128)(2,1)}), bf16[128,16,256]{2,1,0:T(8,128)(2,1)S(1)}, u32[]{:S(2)}, u32[]{:S(2)}) async-start(bf16[128,16,256]{2,1,0:T(8,128)(2,1)} %bitcast.4), calls=%async_computation.1 | async-start | bytes 2097152 | tf_op jit(solution)/shard_map/all_to_all | solution.py:195
  46.9 0.0 reduce-scatter.2.cloned.1.call-start
  47.0 0.1 pad_add_fusion.place
  47.1 0.8 copy-done.2
  47.9 1.2 pick.1
  49.2 0.0 collective-permute-done.1.w_other_ref
  49.2 28.2 %all-to-all-done.1 = bf16[128,16,256]{2,1,0:T(8,128)(2,1)S(1)} async-done(((bf16[128,16,256]{2,1,0:T(8,128)(2,1)}), bf16[128,16,256]{2,1,0:T(8,128)(2,1)S(1)}, u32[]{:S(2)}, u32[]{:S(2)}) %all-to-all-start.1) | async-done | bytes 1048608 | tf_op jit(solution)/shard_map/all_to_all | solution.py:195
  77.4 6.3 %weight_part.1 = bf16[8,8,96,256]{3,2,1,0:T(8,128)(2,1)} custom-call(bf16[8,256,256]{2,1,0:T(8,128)(2,1)S(1)} %bitcast.24, bf16[8,384,256]{2,1,0:T(8,128)(2,1)S(1)} %get-tuple-element.24.hot_ref, bf16[8,384,768]{2,1,0:T(8,128)(2,1)} %bitcast.27), custom_call_target="tpu_custom_call" | custom-call | flops 1610612736 | bytes 3145728 | tf_op jit(solution)/shard_map/weight_part/pallas_call | solution.py:203
  83.7 0.0 reduce-scatter.2.cloned.1.call-update
  83.7 3.2 %collective-permute-start = (bf16[8,256,256]{2,1,0:T(8,128)(2,1)S(1)}, bf16[8,256,256]{2,1,0:T(8,128)(2,1)S(1)}, u32[]{:S(2)}, u32[]{:S(2)}) collective-permute-start(bf16[8,256,256]{2,1,0:T(8,128)(2,1)S(1)} %bitcast.25), channel_id=1, source_target_pairs={{0,8},{8,0},{16,24},{24,16},{32,40},{40,32},{48,56},{56,48},{64,72... | collective-permute-start | bytes 3145736 | tf_op jit(solution)/shard_map/ppermute | solution.py:197
  86.9 2.3 %collective-permute-done.other_ref = bf16[8,256,256]{2,1,0:T(8,128)(2,1)S(1)} collective-permute-done((bf16[8,256,256]{2,1,0:T(8,128)(2,1)S(1)}, bf16[8,256,256]{2,1,0:T(8,128)(2,1)S(1)}, u32[]{:S(2)}, u32[]{:S(2)}) %collective-permute-start) | collective-permute-done | bytes 1048608 | tf_op jit(solution)/shard_map/ppermute | solution.py:197
  89.2 7.8 %hidden_part.1 = (bf16[4,8,24,768]{3,2,1,0:T(8,128)(2,1)}, bf16[4,4,24,768]{3,2,1,0:T(8,128)(2,1)S(1)}, bf16[4,4,24,768]{3,2,1,0:T(8,128)(2,1)S(1)}) custom-call(s32[3]{0:T(128)S(1)} %pad_add_fusion.place, bf16[8,256,256]{2,1,0:T(8,128)(2,1)S(1)} %bitcast.26, bf16[8,256,256]{2,1,0:T(8,128)(2,1)S(1)} %collective-permute-done.other_ref, ...), custom_call_target="tpu_custom_call" | custom-call | flops 1610612736 | bytes 3145728 | tf_op jit(solution)/shard_map/hidden_part/pallas_call | solution.py:220
  97.0 2.6 %collective-permute-start.2 = (bf16[4,4,24,768]{3,2,1,0:T(8,128)(2,1)S(1)}, bf16[4,4,24,768]{3,2,1,0:T(8,128)(2,1)S(1)}, u32[]{:S(2)}, u32[]{:S(2)}) collective-permute-start(bf16[4,4,24,768]{3,2,1,0:T(8,128)(2,1)S(1)} %get-tuple-element.19), channel_id=1, source_target_pairs={{0,16},{8,24},{16,0},{24,8},{32,48},{40,56},{48,32},{56,40},{64,80... | collective-permute-start | bytes 1769480 | tf_op jit(solution)/shard_map/ppermute | solution.py:253
  99.6 2.5 %collective-permute-start.3 = (bf16[4,4,24,768]{3,2,1,0:T(8,128)(2,1)S(1)}, bf16[4,4,24,768]{3,2,1,0:T(8,128)(2,1)S(1)}, u32[]{:S(2)}, u32[]{:S(2)}) collective-permute-start(bf16[4,4,24,768]{3,2,1,0:T(8,128)(2,1)S(1)} %get-tuple-element.20), channel_id=1, source_target_pairs={{0,112},{8,120},{16,32},{24,40},{32,16},{40,24},{48,64},{56,72},{6... | collective-permute-start | bytes 1769480 | tf_op jit(solution)/shard_map/ppermute | solution.py:254
  102.0 11.5 %collective-permute-done.2.near_ref = bf16[4,4,24,768]{3,2,1,0:T(8,128)(2,1)S(1)} collective-permute-done((bf16[4,4,24,768]{3,2,1,0:T(8,128)(2,1)S(1)}, bf16[4,4,24,768]{3,2,1,0:T(8,128)(2,1)S(1)}, u32[]{:S(2)}, u32[]{:S(2)}) %collective-permute-start.2) | collective-permute-done | bytes 589856 | tf_op jit(solution)/shard_map/ppermute | solution.py:253
  113.5 3.5 %collective-permute-done.3.far_ref = bf16[4,4,24,768]{3,2,1,0:T(8,128)(2,1)S(1)} collective-permute-done((bf16[4,4,24,768]{3,2,1,0:T(8,128)(2,1)S(1)}, bf16[4,4,24,768]{3,2,1,0:T(8,128)(2,1)S(1)}, u32[]{:S(2)}, u32[]{:S(2)}) %collective-permute-start.3) | collective-permute-done | bytes 589856 | tf_op jit(solution)/shard_map/ppermute | solution.py:254
  117.0 1.3 copy-done
  118.3 1.7 %pair_sum.1 = bf16[4,8,24,768]{3,2,1,0:T(8,128)(2,1)} custom-call(bf16[4,8,24,768]{3,2,1,0:T(8,128)(2,1)S(1)} %copy-done, bf16[4,4,24,768]{3,2,1,0:T(8,128)(2,1)S(1)} %collective-permute-done.2.near_ref, bf16[4,4,24,768]{3,2,1,0:T(8,128)(2,1)S(1)} %collective-permute-done.3.far_ref), custom_call_target="tpu_custom_call" | custom-call | tf_op jit(solution)/shard_map/pair_sum/pallas_call | solution.py:256
  120.0 3.8 %all-to-all-start.2 = ((bf16[4,8,24,768]{3,2,1,0:T(8,128)(2,1)}), bf16[4,8,24,768]{3,2,1,0:T(8,128)(2,1)S(1)}, u32[]{:S(2)}, u32[]{:S(2)}) async-start(bf16[4,8,24,768]{3,2,1,0:T(8,128)(2,1)} %pair_sum.1), calls=%async_computation.2 | async-start | bytes 2359296 | tf_op jit(solution)/shard_map/all_to_all | solution.py:268
  123.8 1.0 dynamic-slice_bitcast_fusion.hidden_ref
  124.8 27.0 %all-to-all-done.2.parts_ref = bf16[4,8,24,768]{3,2,1,0:T(8,128)(2,1)S(1)} async-done(((bf16[4,8,24,768]{3,2,1,0:T(8,128)(2,1)}), bf16[4,8,24,768]{3,2,1,0:T(8,128)(2,1)S(1)}, u32[]{:S(2)}, u32[]{:S(2)}) %all-to-all-start.2) | async-done | bytes 1179680 | tf_op jit(solution)/shard_map/all_to_all | solution.py:268
  151.8 1.0 finish.1
  (4 shorter events, 0.0 us)
Async XLA Ops:
  7.2 42.0 %collective-permute-start.1 = (bf16[8,768,256]{2,1,0:T(8,128)(2,1)}, bf16[8,768,256]{2,1,0:T(8,128)(2,1)}, u32[]{:S(2)}, u32[]{:S(2)}) collective-permute-start(bf16[8,768,256]{2,1,0:T(8,128)(2,1)} %w_ref.1), channel_id=1, source_target_pairs={{0,8},{8,0},{16,24},{24,16},{32,40},{40,32},{48,56},{56,48},{64,72... | collective-permute-start | bytes 9437192 | tf_op jit(solution)/shard_map/ppermute | solution.py:161
  25.3 10.6 %all-to-all-start = ((bf16[8,16,256]{2,1,0:T(8,128)(2,1)}), bf16[8,16,256]{2,1,0:T(8,128)(2,1)S(1)}, u32[]{:S(2)}, u32[]{:S(2)}) async-start(bf16[8,16,256]{2,1,0:T(8,128)(2,1)} %broadcast_in_dim.9), calls=%async_computation | async-start | bytes 131072 | tf_op jit(solution)/shard_map/all_to_all | solution.py:167
  35.9 1.1 copy-start.1
  37.0 40.4 %all-to-all-start.1 = ((bf16[128,16,256]{2,1,0:T(8,128)(2,1)}), bf16[128,16,256]{2,1,0:T(8,128)(2,1)S(1)}, u32[]{:S(2)}, u32[]{:S(2)}) async-start(bf16[128,16,256]{2,1,0:T(8,128)(2,1)} %bitcast.4), calls=%async_computation.1 | async-start | bytes 2097152 | tf_op jit(solution)/shard_map/all_to_all | solution.py:195
  46.9 105.9 %reduce-scatter.2.cloned.1.call-start = ((), (), s32[]{:S(2)}) async-start(), calls=%async_computation.4 | async-start | bytes 3538944 | tf_op jit(solution)/shard_map/reduce_scatter | solution.py:214
  47.1 0.8 copy-start.2
  83.7 5.5 %collective-permute-start = (bf16[8,256,256]{2,1,0:T(8,128)(2,1)S(1)}, bf16[8,256,256]{2,1,0:T(8,128)(2,1)S(1)}, u32[]{:S(2)}, u32[]{:S(2)}) collective-permute-start(bf16[8,256,256]{2,1,0:T(8,128)(2,1)S(1)} %bitcast.25), channel_id=1, source_target_pairs={{0,8},{8,0},{16,24},{24,16},{32,40},{40,32},{48,56},{56,48},{64,72... | collective-permute-start | bytes 3145736 | tf_op jit(solution)/shard_map/ppermute | solution.py:197
  97.0 16.5 %collective-permute-start.2 = (bf16[4,4,24,768]{3,2,1,0:T(8,128)(2,1)S(1)}, bf16[4,4,24,768]{3,2,1,0:T(8,128)(2,1)S(1)}, u32[]{:S(2)}, u32[]{:S(2)}) collective-permute-start(bf16[4,4,24,768]{3,2,1,0:T(8,128)(2,1)S(1)} %get-tuple-element.19), channel_id=1, source_target_pairs={{0,16},{8,24},{16,0},{24,8},{32,48},{40,56},{48,32},{56,40},{64,80... | collective-permute-start | bytes 1769480 | tf_op jit(solution)/shard_map/ppermute | solution.py:253
  99.6 17.4 %collective-permute-start.3 = (bf16[4,4,24,768]{3,2,1,0:T(8,128)(2,1)S(1)}, bf16[4,4,24,768]{3,2,1,0:T(8,128)(2,1)S(1)}, u32[]{:S(2)}, u32[]{:S(2)}) collective-permute-start(bf16[4,4,24,768]{3,2,1,0:T(8,128)(2,1)S(1)} %get-tuple-element.20), channel_id=1, source_target_pairs={{0,112},{8,120},{16,32},{24,40},{32,16},{40,24},{48,64},{56,72},{6... | collective-permute-start | bytes 1769480 | tf_op jit(solution)/shard_map/ppermute | solution.py:254
  117.0 1.3 copy-start
  120.0 31.8 %all-to-all-start.2 = ((bf16[4,8,24,768]{3,2,1,0:T(8,128)(2,1)}), bf16[4,8,24,768]{3,2,1,0:T(8,128)(2,1)S(1)}, u32[]{:S(2)}, u32[]{:S(2)}) async-start(bf16[4,8,24,768]{3,2,1,0:T(8,128)(2,1)} %pair_sum.1), calls=%async_computation.2 | async-start | bytes 2359296 | tf_op jit(solution)/shard_map/all_to_all | solution.py:268
Sparse Core Ops, SparseCore 0:
  83.8 43.9 reduce-scatter.1

commit v5 on v4

--- a/solution.py
+++ b/solution.py
@@ -19,7 +19,7 @@
     expert_of = (first + iota((experts, tokens), 0)).astype(F32)
     named, gates = [], []
     for c in range(columns):
-        meta = meta_ref[c].astype(F32)
+        meta = meta_ref[c, tokens:, :].astype(F32)
         hit_any = jnp.zeros((experts, tokens), F32)
         gate = jnp.zeros((experts, tokens), F32)
         for k in range(choices):
@@ -69,7 +69,8 @@
     @pl.when(step == 0)
     def _():
         for c in range(columns):
-            rows = jnp.dot(hot_ref[c], tok_ref[c], preferred_element_type=F32).astype(BF)
+            rows = jnp.dot(hot_ref[c], tok_ref[c, : hot_ref.shape[2]], preferred_element_type=F32)
+            rows = rows.astype(BF)
             for x in range(experts):
                 scaled[x, c * most : (c + 1) * most, :] = rows[x * most : (x + 1) * most]
 
@@ -97,7 +98,9 @@
     def _():
         for c in range(columns):
             for src, dst in ((tok_ref, mine), (other_ref, theirs)):
-                rows = jnp.dot(hot_ref[c], src[c], preferred_element_type=F32)
+                rows = jnp.dot(
+                    hot_ref[c], src[c, : hot_ref.shape[2]], preferred_element_type=F32
+                )
                 for x in range(experts):
                     dst[x, c * half : (c + 1) * half, :] = rows[x * half : (x + 1) * half]
 
@@ -162,10 +165,12 @@
     first = me * (slots // n_tensor)
     my_hidden = lax.dynamic_slice_in_dim(hidden_saved[0], first, slots // n_tensor, 1)
 
-    meta = jnp.concatenate([routes[0, 0].T.astype(BF), gates[0, 0].T], 0)
-    meta = jnp.broadcast_to(meta[None], (n_expert,) + meta.shape)
-    meta = lax.all_to_all(meta, "expert", 0, 0, tiled=True)
-    whole = lambda *shape: pl.BlockSpec(shape, lambda x, p: (0,) * len(shape))
+    send = grad_out[0, 0].reshape(own, n_tensor, block).transpose(1, 0, 2)
+    column = lax.all_to_all(send, "tensor", 0, 0, tiled=True).reshape(tokens, block)
+    packed = jnp.concatenate([column, routes[0, 0].T.astype(BF), gates[0, 0].T], 0)
+    packed = jnp.broadcast_to(packed[None], (n_expert,) + packed.shape)
+    tok = lax.all_to_all(packed, "expert", 0, 0, tiled=True)
+    vmem = pl.BlockSpec(memory_space=pltpu.VMEM)
     scaled_hot, hot, gate_col = pl.pallas_call(
         functools.partial(pick_kernel, dims=dims),
         out_shape=(
@@ -176,46 +181,25 @@
         grid_spec=pltpu.PrefetchScalarGridSpec(
             num_scalar_prefetch=1,
             grid=(1,),
-            in_specs=[whole(*meta.shape)],
+            in_specs=[vmem],
             out_specs=(
-                whole(n_expert, experts * most, tokens),
-                whole(n_expert, experts * half, tokens),
-                whole(experts * half, 128),
+                vmem,
+                vmem,
+                vmem,
             ),
         ),
         compiler_params=params,
         cost_estimate=cost,
         name="pick",
-    )(place, meta)
-    scaled_hot, w_other = lax.optimization_barrier((scaled_hot, w_other))
-    send = grad_out[0, 0].reshape(own, n_tensor, block).transpose(1, 0, 2)
-    send = jnp.broadcast_to(send[None], (n_expert,) + send.shape)
-    send = send.reshape(n_expert * n_tensor, own, block)
-    send, _ = lax.optimization_barrier((send, meta))
-    tok = lax.all_to_all(send, ("expert", "tensor"), 0, 0, tiled=True)
-    tok = tok.reshape(n_expert, tokens, block)
+    )(place, tok)
+    tok, w_other = lax.optimization_barrier((tok, w_other))
     other = lax.ppermute(tok, "tensor", pair)
 
     per = 2
-    whole = lambda *shape: pl.BlockSpec(shape, lambda x: (0,) * len(shape))
     per_expert = lambda *shape: pl.BlockSpec((per,) + shape, lambda x: (x, 0, 0))
     block_f = width // n_dp
-    partial = pl.pallas_call(
-        weight_kernel,
-        out_shape=jax.ShapeDtypeStruct((n_dp, experts, block_f, block), BF),
-        grid=(experts // per,),
-        in_specs=[whole(*tok.shape), whole(*scaled_hot.shape), per_expert(slots, width)],
-        out_specs=pl.BlockSpec((n_dp, per, block_f, block), lambda x: (0, x, 0, 0)),
-        scratch_shapes=[pltpu.VMEM((experts, slots, block), BF)],
-        compiler_params=params,
-        cost_estimate=cost,
-        name="weight_part",
-    )(tok, scaled_hot, hidden_saved[0])
-    total = lax.psum_scatter(partial, "dp", scatter_dimension=0, tiled=True)[0]
-
     pairs, near_steps = chips // 2, experts // per // 2
     out_block = (pairs, per, half, width)
-    whole_p = lambda *shape: pl.BlockSpec(shape, lambda x, p: (0,) * len(shape))
     per_expert_p = lambda *shape: pl.BlockSpec((per,) + shape, lambda x, p: (x, 0, 0))
     keep, near, far = pl.pallas_call(
         part_kernel,
@@ -228,9 +212,9 @@
             num_scalar_prefetch=1,
             grid=(experts // per,),
             in_specs=[
-                whole_p(*tok.shape),
-                whole_p(*tok.shape),
-                whole_p(*hot.shape),
+                vmem,
+                vmem,
+                vmem,
                 per_expert_p(width, block),
                 per_expert_p(width, block),
             ],
@@ -245,6 +229,21 @@
         cost_estimate=cost,
         name="hidden_part",
     )(place, tok, other, hot, w_down, w_other)
+
+    most_per = 4
+    scaled_hot, _ = lax.optimization_barrier((scaled_hot, keep))
+    partial = pl.pallas_call(
+        weight_kernel,
+        out_shape=jax.ShapeDtypeStruct((n_dp, experts, block_f, block), BF),
+        grid=(experts // most_per,),
+        in_specs=[vmem, vmem, pl.BlockSpec((most_per, slots, width), lambda x: (x, 0, 0))],
+        out_specs=pl.BlockSpec((n_dp, most_per, block_f, block), lambda x: (0, x, 0, 0)),
+        scratch_shapes=[pltpu.VMEM((experts, slots, block), BF)],
+        compiler_params=params,
+        cost_estimate=cost,
+        name="weight_part",
+    )(tok, scaled_hot, hidden_saved[0])
+    total = lax.psum_scatter(partial, "dp", scatter_dimension=0, tiled=True)[0]
 
     def swap(shift):
         at = lambda z: (z ^ 1) if shift == 0 else ((((z + 1) % chips) ^ 1) - 1) % chips

time: 162 us -> 159 us (0.981)
  blocking collectives: 0 us -> 36.9 us
  waiting for transfers between devices: 78.8 us -> 52.3 us
  starting transfers between devices: 41.5 us -> 30.6 us
  local copies, waits for them, and re-layouts: 5.83 us -> 3.72 us
    all_to_all x0 -> x1, blocking collectives: none -> 36.9 us  [local(): tok = lax.all_to_all(packed, 'expert', 0, 0, tiled=True)]
    all_to_all x2 -> x1, waiting for transfers between devices: 34.5 us -> 8.42 us  [local(): lax.all_to_all(send, 'tensor', 0, 0, tiled=True).reshape(tokens, block)]
    all_to_all x2 -> x1, starting transfers between devices: 13.3 us -> 4.16 us  [local(): lax.all_to_all(send, 'tensor', 0, 0, tiled=True).reshape(tokens, block)]
    broadcast_in_dim x2 -> x1, local copies, waits for them, and re-layouts: 1.74 us -> 0.07 us  [local(): packed = jnp.broadcast_to(packed[None], (n_expert,) + packed.shape)]
  transfers between devices with their start and end apart: 8 -> 7, of which waited for: 6 -> 5; matrix products, arithmetic and copies ran while one was open for 3% -> 3% of each run, Pallas kernels for 7% -> 3%
where the time goes in v5:
time: 159 us; the launch traced here: 157 us
  waiting for transfers between devices  52.3 us (33%)
  blocking collectives  36.9 us (23%)
  starting transfers between devices  30.6 us (19%)
  Pallas kernels  17.5 us (11%)
  between operations  14.1 us (9%)
  local copies, waits for them, and re-layouts  3.72 us (2%)
    all_to_all x1, blocking collectives, local(): tok = lax.all_to_all(packed, 'expert', 0, 0, tiled=True)  36.9 us
    all_to_all x1, waiting for transfers between devices, local(): lax.all_to_all(parts, 'tensor', 0, 0, tiled=True, axis_index_groups=same_...  27.9 us
    ppermute x1, starting transfers between devices, local(): w_other = lax.ppermute(w_down, 'tensor', pair)  16.1 us
    ppermute x1, waiting for transfers between devices, local(): near = lax.ppermute(near, 'tensor', swap(0))  12.1 us
    all_to_all x1, waiting for transfers between devices, local(): lax.all_to_all(send, 'tensor', 0, 0, tiled=True).reshape(tokens, block)  8.42 us
    pallas_call x1, Pallas kernels, local(): pl.pallas_call(part_kernel, out_shape=(jax.ShapeDtypeStruct((pairs, exper...  8.12 us
    pallas_call x1, Pallas kernels, local(): pl.pallas_call(weight_kernel, out_shape=jax.ShapeDtypeStruct((n_dp, exper...  5.48 us
    all_to_all x1, starting transfers between devices, local(): lax.all_to_all(send, 'tensor', 0, 0, tiled=True).reshape(tokens, block)  4.16 us
  transfers between devices with their start and end apart: 7, of which 5 were waited for; matrix products, arithmetic and copies ran while one was open for 3% of the time, Pallas kernels for 3%

profile of v5, /device:TPU:1, one launch (start us, length us, event | category | flops | bytes accessed | tf_op | source)
XLA Modules:
  0.0 156.7 jit_solution(17158689495634490227)
XLA Ops:
  7.2 16.1 %collective-permute-start = (bf16[8,768,256]{2,1,0:T(8,128)(2,1)}, bf16[8,768,256]{2,1,0:T(8,128)(2,1)}, u32[]{:S(2)}, u32[]{:S(2)}) collective-permute-start(bf16[8,768,256]{2,1,0:T(8,128)(2,1)} %w_ref.1), channel_id=1, source_target_pairs={{0,8},{8,0},{16,24},{24,16},{32,40},{40,32},{48,56},{56,48},{64,72... | collective-permute-start | bytes 9437192 | tf_op jit(solution)/shard_map/ppermute | solution.py:164
  23.2 0.9 copy.10
  24.2 0.7 copy.9
  24.9 4.2 %all-to-all-start = ((bf16[16,16,256]{2,1,0:T(8,128)(2,1)}), bf16[16,16,256]{2,1,0:T(8,128)(2,1)S(1)}, u32[]{:S(2)}, u32[]{:S(2)}) async-start(bf16[16,16,256]{2,1,0:T(8,128)(2,1)} %copy.9), calls=%async_computation | async-start | bytes 262144 | tf_op jit(solution)/shard_map/all_to_all | solution.py:169
  29.0 0.0 reduce-scatter.2.cloned.1.call-start
  29.1 0.7 convert_bitcast_fusion
  29.8 8.4 %all-to-all-done = bf16[16,16,256]{2,1,0:T(8,128)(2,1)S(1)} async-done(((bf16[16,16,256]{2,1,0:T(8,128)(2,1)}), bf16[16,16,256]{2,1,0:T(8,128)(2,1)S(1)}, u32[]{:S(2)}, u32[]{:S(2)}) %all-to-all-start) | async-done | bytes 131104 | tf_op jit(solution)/shard_map/all_to_all | solution.py:169
  38.2 0.7 pad_maximum_fusion
  38.9 0.1 broadcast_in_dim.12
  39.0 36.9 %all_to_all.15.meta_ref.tok_ref = bf16[8,272,256]{2,1,0:T(8,128)(2,1)S(1)} all-to-all(bf16[8,272,256]{2,1,0:T(8,128)(2,1)S(1)} %broadcast_in_dim.12), channel_id=1, replica_groups=mesh['dp'=8,'tensor'=16,'expert'=8] {'expert'}, dimensions={0} | all-to-all | bytes 2228224 | tf_op jit(solution)/shard_map/all_to_all | solution.py:172
  75.9 0.0 collective-permute-done.w_other_ref
  75.9 2.3 %collective-permute-start.1 = (bf16[8,272,256]{2,1,0:T(8,128)(2,1)S(1)}, bf16[8,272,256]{2,1,0:T(8,128)(2,1)S(1)}, u32[]{:S(2)}, u32[]{:S(2)}) collective-permute-start(bf16[8,272,256]{2,1,0:T(8,128)(2,1)S(1)} %all_to_all.15.meta_ref.tok_ref), channel_id=1, source_target_pairs={{0,8},{8,0},{16,24},{24,16},{32,40},{40,32},{48,56},{56,48},{64,72... | collective-permute-start | bytes 3342344 | tf_op jit(solution)/shard_map/ppermute | solution.py:196
  78.3 0.1 pad_add_fusion.place
  78.3 1.2 pick.1
  79.6 1.0 collective-permute-done.1.other_ref
  80.6 0.0 copy-start.1
  80.6 1.0 copy-done.1
  81.6 8.1 %hidden_part.1 = (bf16[4,8,24,768]{3,2,1,0:T(8,128)(2,1)}, bf16[4,4,24,768]{3,2,1,0:T(8,128)(2,1)S(1)}, bf16[4,4,24,768]{3,2,1,0:T(8,128)(2,1)S(1)}) custom-call(s32[3]{0:T(128)S(1)} %pad_add_fusion.place, bf16[8,272,256]{2,1,0:T(8,128)(2,1)S(1)} %all_to_all.15.meta_ref.tok_ref, bf16[8,272,256]{2,1,0:T(8,128)(2,1)} %copy-done.1, ...), custom_call_target="tpu_custom_call" | custom-call | flops 1610612736 | bytes 3145728 | tf_op jit(solution)/shard_map/hidden_part/pallas_call | solution.py:204
  89.8 5.5 %weight_part.1 = bf16[8,8,96,256]{3,2,1,0:T(8,128)(2,1)} custom-call(bf16[8,272,256]{2,1,0:T(8,128)(2,1)S(1)} %all_to_all.15.meta_ref.tok_ref, bf16[8,384,256]{2,1,0:T(8,128)(2,1)S(1)} %get-tuple-element.24.hot_ref, bf16[8,384,768]{2,1,0:T(8,128)(2,1)} %bitcast.23), custom_call_target="tpu_custom_call" | custom-call | flops 1610612736 | bytes 3145728 | tf_op jit(solution)/shard_map/weight_part/pallas_call | solution.py:235
  95.2 0.0 copy-start
  95.2 0.0 reduce-scatter.2.cloned.1.call-update
  95.3 2.1 %collective-permute-start.2 = (bf16[4,4,24,768]{3,2,1,0:T(8,128)(2,1)S(1)}, bf16[4,4,24,768]{3,2,1,0:T(8,128)(2,1)S(1)}, u32[]{:S(2)}, u32[]{:S(2)}) collective-permute-start(bf16[4,4,24,768]{3,2,1,0:T(8,128)(2,1)S(1)} %get-tuple-element.18), channel_id=1, source_target_pairs={{0,16},{8,24},{16,0},{24,8},{32,48},{40,56},{48,32},{56,40},{64,80... | collective-permute-start | bytes 1769480 | tf_op jit(solution)/shard_map/ppermute | solution.py:252
  97.4 2.4 %collective-permute-start.3 = (bf16[4,4,24,768]{3,2,1,0:T(8,128)(2,1)S(1)}, bf16[4,4,24,768]{3,2,1,0:T(8,128)(2,1)S(1)}, u32[]{:S(2)}, u32[]{:S(2)}) collective-permute-start(bf16[4,4,24,768]{3,2,1,0:T(8,128)(2,1)S(1)} %get-tuple-element.19), channel_id=1, source_target_pairs={{0,112},{8,120},{16,32},{24,40},{32,16},{40,24},{48,64},{56,72},{6... | collective-permute-start | bytes 1769480 | tf_op jit(solution)/shard_map/ppermute | solution.py:253
  99.8 12.1 %collective-permute-done.2.near_ref = bf16[4,4,24,768]{3,2,1,0:T(8,128)(2,1)S(1)} collective-permute-done((bf16[4,4,24,768]{3,2,1,0:T(8,128)(2,1)S(1)}, bf16[4,4,24,768]{3,2,1,0:T(8,128)(2,1)S(1)}, u32[]{:S(2)}, u32[]{:S(2)}) %collective-permute-start.2) | collective-permute-done | bytes 589856 | tf_op jit(solution)/shard_map/ppermute | solution.py:252
  111.9 2.9 %collective-permute-done.3.far_ref = bf16[4,4,24,768]{3,2,1,0:T(8,128)(2,1)S(1)} collective-permute-done((bf16[4,4,24,768]{3,2,1,0:T(8,128)(2,1)S(1)}, bf16[4,4,24,768]{3,2,1,0:T(8,128)(2,1)S(1)}, u32[]{:S(2)}, u32[]{:S(2)}) %collective-permute-start.3) | collective-permute-done | bytes 589856 | tf_op jit(solution)/shard_map/ppermute | solution.py:253
  114.8 0.0 copy-done
  114.8 1.7 %pair_sum.1 = bf16[4,8,24,768]{3,2,1,0:T(8,128)(2,1)} custom-call(bf16[4,8,24,768]{3,2,1,0:T(8,128)(2,1)S(1)} %copy-done, bf16[4,4,24,768]{3,2,1,0:T(8,128)(2,1)S(1)} %collective-permute-done.2.near_ref, bf16[4,4,24,768]{3,2,1,0:T(8,128)(2,1)S(1)} %collective-permute-done.3.far_ref), custom_call_target="tpu_custom_call" | custom-call | tf_op jit(solution)/shard_map/pair_sum/pallas_call | solution.py:255
  116.5 3.5 %all-to-all-start.2 = ((bf16[4,8,24,768]{3,2,1,0:T(8,128)(2,1)}), bf16[4,8,24,768]{3,2,1,0:T(8,128)(2,1)S(1)}, u32[]{:S(2)}, u32[]{:S(2)}) async-start(bf16[4,8,24,768]{3,2,1,0:T(8,128)(2,1)} %pair_sum.1), calls=%async_computation.2 | async-start | bytes 2359296 | tf_op jit(solution)/shard_map/all_to_all | solution.py:267
  120.0 1.0 dynamic-slice_bitcast_fusion.hidden_ref
  121.0 27.9 %all-to-all-done.2.parts_ref = bf16[4,8,24,768]{3,2,1,0:T(8,128)(2,1)S(1)} async-done(((bf16[4,8,24,768]{3,2,1,0:T(8,128)(2,1)}), bf16[4,8,24,768]{3,2,1,0:T(8,128)(2,1)S(1)}, u32[]{:S(2)}, u32[]{:S(2)}) %all-to-all-start.2) | async-done | bytes 1179680 | tf_op jit(solution)/shard_map/all_to_all | solution.py:267
  148.9 1.0 finish.1
  149.9 0.0 reduce-scatter.2.cloned.1.call-done
Async XLA Ops:
  7.2 68.8 %collective-permute-start = (bf16[8,768,256]{2,1,0:T(8,128)(2,1)}, bf16[8,768,256]{2,1,0:T(8,128)(2,1)}, u32[]{:S(2)}, u32[]{:S(2)}) collective-permute-start(bf16[8,768,256]{2,1,0:T(8,128)(2,1)} %w_ref.1), channel_id=1, source_target_pairs={{0,8},{8,0},{16,24},{24,16},{32,40},{40,32},{48,56},{56,48},{64,72... | collective-permute-start | bytes 9437192 | tf_op jit(solution)/shard_map/ppermute | solution.py:164
  24.9 13.3 %all-to-all-start = ((bf16[16,16,256]{2,1,0:T(8,128)(2,1)}), bf16[16,16,256]{2,1,0:T(8,128)(2,1)S(1)}, u32[]{:S(2)}, u32[]{:S(2)}) async-start(bf16[16,16,256]{2,1,0:T(8,128)(2,1)} %copy.9), calls=%async_computation | async-start | bytes 262144 | tf_op jit(solution)/shard_map/all_to_all | solution.py:169
  29.0 120.9 %reduce-scatter.2.cloned.1.call-start = ((), (), s32[]{:S(2)}) async-start(), calls=%async_computation.4 | async-start | bytes 3538944 | tf_op jit(solution)/shard_map/reduce_scatter | solution.py:246
  75.9 4.7 %collective-permute-start.1 = (bf16[8,272,256]{2,1,0:T(8,128)(2,1)S(1)}, bf16[8,272,256]{2,1,0:T(8,128)(2,1)S(1)}, u32[]{:S(2)}, u32[]{:S(2)}) collective-permute-start(bf16[8,272,256]{2,1,0:T(8,128)(2,1)S(1)} %all_to_all.15.meta_ref.tok_ref), channel_id=1, source_target_pairs={{0,8},{8,0},{16,24},{24,16},{32,40},{40,32},{48,56},{56,48},{64,72... | collective-permute-start | bytes 3342344 | tf_op jit(solution)/shard_map/ppermute | solution.py:196
  80.6 1.0 copy-start.1
  95.2 19.6 %copy-start = (bf16[4,8,24,768]{3,2,1,0:T(8,128)(2,1)S(1)}, bf16[4,8,24,768]{3,2,1,0:T(8,128)(2,1)}, u32[]{:S(2)}) copy-start(bf16[4,8,24,768]{3,2,1,0:T(8,128)(2,1)} %get-tuple-element.17.keep_ref) | copy-start | bytes 3538948
  95.3 16.7 %collective-permute-start.2 = (bf16[4,4,24,768]{3,2,1,0:T(8,128)(2,1)S(1)}, bf16[4,4,24,768]{3,2,1,0:T(8,128)(2,1)S(1)}, u32[]{:S(2)}, u32[]{:S(2)}) collective-permute-start(bf16[4,4,24,768]{3,2,1,0:T(8,128)(2,1)S(1)} %get-tuple-element.18), channel_id=1, source_target_pairs={{0,16},{8,24},{16,0},{24,8},{32,48},{40,56},{48,32},{56,40},{64,80... | collective-permute-start | bytes 1769480 | tf_op jit(solution)/shard_map/ppermute | solution.py:252
  97.4 17.4 %collective-permute-start.3 = (bf16[4,4,24,768]{3,2,1,0:T(8,128)(2,1)S(1)}, bf16[4,4,24,768]{3,2,1,0:T(8,128)(2,1)S(1)}, u32[]{:S(2)}, u32[]{:S(2)}) collective-permute-start(bf16[4,4,24,768]{3,2,1,0:T(8,128)(2,1)S(1)} %get-tuple-element.19), channel_id=1, source_target_pairs={{0,112},{8,120},{16,32},{24,40},{32,16},{40,24},{48,64},{56,72},{6... | collective-permute-start | bytes 1769480 | tf_op jit(solution)/shard_map/ppermute | solution.py:253
  116.5 32.4 %all-to-all-start.2 = ((bf16[4,8,24,768]{3,2,1,0:T(8,128)(2,1)}), bf16[4,8,24,768]{3,2,1,0:T(8,128)(2,1)S(1)}, u32[]{:S(2)}, u32[]{:S(2)}) async-start(bf16[4,8,24,768]{3,2,1,0:T(8,128)(2,1)} %pair_sum.1), calls=%async_computation.2 | async-start | bytes 2359296 | tf_op jit(solution)/shard_map/all_to_all | solution.py:267
Sparse Core Ops, SparseCore 0:
  95.4 40.8 reduce-scatter.1

commit v6 on v5

--- a/solution.py
+++ b/solution.py
@@ -192,7 +192,6 @@
         cost_estimate=cost,
         name="pick",
     )(place, tok)
-    tok, w_other = lax.optimization_barrier((tok, w_other))
     other = lax.ppermute(tok, "tensor", pair)
 
     per = 2
@@ -225,7 +224,7 @@
             ),
             scratch_shapes=[pltpu.VMEM((experts, slots // 2, block), F32)] * 2,
         ),
-        compiler_params=params,
+        compiler_params=pltpu.CompilerParams(vmem_limit_bytes=48 * 1024 * 1024),
         cost_estimate=cost,
         name="hidden_part",
     )(place, tok, other, hot, w_down, w_other)
@@ -251,6 +250,7 @@
 
     near = lax.ppermute(near, "tensor", swap(0))
     far = lax.ppermute(far, "tensor", swap(1))
+    keep, _ = lax.optimization_barrier((keep, partial))
     row = lambda n: pl.BlockSpec((1, n, half, width), lambda m: (m, 0, 0, 0))
     parts = pl.pallas_call(
         add_kernel,
@@ -259,6 +259,7 @@
         in_specs=[row(experts), row(experts // 2), row(experts // 2)],
         out_specs=row(experts),
         compiler_params=params,
+        cost_estimate=pl.CostEstimate(flops=60000000000, bytes_accessed=0, transcendentals=0),
         name="pair_sum",
     )(keep, near, far)
     same_kind = [

time: 159 us -> 152 us (0.956)
  waiting for transfers between devices: 52.3 us -> 45 us
    ppermute x1, starting transfers between devices: 16.1 us -> 2.02 us  [local(): w_other = lax.ppermute(w_down, 'tensor', pair)]
    all_to_all x1, starting transfers between devices: 4.16 us -> 18.2 us  [local(): lax.all_to_all(send, 'tensor', 0, 0, tiled=True).reshape(tokens, block)]
    ppermute x1, waiting for transfers between devices: 12.1 us -> 6.87 us  [local(): near = lax.ppermute(near, 'tensor', swap(0))]
    all_to_all x1, waiting for transfers between devices: 8.42 us -> 6.4 us  [local(): lax.all_to_all(send, 'tensor', 0, 0, tiled=True).reshape(tokens, block)]
    pallas_call x1, Pallas kernels: 1.66 us -> 3.44 us  [local(): pl.pallas_call(add_kernel, out_shape=jax.ShapeDtypeStruct(keep.shape, BF)...]
  transfers between devices with their start and end apart: 7 -> 7, of which waited for: 5 -> 5; matrix products, arithmetic and copies ran while one was open for 3% -> 2% of each run, Pallas kernels for 3% -> 7%
where the time goes in v6:
time: 152 us; the launch traced here: 150 us
  waiting for transfers between devices  45 us (30%)
  blocking collectives  36.9 us (24%)
  starting transfers between devices  30.5 us (20%)
  Pallas kernels  19 us (12%)
  between operations  14.1 us (9%)
  local copies, waits for them, and re-layouts  2.7 us (2%)
    all_to_all x1, blocking collectives, local(): tok = lax.all_to_all(packed, 'expert', 0, 0, tiled=True)  36.9 us
    all_to_all x1, waiting for transfers between devices, local(): lax.all_to_all(parts, 'tensor', 0, 0, tiled=True, axis_index_groups=same_...  27.8 us
    all_to_all x1, starting transfers between devices, local(): lax.all_to_all(send, 'tensor', 0, 0, tiled=True).reshape(tokens, block)  18.2 us
    pallas_call x1, Pallas kernels, local(): pl.pallas_call(part_kernel, out_shape=(jax.ShapeDtypeStruct((pairs, exper...  7.86 us
    ppermute x1, waiting for transfers between devices, local(): near = lax.ppermute(near, 'tensor', swap(0))  6.87 us
    all_to_all x1, waiting for transfers between devices, local(): lax.all_to_all(send, 'tensor', 0, 0, tiled=True).reshape(tokens, block)  6.4 us
    pallas_call x1, Pallas kernels, local(): pl.pallas_call(weight_kernel, out_shape=jax.ShapeDtypeStruct((n_dp, exper...  5.48 us
    all_to_all x1, starting transfers between devices, local(): lax.all_to_all(parts, 'tensor', 0, 0, tiled=True, axis_index_groups=same_...  3.53 us
  transfers between devices with their start and end apart: 7, of which 5 were waited for; matrix products, arithmetic and copies ran while one was open for 2% of the time, Pallas kernels for 7%

profile of v6, /device:TPU:1, one launch (start us, length us, event | category | flops | bytes accessed | tf_op | source)
XLA Modules:
  0.0 149.7 jit_solution(3658925140739464843)
XLA Ops:
  7.2 0.9 copy.10
  8.1 0.7 copy.9
  8.8 18.2 %all-to-all-start = ((bf16[16,16,256]{2,1,0:T(8,128)(2,1)}), bf16[16,16,256]{2,1,0:T(8,128)(2,1)S(1)}, u32[]{:S(2)}, u32[]{:S(2)}) async-start(bf16[16,16,256]{2,1,0:T(8,128)(2,1)} %copy.9), calls=%async_computation | async-start | bytes 262144 | tf_op jit(solution)/shard_map/all_to_all | solution.py:169
  27.0 0.0 reduce-scatter.2.cloned.1.call-start
  27.0 2.0 %collective-permute-start.1 = (bf16[8,768,256]{2,1,0:T(8,128)(2,1)}, bf16[8,768,256]{2,1,0:T(8,128)(2,1)}, u32[]{:S(2)}, u32[]{:S(2)}) collective-permute-start(bf16[8,768,256]{2,1,0:T(8,128)(2,1)} %w_ref.1), channel_id=1, source_target_pairs={{0,8},{8,0},{16,24},{24,16},{32,40},{40,32},{48,56},{56,48},{64,72... | collective-permute-start | bytes 9437192 | tf_op jit(solution)/shard_map/ppermute | solution.py:164
  29.1 0.7 convert_bitcast_fusion
  29.8 6.4 %all-to-all-done = bf16[16,16,256]{2,1,0:T(8,128)(2,1)S(1)} async-done(((bf16[16,16,256]{2,1,0:T(8,128)(2,1)}), bf16[16,16,256]{2,1,0:T(8,128)(2,1)S(1)}, u32[]{:S(2)}, u32[]{:S(2)}) %all-to-all-start) | async-done | bytes 131104 | tf_op jit(solution)/shard_map/all_to_all | solution.py:169
  36.2 0.7 pad_maximum_fusion
  36.9 0.1 broadcast_in_dim.12
  36.9 36.9 %all_to_all.15.meta_ref.tok_ref = bf16[8,272,256]{2,1,0:T(8,128)(2,1)S(1)} all-to-all(bf16[8,272,256]{2,1,0:T(8,128)(2,1)S(1)} %broadcast_in_dim.12), channel_id=1, replica_groups=mesh['dp'=8,'tensor'=16,'expert'=8] {'expert'}, dimensions={0} | all-to-all | bytes 2228224 | tf_op jit(solution)/shard_map/all_to_all | solution.py:172
  73.9 2.3 %collective-permute-start = (bf16[8,272,256]{2,1,0:T(8,128)(2,1)S(1)}, bf16[8,272,256]{2,1,0:T(8,128)(2,1)S(1)}, u32[]{:S(2)}, u32[]{:S(2)}) collective-permute-start(bf16[8,272,256]{2,1,0:T(8,128)(2,1)S(1)} %all_to_all.15.meta_ref.tok_ref), channel_id=1, source_target_pairs={{0,8},{8,0},{16,24},{24,16},{32,40},{40,32},{48,56},{56,48},{64,72... | collective-permute-start | bytes 3342344 | tf_op jit(solution)/shard_map/ppermute | solution.py:195
  76.2 0.1 pad_add_fusion.place
  76.3 1.2 pick.1
  77.6 0.0 collective-permute-done.1.w_other_ref
  77.6 1.0 collective-permute-done.other_ref
  78.6 7.9 %hidden_part.1 = (bf16[4,8,24,768]{3,2,1,0:T(8,128)(2,1)S(1)}, bf16[4,4,24,768]{3,2,1,0:T(8,128)(2,1)}, bf16[4,4,24,768]{3,2,1,0:T(8,128)(2,1)}) custom-call(s32[3]{0:T(128)S(1)} %pad_add_fusion.place, bf16[8,272,256]{2,1,0:T(8,128)(2,1)S(1)} %all_to_all.15.meta_ref.tok_ref, bf16[8,272,256]{2,1,0:T(8,128)(2,1)S(1)} %collective-permute-done.other_ref, ...), custom_call_target="tpu_custom_call" | custom-call | flops 1610612736 | bytes 3145728 | tf_op jit(solution)/shard_map/hidden_part/pallas_call | solution.py:203
  86.4 2.0 %collective-permute-start.2 = (bf16[4,4,24,768]{3,2,1,0:T(8,128)(2,1)}, bf16[4,4,24,768]{3,2,1,0:T(8,128)(2,1)S(1)}, u32[]{:S(2)}, u32[]{:S(2)}) collective-permute-start(bf16[4,4,24,768]{3,2,1,0:T(8,128)(2,1)} %get-tuple-element.18), channel_id=1, source_target_pairs={{0,16},{8,24},{16,0},{24,8},{32,48},{40,56},{48,32},{56,40},{64,80... | collective-permute-start | bytes 1769480 | tf_op jit(solution)/shard_map/ppermute | solution.py:251
  88.4 2.4 %collective-permute-start.3 = (bf16[4,4,24,768]{3,2,1,0:T(8,128)(2,1)}, bf16[4,4,24,768]{3,2,1,0:T(8,128)(2,1)}, u32[]{:S(2)}, u32[]{:S(2)}) collective-permute-start(bf16[4,4,24,768]{3,2,1,0:T(8,128)(2,1)} %get-tuple-element.19), channel_id=1, source_target_pairs={{0,112},{8,120},{16,32},{24,40},{32,16},{40,24},{48,64},{56,72},{6... | collective-permute-start | bytes 1769480 | tf_op jit(solution)/shard_map/ppermute | solution.py:252
  90.8 5.5 %weight_part.1 = bf16[8,8,96,256]{3,2,1,0:T(8,128)(2,1)} custom-call(bf16[8,272,256]{2,1,0:T(8,128)(2,1)S(1)} %all_to_all.15.meta_ref.tok_ref, bf16[8,384,256]{2,1,0:T(8,128)(2,1)S(1)} %get-tuple-element.16.hot_ref, bf16[8,384,768]{2,1,0:T(8,128)(2,1)} %bitcast.23), custom_call_target="tpu_custom_call" | custom-call | flops 1610612736 | bytes 3145728 | tf_op jit(solution)/shard_map/weight_part/pallas_call | solution.py:234
  96.3 0.0 reduce-scatter.2.cloned.1.call-update
  96.3 6.9 %collective-permute-done.2.near_ref = bf16[4,4,24,768]{3,2,1,0:T(8,128)(2,1)S(1)} collective-permute-done((bf16[4,4,24,768]{3,2,1,0:T(8,128)(2,1)}, bf16[4,4,24,768]{3,2,1,0:T(8,128)(2,1)S(1)}, u32[]{:S(2)}, u32[]{:S(2)}) %collective-permute-start.2) | collective-permute-done | bytes 589856 | tf_op jit(solution)/shard_map/ppermute | solution.py:251
  103.2 2.9 %collective-permute-done.3.far_ref = bf16[4,4,24,768]{3,2,1,0:T(8,128)(2,1)} collective-permute-done((bf16[4,4,24,768]{3,2,1,0:T(8,128)(2,1)}, bf16[4,4,24,768]{3,2,1,0:T(8,128)(2,1)}, u32[]{:S(2)}, u32[]{:S(2)}) %collective-permute-start.3) | collective-permute-done | bytes 589856 | tf_op jit(solution)/shard_map/ppermute | solution.py:252
  106.1 3.4 %pair_sum.1 = bf16[4,8,24,768]{3,2,1,0:T(8,128)(2,1)} custom-call(bf16[4,8,24,768]{3,2,1,0:T(8,128)(2,1)S(1)} %get-tuple-element.17.keep_ref, bf16[4,4,24,768]{3,2,1,0:T(8,128)(2,1)S(1)} %collective-permute-done.2.near_ref, bf16[4,4,24,768]{3,2,1,0:T(8,128)(2,1)} %collective-permute-done.3.far_ref), custom_call_target="tpu_custom_call" | custom-call | flops 60000002048 | tf_op jit(solution)/shard_map/pair_sum/pallas_call | solution.py:255
  109.5 3.5 %all-to-all-start.2 = ((bf16[4,8,24,768]{3,2,1,0:T(8,128)(2,1)}), bf16[4,8,24,768]{3,2,1,0:T(8,128)(2,1)S(1)}, u32[]{:S(2)}, u32[]{:S(2)}) async-start(bf16[4,8,24,768]{3,2,1,0:T(8,128)(2,1)} %pair_sum.1), calls=%async_computation.2 | async-start | bytes 2359296 | tf_op jit(solution)/shard_map/all_to_all | solution.py:268
  113.0 1.0 dynamic-slice_bitcast_fusion.hidden_ref
  114.0 27.8 %all-to-all-done.2.parts_ref = bf16[4,8,24,768]{3,2,1,0:T(8,128)(2,1)S(1)} async-done(((bf16[4,8,24,768]{3,2,1,0:T(8,128)(2,1)}), bf16[4,8,24,768]{3,2,1,0:T(8,128)(2,1)S(1)}, u32[]{:S(2)}, u32[]{:S(2)}) %all-to-all-start.2) | async-done | bytes 1179680 | tf_op jit(solution)/shard_map/all_to_all | solution.py:268
  141.8 1.0 finish.1
  142.9 0.0 reduce-scatter.2.cloned.1.call-done
Async XLA Ops:
  8.8 27.4 %all-to-all-start = ((bf16[16,16,256]{2,1,0:T(8,128)(2,1)}), bf16[16,16,256]{2,1,0:T(8,128)(2,1)S(1)}, u32[]{:S(2)}, u32[]{:S(2)}) async-start(bf16[16,16,256]{2,1,0:T(8,128)(2,1)} %copy.9), calls=%async_computation | async-start | bytes 262144 | tf_op jit(solution)/shard_map/all_to_all | solution.py:169
  27.0 115.9 %reduce-scatter.2.cloned.1.call-start = ((), (), s32[]{:S(2)}) async-start(), calls=%async_computation.4 | async-start | bytes 3538944 | tf_op jit(solution)/shard_map/reduce_scatter | solution.py:245
  27.0 50.5 %collective-permute-start.1 = (bf16[8,768,256]{2,1,0:T(8,128)(2,1)}, bf16[8,768,256]{2,1,0:T(8,128)(2,1)}, u32[]{:S(2)}, u32[]{:S(2)}) collective-permute-start(bf16[8,768,256]{2,1,0:T(8,128)(2,1)} %w_ref.1), channel_id=1, source_target_pairs={{0,8},{8,0},{16,24},{24,16},{32,40},{40,32},{48,56},{56,48},{64,72... | collective-permute-start | bytes 9437192 | tf_op jit(solution)/shard_map/ppermute | solution.py:164
  73.9 4.7 %collective-permute-start = (bf16[8,272,256]{2,1,0:T(8,128)(2,1)S(1)}, bf16[8,272,256]{2,1,0:T(8,128)(2,1)S(1)}, u32[]{:S(2)}, u32[]{:S(2)}) collective-permute-start(bf16[8,272,256]{2,1,0:T(8,128)(2,1)S(1)} %all_to_all.15.meta_ref.tok_ref), channel_id=1, source_target_pairs={{0,8},{8,0},{16,24},{24,16},{32,40},{40,32},{48,56},{56,48},{64,72... | collective-permute-start | bytes 3342344 | tf_op jit(solution)/shard_map/ppermute | solution.py:195
  86.4 16.7 %collective-permute-start.2 = (bf16[4,4,24,768]{3,2,1,0:T(8,128)(2,1)}, bf16[4,4,24,768]{3,2,1,0:T(8,128)(2,1)S(1)}, u32[]{:S(2)}, u32[]{:S(2)}) collective-permute-start(bf16[4,4,24,768]{3,2,1,0:T(8,128)(2,1)} %get-tuple-element.18), channel_id=1, source_target_pairs={{0,16},{8,24},{16,0},{24,8},{32,48},{40,56},{48,32},{56,40},{64,80... | collective-permute-start | bytes 1769480 | tf_op jit(solution)/shard_map/ppermute | solution.py:251
  88.4 17.6 %collective-permute-start.3 = (bf16[4,4,24,768]{3,2,1,0:T(8,128)(2,1)}, bf16[4,4,24,768]{3,2,1,0:T(8,128)(2,1)}, u32[]{:S(2)}, u32[]{:S(2)}) collective-permute-start(bf16[4,4,24,768]{3,2,1,0:T(8,128)(2,1)} %get-tuple-element.19), channel_id=1, source_target_pairs={{0,112},{8,120},{16,32},{24,40},{32,16},{40,24},{48,64},{56,72},{6... | collective-permute-start | bytes 1769480 | tf_op jit(solution)/shard_map/ppermute | solution.py:252
  109.5 32.3 %all-to-all-start.2 = ((bf16[4,8,24,768]{3,2,1,0:T(8,128)(2,1)}), bf16[4,8,24,768]{3,2,1,0:T(8,128)(2,1)S(1)}, u32[]{:S(2)}, u32[]{:S(2)}) async-start(bf16[4,8,24,768]{3,2,1,0:T(8,128)(2,1)} %pair_sum.1), calls=%async_computation.2 | async-start | bytes 2359296 | tf_op jit(solution)/shard_map/all_to_all | solution.py:268
Sparse Core Ops, SparseCore 0:
  96.4 44.1 reduce-scatter.1

commit v7 on v6

--- a/solution.py
+++ b/solution.py
@@ -188,7 +188,7 @@
                 vmem,
             ),
         ),
-        compiler_params=params,
+        compiler_params=pltpu.CompilerParams(vmem_limit_bytes=16 * 1024 * 1024),
         cost_estimate=cost,
         name="pick",
     )(place, tok)
@@ -224,7 +224,7 @@
             ),
             scratch_shapes=[pltpu.VMEM((experts, slots // 2, block), F32)] * 2,
         ),
-        compiler_params=pltpu.CompilerParams(vmem_limit_bytes=48 * 1024 * 1024),
+        compiler_params=pltpu.CompilerParams(vmem_limit_bytes=32 * 1024 * 1024),
         cost_estimate=cost,
         name="hidden_part",
     )(place, tok, other, hot, w_down, w_other)
@@ -251,11 +251,11 @@
     near = lax.ppermute(near, "tensor", swap(0))
     far = lax.ppermute(far, "tensor", swap(1))
     keep, _ = lax.optimization_barrier((keep, partial))
-    row = lambda n: pl.BlockSpec((1, n, half, width), lambda m: (m, 0, 0, 0))
+    row = lambda n: pl.BlockSpec((2, n, half, width), lambda m: (m, 0, 0, 0))
     parts = pl.pallas_call(
         add_kernel,
         out_shape=jax.ShapeDtypeStruct(keep.shape, BF),
-        grid=(pairs,),
+        grid=(pairs // 2,),
         in_specs=[row(experts), row(experts // 2), row(experts // 2)],
         out_specs=row(experts),
         compiler_params=params,

time: 152 us -> 150 us (0.987)
  Pallas kernels: 19 us -> 17.2 us
where the time goes in v7:
time: 150 us; the launch traced here: 148 us
  waiting for transfers between devices  45 us (30%)
  blocking collectives  36.9 us (25%)
  starting transfers between devices  30.5 us (20%)
  Pallas kernels  17.2 us (11%)
  between operations  14.1 us (9%)
  local copies, waits for them, and re-layouts  2.7 us (2%)
    all_to_all x1, blocking collectives, local(): tok = lax.all_to_all(packed, 'expert', 0, 0, tiled=True)  36.9 us
    all_to_all x1, waiting for transfers between devices, local(): lax.all_to_all(parts, 'tensor', 0, 0, tiled=True, axis_index_groups=same_...  27.9 us
    all_to_all x1, starting transfers between devices, local(): lax.all_to_all(send, 'tensor', 0, 0, tiled=True).reshape(tokens, block)  18.2 us
    pallas_call x1, Pallas kernels, local(): pl.pallas_call(part_kernel, out_shape=(jax.ShapeDtypeStruct((pairs, exper...  7.35 us
    ppermute x1, waiting for transfers between devices, local(): near = lax.ppermute(near, 'tensor', swap(0))  6.86 us
    all_to_all x1, waiting for transfers between devices, local(): lax.all_to_all(send, 'tensor', 0, 0, tiled=True).reshape(tokens, block)  6.4 us
    pallas_call x1, Pallas kernels, local(): pl.pallas_call(weight_kernel, out_shape=jax.ShapeDtypeStruct((n_dp, exper...  5.47 us
    all_to_all x1, starting transfers between devices, local(): lax.all_to_all(parts, 'tensor', 0, 0, tiled=True, axis_index_groups=same_...  3.53 us
  transfers between devices with their start and end apart: 7, of which 5 were waited for; matrix products, arithmetic and copies ran while one was open for 2% of the time, Pallas kernels for 7%

profile of v7, /device:TPU:1, one launch (start us, length us, event | category | flops | bytes accessed | tf_op | source)
XLA Modules:
  0.0 147.9 jit_solution(76374340265381791)
XLA Ops:
  7.2 0.9 copy.10
  8.1 0.7 copy.9
  8.8 18.2 %all-to-all-start = ((bf16[16,16,256]{2,1,0:T(8,128)(2,1)}), bf16[16,16,256]{2,1,0:T(8,128)(2,1)S(1)}, u32[]{:S(2)}, u32[]{:S(2)}) async-start(bf16[16,16,256]{2,1,0:T(8,128)(2,1)} %copy.9), calls=%async_computation | async-start | bytes 262144 | tf_op jit(solution)/shard_map/all_to_all | solution.py:169
  27.0 0.0 reduce-scatter.2.cloned.1.call-start
  27.0 2.0 %collective-permute-start.1 = (bf16[8,768,256]{2,1,0:T(8,128)(2,1)}, bf16[8,768,256]{2,1,0:T(8,128)(2,1)}, u32[]{:S(2)}, u32[]{:S(2)}) collective-permute-start(bf16[8,768,256]{2,1,0:T(8,128)(2,1)} %w_ref.1), channel_id=1, source_target_pairs={{0,8},{8,0},{16,24},{24,16},{32,40},{40,32},{48,56},{56,48},{64,72... | collective-permute-start | bytes 9437192 | tf_op jit(solution)/shard_map/ppermute | solution.py:164
  29.1 0.7 convert_bitcast_fusion
  29.8 6.4 %all-to-all-done = bf16[16,16,256]{2,1,0:T(8,128)(2,1)S(1)} async-done(((bf16[16,16,256]{2,1,0:T(8,128)(2,1)}), bf16[16,16,256]{2,1,0:T(8,128)(2,1)S(1)}, u32[]{:S(2)}, u32[]{:S(2)}) %all-to-all-start) | async-done | bytes 131104 | tf_op jit(solution)/shard_map/all_to_all | solution.py:169
  36.2 0.7 pad_maximum_fusion
  36.9 0.1 broadcast_in_dim.12
  36.9 36.9 %all_to_all.15.meta_ref.tok_ref = bf16[8,272,256]{2,1,0:T(8,128)(2,1)S(1)} all-to-all(bf16[8,272,256]{2,1,0:T(8,128)(2,1)S(1)} %broadcast_in_dim.12), channel_id=1, replica_groups=mesh['dp'=8,'tensor'=16,'expert'=8] {'expert'}, dimensions={0} | all-to-all | bytes 2228224 | tf_op jit(solution)/shard_map/all_to_all | solution.py:172
  73.9 2.3 %collective-permute-start = (bf16[8,272,256]{2,1,0:T(8,128)(2,1)S(1)}, bf16[8,272,256]{2,1,0:T(8,128)(2,1)S(1)}, u32[]{:S(2)}, u32[]{:S(2)}) collective-permute-start(bf16[8,272,256]{2,1,0:T(8,128)(2,1)S(1)} %all_to_all.15.meta_ref.tok_ref), channel_id=1, source_target_pairs={{0,8},{8,0},{16,24},{24,16},{32,40},{40,32},{48,56},{56,48},{64,72... | collective-permute-start | bytes 3342344 | tf_op jit(solution)/shard_map/ppermute | solution.py:195
  76.2 0.1 pad_add_fusion.place
  76.3 0.0 copy-start
  76.3 1.2 pick.1
  77.6 0.0 collective-permute-done.1.w_other_ref
  77.6 1.0 collective-permute-done.other_ref
  78.6 0.0 copy-done
  78.6 7.3 %hidden_part.1 = (bf16[4,8,24,768]{3,2,1,0:T(8,128)(2,1)S(1)}, bf16[4,4,24,768]{3,2,1,0:T(8,128)(2,1)}, bf16[4,4,24,768]{3,2,1,0:T(8,128)(2,1)}) custom-call(s32[3]{0:T(128)S(1)} %pad_add_fusion.place, bf16[8,272,256]{2,1,0:T(8,128)(2,1)S(1)} %all_to_all.15.meta_ref.tok_ref, bf16[8,272,256]{2,1,0:T(8,128)(2,1)S(1)} %collective-permute-done.other_ref, ...), custom_call_target="tpu_custom_call" | custom-call | flops 1610612736 | bytes 3145728 | tf_op jit(solution)/shard_map/hidden_part/pallas_call | solution.py:203
  85.9 2.0 %collective-permute-start.2 = (bf16[4,4,24,768]{3,2,1,0:T(8,128)(2,1)}, bf16[4,4,24,768]{3,2,1,0:T(8,128)(2,1)S(1)}, u32[]{:S(2)}, u32[]{:S(2)}) collective-permute-start(bf16[4,4,24,768]{3,2,1,0:T(8,128)(2,1)} %get-tuple-element.18), channel_id=1, source_target_pairs={{0,16},{8,24},{16,0},{24,8},{32,48},{40,56},{48,32},{56,40},{64,80... | collective-permute-start | bytes 1769480 | tf_op jit(solution)/shard_map/ppermute | solution.py:251
  87.9 2.4 %collective-permute-start.3 = (bf16[4,4,24,768]{3,2,1,0:T(8,128)(2,1)}, bf16[4,4,24,768]{3,2,1,0:T(8,128)(2,1)}, u32[]{:S(2)}, u32[]{:S(2)}) collective-permute-start(bf16[4,4,24,768]{3,2,1,0:T(8,128)(2,1)} %get-tuple-element.19), channel_id=1, source_target_pairs={{0,112},{8,120},{16,32},{24,40},{32,16},{40,24},{48,64},{56,72},{6... | collective-permute-start | bytes 1769480 | tf_op jit(solution)/shard_map/ppermute | solution.py:252
  90.3 5.5 %weight_part.1 = bf16[8,8,96,256]{3,2,1,0:T(8,128)(2,1)} custom-call(bf16[8,272,256]{2,1,0:T(8,128)(2,1)S(1)} %all_to_all.15.meta_ref.tok_ref, bf16[8,384,256]{2,1,0:T(8,128)(2,1)S(1)} %get-tuple-element.16.hot_ref, bf16[8,384,768]{2,1,0:T(8,128)(2,1)} %bitcast.23), custom_call_target="tpu_custom_call" | custom-call | flops 1610612736 | bytes 3145728 | tf_op jit(solution)/shard_map/weight_part/pallas_call | solution.py:234
  95.8 0.0 reduce-scatter.2.cloned.1.call-update
  95.8 6.9 %collective-permute-done.2.near_ref = bf16[4,4,24,768]{3,2,1,0:T(8,128)(2,1)S(1)} collective-permute-done((bf16[4,4,24,768]{3,2,1,0:T(8,128)(2,1)}, bf16[4,4,24,768]{3,2,1,0:T(8,128)(2,1)S(1)}, u32[]{:S(2)}, u32[]{:S(2)}) %collective-permute-start.2) | collective-permute-done | bytes 589856 | tf_op jit(solution)/shard_map/ppermute | solution.py:251
  102.7 2.9 %collective-permute-done.3.far_ref = bf16[4,4,24,768]{3,2,1,0:T(8,128)(2,1)} collective-permute-done((bf16[4,4,24,768]{3,2,1,0:T(8,128)(2,1)}, bf16[4,4,24,768]{3,2,1,0:T(8,128)(2,1)}, u32[]{:S(2)}, u32[]{:S(2)}) %collective-permute-start.3) | collective-permute-done | bytes 589856 | tf_op jit(solution)/shard_map/ppermute | solution.py:252
  105.5 2.1 %pair_sum.1 = bf16[4,8,24,768]{3,2,1,0:T(8,128)(2,1)} custom-call(bf16[4,8,24,768]{3,2,1,0:T(8,128)(2,1)S(1)} %get-tuple-element.17.keep_ref, bf16[4,4,24,768]{3,2,1,0:T(8,128)(2,1)S(1)} %collective-permute-done.2.near_ref, bf16[4,4,24,768]{3,2,1,0:T(8,128)(2,1)} %collective-permute-done.3.far_ref), custom_call_target="tpu_custom_call" | custom-call | flops 60000002048 | tf_op jit(solution)/shard_map/pair_sum/pallas_call | solution.py:255
  107.7 3.5 %all-to-all-start.2 = ((bf16[4,8,24,768]{3,2,1,0:T(8,128)(2,1)}), bf16[4,8,24,768]{3,2,1,0:T(8,128)(2,1)S(1)}, u32[]{:S(2)}, u32[]{:S(2)}) async-start(bf16[4,8,24,768]{3,2,1,0:T(8,128)(2,1)} %pair_sum.1), calls=%async_computation.2 | async-start | bytes 2359296 | tf_op jit(solution)/shard_map/all_to_all | solution.py:268
  111.2 1.0 dynamic-slice_bitcast_fusion.hidden_ref
  112.2 27.9 %all-to-all-done.2.parts_ref = bf16[4,8,24,768]{3,2,1,0:T(8,128)(2,1)S(1)} async-done(((bf16[4,8,24,768]{3,2,1,0:T(8,128)(2,1)}), bf16[4,8,24,768]{3,2,1,0:T(8,128)(2,1)S(1)}, u32[]{:S(2)}, u32[]{:S(2)}) %all-to-all-start.2) | async-done | bytes 1179680 | tf_op jit(solution)/shard_map/all_to_all | solution.py:268
  140.1 1.0 finish.1
  141.1 0.0 reduce-scatter.2.cloned.1.call-done
Async XLA Ops:
  8.8 27.4 %all-to-all-start = ((bf16[16,16,256]{2,1,0:T(8,128)(2,1)}), bf16[16,16,256]{2,1,0:T(8,128)(2,1)S(1)}, u32[]{:S(2)}, u32[]{:S(2)}) async-start(bf16[16,16,256]{2,1,0:T(8,128)(2,1)} %copy.9), calls=%async_computation | async-start | bytes 262144 | tf_op jit(solution)/shard_map/all_to_all | solution.py:169
  27.0 114.1 %reduce-scatter.2.cloned.1.call-start = ((), (), s32[]{:S(2)}) async-start(), calls=%async_computation.4 | async-start | bytes 3538944 | tf_op jit(solution)/shard_map/reduce_scatter | solution.py:245
  27.0 50.5 %collective-permute-start.1 = (bf16[8,768,256]{2,1,0:T(8,128)(2,1)}, bf16[8,768,256]{2,1,0:T(8,128)(2,1)}, u32[]{:S(2)}, u32[]{:S(2)}) collective-permute-start(bf16[8,768,256]{2,1,0:T(8,128)(2,1)} %w_ref.1), channel_id=1, source_target_pairs={{0,8},{8,0},{16,24},{24,16},{32,40},{40,32},{48,56},{56,48},{64,72... | collective-permute-start | bytes 9437192 | tf_op jit(solution)/shard_map/ppermute | solution.py:164
  73.9 4.7 %collective-permute-start = (bf16[8,272,256]{2,1,0:T(8,128)(2,1)S(1)}, bf16[8,272,256]{2,1,0:T(8,128)(2,1)S(1)}, u32[]{:S(2)}, u32[]{:S(2)}) collective-permute-start(bf16[8,272,256]{2,1,0:T(8,128)(2,1)S(1)} %all_to_all.15.meta_ref.tok_ref), channel_id=1, source_target_pairs={{0,8},{8,0},{16,24},{24,16},{32,40},{40,32},{48,56},{56,48},{64,72... | collective-permute-start | bytes 3342344 | tf_op jit(solution)/shard_map/ppermute | solution.py:195
  76.3 2.3 %copy-start = (bf16[8,768,256]{2,1,0:T(8,128)(2,1)S(1)}, bf16[8,768,256]{2,1,0:T(8,128)(2,1)}, u32[]{:S(2)}) copy-start(bf16[8,768,256]{2,1,0:T(8,128)(2,1)} %w_ref.1) | copy-start | bytes 9437188
  85.9 16.7 %collective-permute-start.2 = (bf16[4,4,24,768]{3,2,1,0:T(8,128)(2,1)}, bf16[4,4,24,768]{3,2,1,0:T(8,128)(2,1)S(1)}, u32[]{:S(2)}, u32[]{:S(2)}) collective-permute-start(bf16[4,4,24,768]{3,2,1,0:T(8,128)(2,1)} %get-tuple-element.18), channel_id=1, source_target_pairs={{0,16},{8,24},{16,0},{24,8},{32,48},{40,56},{48,32},{56,40},{64,80... | collective-permute-start | bytes 1769480 | tf_op jit(solution)/shard_map/ppermute | solution.py:251
  87.9 17.6 %collective-permute-start.3 = (bf16[4,4,24,768]{3,2,1,0:T(8,128)(2,1)}, bf16[4,4,24,768]{3,2,1,0:T(8,128)(2,1)}, u32[]{:S(2)}, u32[]{:S(2)}) collective-permute-start(bf16[4,4,24,768]{3,2,1,0:T(8,128)(2,1)} %get-tuple-element.19), channel_id=1, source_target_pairs={{0,112},{8,120},{16,32},{24,40},{32,16},{40,24},{48,64},{56,72},{6... | collective-permute-start | bytes 1769480 | tf_op jit(solution)/shard_map/ppermute | solution.py:252
  107.7 32.4 %all-to-all-start.2 = ((bf16[4,8,24,768]{3,2,1,0:T(8,128)(2,1)}), bf16[4,8,24,768]{3,2,1,0:T(8,128)(2,1)S(1)}, u32[]{:S(2)}, u32[]{:S(2)}) async-start(bf16[4,8,24,768]{3,2,1,0:T(8,128)(2,1)} %pair_sum.1), calls=%async_computation.2 | async-start | bytes 2359296 | tf_op jit(solution)/shard_map/all_to_all | solution.py:268
Sparse Core Ops, SparseCore 0:
  95.9 44.1 reduce-scatter.1

commit v8 on v7

--- a/solution.py
+++ b/solution.py
@@ -15,11 +15,11 @@
     return lax.broadcasted_iota(jnp.int32, shape, dim)
 
 
-def tables(meta_ref, columns, first, experts, tokens, choices):
-    expert_of = (first + iota((experts, tokens), 0)).astype(F32)
+def tables(meta_ref, columns, place_x, experts, tokens, choices):
+    expert_of = (place_x * experts + iota((experts, tokens), 0)).astype(F32)
     named, gates = [], []
     for c in range(columns):
-        meta = meta_ref[c, tokens:, :].astype(F32)
+        meta = meta_ref[c ^ place_x, :, :].astype(F32)
         hit_any = jnp.zeros((experts, tokens), F32)
         gate = jnp.zeros((experts, tokens), F32)
         for k in range(choices):
@@ -48,7 +48,7 @@
     experts, columns, tokens, choices, most = dims
     half = most // 2
     base = place[2] * half
-    table, gates = tables(meta_ref, columns, place[0] * experts, experts, tokens, choices)
+    table, gates = tables(meta_ref, columns, place[0], experts, tokens, choices)
     for c in range(columns):
         scaled_hot_ref[c] = picker(table[c], gates[c], 0, most, experts, tokens).astype(BF)
         hot_ref[c] = picker(table[c], None, base, half, experts, tokens).astype(BF)
@@ -166,10 +166,16 @@
     my_hidden = lax.dynamic_slice_in_dim(hidden_saved[0], first, slots // n_tensor, 1)
 
     send = grad_out[0, 0].reshape(own, n_tensor, block).transpose(1, 0, 2)
-    column = lax.all_to_all(send, "tensor", 0, 0, tiled=True).reshape(tokens, block)
-    packed = jnp.concatenate([column, routes[0, 0].T.astype(BF), gates[0, 0].T], 0)
-    packed = jnp.broadcast_to(packed[None], (n_expert,) + packed.shape)
-    tok = lax.all_to_all(packed, "expert", 0, 0, tiled=True)
+    send = jnp.broadcast_to(send[None], (n_expert,) + send.shape)
+    send = send.reshape(n_expert * n_tensor, own, block)
+    tok = lax.all_to_all(send, ("expert", "tensor"), 0, 0, tiled=True)
+    tok = tok.reshape(n_expert, tokens, block)
+    meta = jnp.concatenate([routes[0, 0].T.astype(BF), gates[0, 0].T], 0)[None]
+    reach = 1
+    while reach < n_expert:
+        far_meta = lax.ppermute(meta, "expert", [(i, i ^ reach) for i in range(n_expert)])
+        meta = jnp.concatenate([meta, far_meta], 0)
+        reach = 2 * reach
     vmem = pl.BlockSpec(memory_space=pltpu.VMEM)
     scaled_hot, hot, gate_col = pl.pallas_call(
         functools.partial(pick_kernel, dims=dims),
@@ -191,7 +197,8 @@
         compiler_params=pltpu.CompilerParams(vmem_limit_bytes=16 * 1024 * 1024),
         cost_estimate=cost,
         name="pick",
-    )(place, tok)
+    )(place, meta)
+    tok, hot = lax.optimization_barrier((tok, hot))
     other = lax.ppermute(tok, "tensor", pair)
 
     per = 2
@@ -224,7 +231,7 @@
             ),
             scratch_shapes=[pltpu.VMEM((experts, slots // 2, block), F32)] * 2,
         ),
-        compiler_params=pltpu.CompilerParams(vmem_limit_bytes=32 * 1024 * 1024),
+        compiler_params=pltpu.CompilerParams(vmem_limit_bytes=48 * 1024 * 1024),
         cost_estimate=cost,
         name="hidden_part",
     )(place, tok, other, hot, w_down, w_other)

time: 150 us -> 161 us (1.073)
  blocking collectives: 36.9 us -> 0 us
  starting transfers between devices: 30.5 us -> 56.7 us
  waiting for transfers between devices: 45 us -> 65.9 us
    all_to_all x1 -> x0, blocking collectives: 36.9 us -> none  [local(): tok = lax.all_to_all(packed, 'expert', 0, 0, tiled=True)]
    ppermute x0 -> x3, waiting for transfers between devices: none -> 26 us  [local(): lax.ppermute(meta, 'expert', [(i, i ^ reach) for i in range(n_expert)])]
    ppermute x1, starting transfers between devices: 2.02 us -> 16.2 us  [local(): w_other = lax.ppermute(w_down, 'tensor', pair)]
    ppermute x0 -> x3, starting transfers between devices: none -> 12 us  [local(): lax.ppermute(meta, 'expert', [(i, i ^ reach) for i in range(n_expert)])]
    all_to_all x1, starting transfers between devices: 18.2 us -> 10.4 us  [local(): tok = lax.all_to_all(send, ('expert', 'tensor'), 0, 0, tiled=True)]
    all_to_all x1, waiting for transfers between devices: 6.4 us -> 0.01 us  [local(): tok = lax.all_to_all(send, ('expert', 'tensor'), 0, 0, tiled=True)]
    ppermute x1, waiting for transfers between devices: 6.86 us -> 3.81 us  [local(): near = lax.ppermute(near, 'tensor', swap(0))]
    ppermute x1, starting transfers between devices: 2.33 us -> 5.17 us  [local(): other = lax.ppermute(tok, 'tensor', pair)]
  transfers between devices with their start and end apart: 7 -> 10, of which waited for: 5 -> 8; matrix products, arithmetic and copies ran while one was open for 2% -> 2% of each run, Pallas kernels for 7% -> 6%
where the time goes in v8:
time: 161 us; the launch traced here: 159 us
  waiting for transfers between devices  65.9 us (41%)
  starting transfers between devices  56.7 us (35%)
  Pallas kernels  17.8 us (11%)
  between operations  14.2 us (9%)
  local copies, waits for them, and re-layouts  4.08 us (3%)
    all_to_all x1, waiting for transfers between devices, local(): lax.all_to_all(parts, 'tensor', 0, 0, tiled=True, axis_index_groups=same_...  27.8 us
    ppermute x3, waiting for transfers between devices, local(): lax.ppermute(meta, 'expert', [(i, i ^ reach) for i in range(n_expert)])  26 us
    ppermute x1, starting transfers between devices, local(): w_other = lax.ppermute(w_down, 'tensor', pair)  16.2 us
    ppermute x3, starting transfers between devices, local(): lax.ppermute(meta, 'expert', [(i, i ^ reach) for i in range(n_expert)])  12 us
    all_to_all x1, starting transfers between devices, local(): tok = lax.all_to_all(send, ('expert', 'tensor'), 0, 0, tiled=True)  10.4 us
    pallas_call x1, Pallas kernels, local(): pl.pallas_call(part_kernel, out_shape=(jax.ShapeDtypeStruct((pairs, exper...  7.88 us
    pallas_call x1, Pallas kernels, local(): pl.pallas_call(weight_kernel, out_shape=jax.ShapeDtypeStruct((n_dp, exper...  5.5 us
    all_to_all x1, starting transfers between devices, local(): lax.all_to_all(parts, 'tensor', 0, 0, tiled=True, axis_index_groups=same_...  5.45 us
  transfers between devices with their start and end apart: 10, of which 8 were waited for; matrix products, arithmetic and copies ran while one was open for 2% of the time, Pallas kernels for 6%

profile of v8, /device:TPU:1, one launch (start us, length us, event | category | flops | bytes accessed | tf_op | source)
XLA Modules:
  0.0 158.8 jit_solution(9782097783118471506)
XLA Ops:
  7.2 0.0 copy-start.2
  7.2 16.2 %collective-permute-start.4 = (bf16[8,768,256]{2,1,0:T(8,128)(2,1)}, bf16[8,768,256]{2,1,0:T(8,128)(2,1)}, u32[]{:S(2)}, u32[]{:S(2)}) collective-permute-start(bf16[8,768,256]{2,1,0:T(8,128)(2,1)} %w_ref.1), channel_id=1, source_target_pairs={{0,8},{8,0},{16,24},{24,16},{32,40},{40,32},{48,56},{56,48},{64,72... | collective-permute-start | bytes 9437192 | tf_op jit(solution)/shard_map/ppermute | solution.py:164
  23.4 0.9 copy.9
  24.4 1.1 broadcast_in_dim.15
  25.5 10.4 %all-to-all-start = ((bf16[128,16,256]{2,1,0:T(8,128)(2,1)}), bf16[128,16,256]{2,1,0:T(8,128)(2,1)S(1)}, u32[]{:S(2)}, u32[]{:S(2)}) async-start(bf16[128,16,256]{2,1,0:T(8,128)(2,1)} %bitcast.4), calls=%async_computation | async-start | bytes 2097152 | tf_op jit(solution)/shard_map/all_to_all | solution.py:171
  35.9 0.0 reduce-scatter.2.cloned.1.call-start
  36.0 3.3 %collective-permute-start = (bf16[1,16,256]{2,1,0:T(8,128)(2,1)S(1)}, bf16[1,16,256]{2,1,0:T(8,128)(2,1)S(1)}, u32[]{:S(2)}, u32[]{:S(2)}) collective-permute-start(bf16[1,16,256]{2,1,0:T(8,128)(2,1)S(1)} %maximum_bitcast_fusion), channel_id=1, source_target_pairs={{0,1},{1,0},{2,3},{3,2},{4,5},{5,4},{6,7},{7,6},{8,9},{9,8},{10,11... | collective-permute-start | bytes 24584 | tf_op jit(solution)/shard_map/ppermute | solution.py:176
  39.3 20.6 %collective-permute-done = bf16[1,16,256]{2,1,0:T(8,128)(2,1)S(1)} collective-permute-done((bf16[1,16,256]{2,1,0:T(8,128)(2,1)S(1)}, bf16[1,16,256]{2,1,0:T(8,128)(2,1)S(1)}, u32[]{:S(2)}, u32[]{:S(2)}) %collective-permute-start) | collective-permute-done | bytes 8224 | tf_op jit(solution)/shard_map/ppermute | solution.py:176
  59.8 2.3 %collective-permute-start.1 = (bf16[2,16,256]{2,1,0:T(8,128)(2,1)S(1)}, bf16[2,16,256]{2,1,0:T(8,128)(2,1)S(1)}, u32[]{:S(2)}, u32[]{:S(2)}) collective-permute-start(bf16[2,16,256]{2,1,0:T(8,128)(2,1)S(1)} %pad_maximum_fusion.2), channel_id=1, source_target_pairs={{0,2},{1,3},{2,0},{3,1},{4,6},{5,7},{6,4},{7,5},{8,10},{9,11},{10,... | collective-permute-start | bytes 49160 | tf_op jit(solution)/shard_map/ppermute | solution.py:176
  62.1 3.5 %collective-permute-done.1 = bf16[2,16,256]{2,1,0:T(8,128)(2,1)S(1)} collective-permute-done((bf16[2,16,256]{2,1,0:T(8,128)(2,1)S(1)}, bf16[2,16,256]{2,1,0:T(8,128)(2,1)S(1)}, u32[]{:S(2)}, u32[]{:S(2)}) %collective-permute-start.1) | collective-permute-done | bytes 16416 | tf_op jit(solution)/shard_map/ppermute | solution.py:176
  65.6 6.5 %collective-permute-start.2 = (bf16[4,16,256]{2,1,0:T(8,128)(2,1)S(1)}, bf16[4,16,256]{2,1,0:T(8,128)(2,1)S(1)}, u32[]{:S(2)}, u32[]{:S(2)}) collective-permute-start(bf16[4,16,256]{2,1,0:T(8,128)(2,1)S(1)} %pad_maximum_fusion.1), channel_id=1, source_target_pairs={{0,4},{1,5},{2,6},{3,7},{4,0},{5,1},{6,2},{7,3},{8,12},{9,13},{10,... | collective-permute-start | bytes 98312 | tf_op jit(solution)/shard_map/ppermute | solution.py:176
  72.1 0.1 pad_add_fusion.place
  72.2 2.0 %collective-permute-done.2 = bf16[4,16,256]{2,1,0:T(8,128)(2,1)S(1)} collective-permute-done((bf16[4,16,256]{2,1,0:T(8,128)(2,1)S(1)}, bf16[4,16,256]{2,1,0:T(8,128)(2,1)S(1)}, u32[]{:S(2)}, u32[]{:S(2)}) %collective-permute-start.2) | collective-permute-done | bytes 32800 | tf_op jit(solution)/shard_map/ppermute | solution.py:176
  74.2 1.2 pick.1
  75.5 0.0 all-to-all-done
  75.5 5.2 %collective-permute-start.3 = (bf16[8,256,256]{2,1,0:T(8,128)(2,1)S(1)}, bf16[8,256,256]{2,1,0:T(8,128)(2,1)S(1)}, u32[]{:S(2)}, u32[]{:S(2)}) collective-permute-start(bf16[8,256,256]{2,1,0:T(8,128)(2,1)S(1)} %bitcast.26), channel_id=1, source_target_pairs={{0,8},{8,0},{16,24},{24,16},{32,40},{40,32},{48,56},{56,48},{64,72... | collective-permute-start | bytes 3145736 | tf_op jit(solution)/shard_map/ppermute | solution.py:202
  80.6 2.3 %collective-permute-done.3.other_ref = bf16[8,256,256]{2,1,0:T(8,128)(2,1)S(1)} collective-permute-done((bf16[8,256,256]{2,1,0:T(8,128)(2,1)S(1)}, bf16[8,256,256]{2,1,0:T(8,128)(2,1)S(1)}, u32[]{:S(2)}, u32[]{:S(2)}) %collective-permute-start.3) | collective-permute-done | bytes 1048608 | tf_op jit(solution)/shard_map/ppermute | solution.py:202
  82.9 0.0 collective-permute-done.4.w_other_ref
  82.9 7.9 %hidden_part.1 = (bf16[4,8,24,768]{3,2,1,0:T(8,128)(2,1)S(1)}, bf16[4,4,24,768]{3,2,1,0:T(8,128)(2,1)}, bf16[4,4,24,768]{3,2,1,0:T(8,128)(2,1)}) custom-call(s32[3]{0:T(128)S(1)} %pad_add_fusion.place, bf16[8,256,256]{2,1,0:T(8,128)(2,1)S(1)} %bitcast.27, bf16[8,256,256]{2,1,0:T(8,128)(2,1)S(1)} %collective-permute-done.3.other_ref, ...), custom_call_target="tpu_custom_call" | custom-call | flops 1610612736 | bytes 3145728 | tf_op jit(solution)/shard_map/hidden_part/pallas_call | solution.py:210
  90.8 1.0 copy-done
  91.8 3.0 %collective-permute-start.5 = (bf16[4,4,24,768]{3,2,1,0:T(8,128)(2,1)}, bf16[4,4,24,768]{3,2,1,0:T(8,128)(2,1)S(1)}, u32[]{:S(2)}, u32[]{:S(2)}) collective-permute-start(bf16[4,4,24,768]{3,2,1,0:T(8,128)(2,1)} %get-tuple-element.22), channel_id=1, source_target_pairs={{0,16},{8,24},{16,0},{24,8},{32,48},{40,56},{48,32},{56,40},{64,80... | collective-permute-start | bytes 1769480 | tf_op jit(solution)/shard_map/ppermute | solution.py:258
  94.8 4.4 %collective-permute-start.6 = (bf16[4,4,24,768]{3,2,1,0:T(8,128)(2,1)}, bf16[4,4,24,768]{3,2,1,0:T(8,128)(2,1)}, u32[]{:S(2)}, u32[]{:S(2)}) collective-permute-start(bf16[4,4,24,768]{3,2,1,0:T(8,128)(2,1)} %get-tuple-element.23), channel_id=1, source_target_pairs={{0,112},{8,120},{16,32},{24,40},{32,16},{40,24},{48,64},{56,72},{6... | collective-permute-start | bytes 1769480 | tf_op jit(solution)/shard_map/ppermute | solution.py:259
  99.2 5.5 %weight_part.1 = bf16[8,8,96,256]{3,2,1,0:T(8,128)(2,1)} custom-call(bf16[8,256,256]{2,1,0:T(8,128)(2,1)S(1)} %bitcast.28, bf16[8,384,256]{2,1,0:T(8,128)(2,1)S(1)} %get-tuple-element.20.hot_ref, bf16[8,384,768]{2,1,0:T(8,128)(2,1)} %bitcast.29), custom_call_target="tpu_custom_call" | custom-call | flops 1610612736 | bytes 3145728 | tf_op jit(solution)/shard_map/weight_part/pallas_call | solution.py:241
  104.7 0.0 reduce-scatter.2.cloned.1.call-update
  104.8 3.8 %collective-permute-done.5.near_ref = bf16[4,4,24,768]{3,2,1,0:T(8,128)(2,1)S(1)} collective-permute-done((bf16[4,4,24,768]{3,2,1,0:T(8,128)(2,1)}, bf16[4,4,24,768]{3,2,1,0:T(8,128)(2,1)S(1)}, u32[]{:S(2)}, u32[]{:S(2)}) %collective-permute-start.5) | collective-permute-done | bytes 589856 | tf_op jit(solution)/shard_map/ppermute | solution.py:258
  108.6 3.9 %collective-permute-done.6.far_ref = bf16[4,4,24,768]{3,2,1,0:T(8,128)(2,1)} collective-permute-done((bf16[4,4,24,768]{3,2,1,0:T(8,128)(2,1)}, bf16[4,4,24,768]{3,2,1,0:T(8,128)(2,1)}, u32[]{:S(2)}, u32[]{:S(2)}) %collective-permute-start.6) | collective-permute-done | bytes 589856 | tf_op jit(solution)/shard_map/ppermute | solution.py:259
  112.5 2.1 %pair_sum.1 = bf16[4,8,24,768]{3,2,1,0:T(8,128)(2,1)} custom-call(bf16[4,8,24,768]{3,2,1,0:T(8,128)(2,1)S(1)} %copy-done.1, bf16[4,4,24,768]{3,2,1,0:T(8,128)(2,1)S(1)} %collective-permute-done.5.near_ref, bf16[4,4,24,768]{3,2,1,0:T(8,128)(2,1)} %collective-permute-done.6.far_ref), custom_call_target="tpu_custom_call" | custom-call | flops 60000002048 | tf_op jit(solution)/shard_map/pair_sum/pallas_call | solution.py:262
  114.6 5.5 %all-to-all-start.1 = ((bf16[4,8,24,768]{3,2,1,0:T(8,128)(2,1)}), bf16[4,8,24,768]{3,2,1,0:T(8,128)(2,1)S(1)}, u32[]{:S(2)}, u32[]{:S(2)}) async-start(bf16[4,8,24,768]{3,2,1,0:T(8,128)(2,1)} %pair_sum.1), calls=%async_computation.1 | async-start | bytes 2359296 | tf_op jit(solution)/shard_map/all_to_all | solution.py:275
  120.1 1.0 dynamic-slice_bitcast_fusion.hidden_ref
  121.1 27.8 %all-to-all-done.1.parts_ref = bf16[4,8,24,768]{3,2,1,0:T(8,128)(2,1)S(1)} async-done(((bf16[4,8,24,768]{3,2,1,0:T(8,128)(2,1)}), bf16[4,8,24,768]{3,2,1,0:T(8,128)(2,1)S(1)}, u32[]{:S(2)}, u32[]{:S(2)}) %all-to-all-start.1) | async-done | bytes 1179680 | tf_op jit(solution)/shard_map/all_to_all | solution.py:275
  148.8 1.0 finish.1
  149.9 2.1 %reduce-scatter.2.cloned.1.call-done = bf16[1,8,96,256]{3,2,1,0:T(8,128)(2,1)} async-done(((bf16[8,8,96,256]{3,2,1,0:T(8,128)(2,1)}), bf16[1,8,96,256]{3,2,1,0:T(8,128)(2,1)}) %reduce-scatter.2.cloned.1.call-update) | async-done | bytes 393232 | tf_op jit(solution)/shard_map/reduce_scatter | solution.py:252
  (12 shorter events, 0.1 us)
Async XLA Ops:
  7.2 28.8 %copy-start.2 = (s32[1,1,256,8]{2,3,1,0:T(8,128)S(1)}, s32[1,1,256,8]{2,3,1,0:T(8,128)}, u32[]{:S(2)}) copy-start(s32[1,1,256,8]{2,3,1,0:T(8,128)} %param.6) | copy-start | bytes 24580
  7.2 28.8 %copy-start.3 = (bf16[1,1,256,8]{2,3,1,0:T(8,128)(2,1)S(1)}, bf16[1,1,256,8]{2,3,1,0:T(8,128)(2,1)}, u32[]{:S(2)}) copy-start(bf16[1,1,256,8]{2,3,1,0:T(8,128)(2,1)} %param.7) | copy-start | bytes 12292
  7.2 75.7 %collective-permute-start.4 = (bf16[8,768,256]{2,1,0:T(8,128)(2,1)}, bf16[8,768,256]{2,1,0:T(8,128)(2,1)}, u32[]{:S(2)}, u32[]{:S(2)}) collective-permute-start(bf16[8,768,256]{2,1,0:T(8,128)(2,1)} %w_ref.1), channel_id=1, source_target_pairs={{0,8},{8,0},{16,24},{24,16},{32,40},{40,32},{48,56},{56,48},{64,72... | collective-permute-start | bytes 9437192 | tf_op jit(solution)/shard_map/ppermute | solution.py:164
  25.5 50.0 %all-to-all-start = ((bf16[128,16,256]{2,1,0:T(8,128)(2,1)}), bf16[128,16,256]{2,1,0:T(8,128)(2,1)S(1)}, u32[]{:S(2)}, u32[]{:S(2)}) async-start(bf16[128,16,256]{2,1,0:T(8,128)(2,1)} %bitcast.4), calls=%async_computation | async-start | bytes 2097152 | tf_op jit(solution)/shard_map/all_to_all | solution.py:171
  35.9 116.1 %reduce-scatter.2.cloned.1.call-start = ((), (), s32[]{:S(2)}) async-start(), calls=%async_computation.3 | async-start | bytes 3538944 | tf_op jit(solution)/shard_map/reduce_scatter | solution.py:252
  36.0 23.9 %collective-permute-start = (bf16[1,16,256]{2,1,0:T(8,128)(2,1)S(1)}, bf16[1,16,256]{2,1,0:T(8,128)(2,1)S(1)}, u32[]{:S(2)}, u32[]{:S(2)}) collective-permute-start(bf16[1,16,256]{2,1,0:T(8,128)(2,1)S(1)} %maximum_bitcast_fusion), channel_id=1, source_target_pairs={{0,1},{1,0},{2,3},{3,2},{4,5},{5,4},{6,7},{7,6},{8,9},{9,8},{10,11... | collective-permute-start | bytes 24584 | tf_op jit(solution)/shard_map/ppermute | solution.py:176
  59.8 5.8 %collective-permute-start.1 = (bf16[2,16,256]{2,1,0:T(8,128)(2,1)S(1)}, bf16[2,16,256]{2,1,0:T(8,128)(2,1)S(1)}, u32[]{:S(2)}, u32[]{:S(2)}) collective-permute-start(bf16[2,16,256]{2,1,0:T(8,128)(2,1)S(1)} %pad_maximum_fusion.2), channel_id=1, source_target_pairs={{0,2},{1,3},{2,0},{3,1},{4,6},{5,7},{6,4},{7,5},{8,10},{9,11},{10,... | collective-permute-start | bytes 49160 | tf_op jit(solution)/shard_map/ppermute | solution.py:176
  65.6 8.6 %collective-permute-start.2 = (bf16[4,16,256]{2,1,0:T(8,128)(2,1)S(1)}, bf16[4,16,256]{2,1,0:T(8,128)(2,1)S(1)}, u32[]{:S(2)}, u32[]{:S(2)}) collective-permute-start(bf16[4,16,256]{2,1,0:T(8,128)(2,1)S(1)} %pad_maximum_fusion.1), channel_id=1, source_target_pairs={{0,4},{1,5},{2,6},{3,7},{4,0},{5,1},{6,2},{7,3},{8,12},{9,13},{10,... | collective-permute-start | bytes 98312 | tf_op jit(solution)/shard_map/ppermute | solution.py:176
  75.5 7.4 %collective-permute-start.3 = (bf16[8,256,256]{2,1,0:T(8,128)(2,1)S(1)}, bf16[8,256,256]{2,1,0:T(8,128)(2,1)S(1)}, u32[]{:S(2)}, u32[]{:S(2)}) collective-permute-start(bf16[8,256,256]{2,1,0:T(8,128)(2,1)S(1)} %bitcast.26), channel_id=1, source_target_pairs={{0,8},{8,0},{16,24},{24,16},{32,40},{40,32},{48,56},{56,48},{64,72... | collective-permute-start | bytes 3145736 | tf_op jit(solution)/shard_map/ppermute | solution.py:202
  90.8 1.0 copy-start
  91.8 16.8 %collective-permute-start.5 = (bf16[4,4,24,768]{3,2,1,0:T(8,128)(2,1)}, bf16[4,4,24,768]{3,2,1,0:T(8,128)(2,1)S(1)}, u32[]{:S(2)}, u32[]{:S(2)}) collective-permute-start(bf16[4,4,24,768]{3,2,1,0:T(8,128)(2,1)} %get-tuple-element.22), channel_id=1, source_target_pairs={{0,16},{8,24},{16,0},{24,8},{32,48},{40,56},{48,32},{56,40},{64,80... | collective-permute-start | bytes 1769480 | tf_op jit(solution)/shard_map/ppermute | solution.py:258
  94.8 17.7 %collective-permute-start.6 = (bf16[4,4,24,768]{3,2,1,0:T(8,128)(2,1)}, bf16[4,4,24,768]{3,2,1,0:T(8,128)(2,1)}, u32[]{:S(2)}, u32[]{:S(2)}) collective-permute-start(bf16[4,4,24,768]{3,2,1,0:T(8,128)(2,1)} %get-tuple-element.23), channel_id=1, source_target_pairs={{0,112},{8,120},{16,32},{24,40},{32,16},{40,24},{48,64},{56,72},{6... | collective-permute-start | bytes 1769480 | tf_op jit(solution)/shard_map/ppermute | solution.py:259
  104.7 7.8 %copy-start.1 = (bf16[4,8,24,768]{3,2,1,0:T(8,128)(2,1)S(1)}, bf16[4,8,24,768]{3,2,1,0:T(8,128)(2,1)}, u32[]{:S(2)}) copy-start(bf16[4,8,24,768]{3,2,1,0:T(8,128)(2,1)} %copy-done) | copy-start | bytes 3538948
  114.6 34.2 %all-to-all-start.1 = ((bf16[4,8,24,768]{3,2,1,0:T(8,128)(2,1)}), bf16[4,8,24,768]{3,2,1,0:T(8,128)(2,1)S(1)}, u32[]{:S(2)}, u32[]{:S(2)}) async-start(bf16[4,8,24,768]{3,2,1,0:T(8,128)(2,1)} %pair_sum.1), calls=%async_computation.1 | async-start | bytes 2359296 | tf_op jit(solution)/shard_map/all_to_all | solution.py:275
Sparse Core Ops, SparseCore 0:
  104.9 47.0 reduce-scatter.1

commit v9 on v7

--- a/solution.py
+++ b/solution.py
@@ -86,21 +86,19 @@
 
 
 def part_kernel(
-    place, tok_ref, other_ref, hot_ref, w_ref, w_other_ref, keep_ref, near_ref, far_ref, mine, theirs
+    place, tok_ref, other_ref, hot_ref, w_ref, w_other_ref, keep_ref, give_ref, mine, theirs, *, low, half
 ):
-    columns, rows_half, _ = hot_ref.shape
+    columns, _, tokens = hot_ref.shape
     experts = mine.shape[0]
-    half = rows_half // experts
     step = pl.program_id(0)
     per = w_ref.shape[0]
 
     @pl.when(step == 0)
     def _():
         for c in range(columns):
+            hot = hot_ref[c, low * half : (low + experts) * half, :]
             for src, dst in ((tok_ref, mine), (other_ref, theirs)):
-                rows = jnp.dot(
-                    hot_ref[c], src[c, : hot_ref.shape[2]], preferred_element_type=F32
-                )
+                rows = jnp.dot(hot, src[c, :tokens], preferred_element_type=F32)
                 for x in range(experts):
                     dst[x, c * half : (c + 1) * half, :] = rows[x * half : (x + 1) * half]
 
@@ -114,21 +112,13 @@
         )
         part = part.reshape(columns // 2, 2, half, part.shape[1])
         keep_ref[:, i] = jnp.where(odd, part[:, 1], part[:, 0]).astype(BF)
-        give = jnp.where(odd, part[:, 0], part[:, 1]).astype(BF)
-
-        @pl.when(x < experts // 2)
-        def _():
-            near_ref[:, i] = give
-
-        @pl.when(x >= experts // 2)
-        def _():
-            far_ref[:, i] = give
-
-
-def add_kernel(keep_ref, near_ref, far_ref, out_ref):
+        give_ref[:, i] = jnp.where(odd, part[:, 0], part[:, 1]).astype(BF)
+
+
+def add_kernel(keep_a_ref, keep_b_ref, near_ref, far_ref, out_ref):
     h = near_ref.shape[1]
-    out_ref[:, :h] = (keep_ref[:, :h].astype(F32) + near_ref[...].astype(F32)).astype(BF)
-    out_ref[:, h:] = (keep_ref[:, h:].astype(F32) + far_ref[...].astype(F32)).astype(BF)
+    out_ref[:, :h] = (keep_a_ref[...].astype(F32) + near_ref[...].astype(F32)).astype(BF)
+    out_ref[:, h:] = (keep_b_ref[...].astype(F32) + far_ref[...].astype(F32)).astype(BF)
 
 
 def finish_kernel(parts_ref, gate_ref, hidden_ref, grad_ref, gates_ref):
@@ -197,71 +187,66 @@
     per = 2
     per_expert = lambda *shape: pl.BlockSpec((per,) + shape, lambda x: (x, 0, 0))
     block_f = width // n_dp
-    pairs, near_steps = chips // 2, experts // per // 2
-    out_block = (pairs, per, half, width)
-    per_expert_p = lambda *shape: pl.BlockSpec((per,) + shape, lambda x, p: (x, 0, 0))
-    keep, near, far = pl.pallas_call(
-        part_kernel,
-        out_shape=(
-            jax.ShapeDtypeStruct((pairs, experts, half, width), BF),
-            jax.ShapeDtypeStruct((pairs, experts // 2, half, width), BF),
-            jax.ShapeDtypeStruct((pairs, experts // 2, half, width), BF),
-        ),
-        grid_spec=pltpu.PrefetchScalarGridSpec(
-            num_scalar_prefetch=1,
-            grid=(experts // per,),
-            in_specs=[
-                vmem,
-                vmem,
-                vmem,
-                per_expert_p(width, block),
-                per_expert_p(width, block),
-            ],
-            out_specs=(
-                pl.BlockSpec(out_block, lambda x, p: (0, x, 0, 0)),
-                pl.BlockSpec(out_block, lambda x, p: (0, jnp.minimum(x, near_steps - 1), 0, 0)),
-                pl.BlockSpec(out_block, lambda x, p: (0, jnp.maximum(x - near_steps, 0), 0, 0)),
+    pairs = chips // 2
+    per_expert_p = lambda low, *shape: pl.BlockSpec((per,) + shape, lambda x, p: (x + low // per, 0, 0))
+
+    def hidden_parts(low, count, hot):
+        out = jax.ShapeDtypeStruct((pairs, count, half, width), BF)
+        return pl.pallas_call(
+            functools.partial(part_kernel, low=low, half=half),
+            out_shape=(out, out),
+            grid_spec=pltpu.PrefetchScalarGridSpec(
+                num_scalar_prefetch=1,
+                grid=(count // per,),
+                in_specs=[
+                    vmem,
+                    vmem,
+                    vmem,
+                    per_expert_p(low, width, block),
+                    per_expert_p(low, width, block),
+                ],
+                out_specs=(pl.BlockSpec((pairs, per, half, width), lambda x, p: (0, x, 0, 0)),) * 2,
+                scratch_shapes=[pltpu.VMEM((count, slots // 2, block), F32)] * 2,
             ),
-            scratch_shapes=[pltpu.VMEM((experts, slots // 2, block), F32)] * 2,
-        ),
-        compiler_params=pltpu.CompilerParams(vmem_limit_bytes=32 * 1024 * 1024),
-        cost_estimate=cost,
-        name="hidden_part",
-    )(place, tok, other, hot, w_down, w_other)
-
-    most_per = 4
-    scaled_hot, _ = lax.optimization_barrier((scaled_hot, keep))
+            compiler_params=pltpu.CompilerParams(vmem_limit_bytes=32 * 1024 * 1024),
+            cost_estimate=cost,
+            name="hidden_part",
+        )(place, tok, other, hot, w_down, w_other)
+
+    def swap(shift):
+        at = lambda z: (z ^ 1) if shift == 0 else ((((z + 1) % chips) ^ 1) - 1) % chips
+        return [(2 * z + c, 2 * at(z) + c) for z in range(chips) for c in range(2)]
+
+    split = experts - per
+    keep_a, near = hidden_parts(0, split, hot)
+    near_back = lax.ppermute(near, "tensor", swap(0))
+    scaled_hot, _ = lax.optimization_barrier((scaled_hot, near))
     partial = pl.pallas_call(
         weight_kernel,
         out_shape=jax.ShapeDtypeStruct((n_dp, experts, block_f, block), BF),
-        grid=(experts // most_per,),
-        in_specs=[vmem, vmem, pl.BlockSpec((most_per, slots, width), lambda x: (x, 0, 0))],
-        out_specs=pl.BlockSpec((n_dp, most_per, block_f, block), lambda x: (0, x, 0, 0)),
+        grid=(experts // 4,),
+        in_specs=[vmem, vmem, pl.BlockSpec((4, slots, width), lambda x: (x, 0, 0))],
+        out_specs=pl.BlockSpec((n_dp, 4, block_f, block), lambda x: (0, x, 0, 0)),
         scratch_shapes=[pltpu.VMEM((experts, slots, block), BF)],
         compiler_params=params,
         cost_estimate=cost,
         name="weight_part",
     )(tok, scaled_hot, hidden_saved[0])
     total = lax.psum_scatter(partial, "dp", scatter_dimension=0, tiled=True)[0]
-
-    def swap(shift):
-        at = lambda z: (z ^ 1) if shift == 0 else ((((z + 1) % chips) ^ 1) - 1) % chips
-        return [(2 * z + c, 2 * at(z) + c) for z in range(chips) for c in range(2)]
-
-    near = lax.ppermute(near, "tensor", swap(0))
-    far = lax.ppermute(far, "tensor", swap(1))
-    keep, _ = lax.optimization_barrier((keep, partial))
+    hot_late, _ = lax.optimization_barrier((hot, partial))
+    keep_b, far = hidden_parts(split, experts - split, hot_late)
+    far_back = lax.ppermute(far, "tensor", swap(1))
     row = lambda n: pl.BlockSpec((2, n, half, width), lambda m: (m, 0, 0, 0))
     parts = pl.pallas_call(
         add_kernel,
-        out_shape=jax.ShapeDtypeStruct(keep.shape, BF),
+        out_shape=jax.ShapeDtypeStruct((pairs, experts, half, width), BF),
         grid=(pairs // 2,),
-        in_specs=[row(experts), row(experts // 2), row(experts // 2)],
+        in_specs=[row(split), row(experts - split), row(split), row(experts - split)],
         out_specs=row(experts),
         compiler_params=params,
-        cost_estimate=pl.CostEstimate(flops=60000000000, bytes_accessed=0, transcendentals=0),
+        cost_estimate=pl.CostEstimate(flops=42000000000, bytes_accessed=0, transcendentals=0),
         name="pair_sum",
-    )(keep, near, far)
+    )(keep_a, keep_b, near_back, far_back)
     same_kind = [
         [2 * (2 * m + p) + c for m in range(pairs)] for p in range(2) for c in range(2)
     ]

time: 150 us -> 153 us (1.020)
  local copies, waits for them, and re-layouts: 2.7 us -> 5.55 us
    unnamed x3 -> x9, local copies, waits for them, and re-layouts: 0.93 us -> 3.78 us
    pallas_call x2 -> x3, Pallas kernels: 9.48 us -> 10.5 us  [the longest x2 8.26 us: hidden_parts(): pl.pallas_call(functools.partial(part_kernel, low=low, half=half), out_sh...]
  transfers between devices with their start and end apart: 7 -> 7, of which waited for: 5 -> 4; matrix products, arithmetic and copies ran while one was open for 2% -> 2% of each run, Pallas kernels for 7% -> 8%
where the time goes in v9:
time: 153 us; the launch traced here: 151 us
  waiting for transfers between devices  44 us (29%)
  blocking collectives  36.9 us (24%)
  starting transfers between devices  30.5 us (20%)
  Pallas kernels  18.2 us (12%)
  between operations  14.1 us (9%)
  local copies, waits for them, and re-layouts  5.55 us (4%)
    all_to_all x1, blocking collectives, local(): tok = lax.all_to_all(packed, 'expert', 0, 0, tiled=True)  36.9 us
    all_to_all x1, waiting for transfers between devices, local(): lax.all_to_all(parts, 'tensor', 0, 0, tiled=True, axis_index_groups=same_...  27.9 us
    all_to_all x1, starting transfers between devices, local(): lax.all_to_all(send, 'tensor', 0, 0, tiled=True).reshape(tokens, block)  18.2 us
    ppermute x1, waiting for transfers between devices, local(): far_back = lax.ppermute(far, 'tensor', swap(1))  8.73 us
    pallas_call x2, Pallas kernels, hidden_parts(): pl.pallas_call(functools.partial(part_kernel, low=low, half=half), out_sh...  8.26 us
    all_to_all x1, waiting for transfers between devices, local(): lax.all_to_all(send, 'tensor', 0, 0, tiled=True).reshape(tokens, block)  6.4 us
    pallas_call x1, Pallas kernels, local(): pl.pallas_call(weight_kernel, out_shape=jax.ShapeDtypeStruct((n_dp, exper...  5.51 us
    unnamed x9, local copies, waits for them, and re-layouts  3.78 us
  transfers between devices with their start and end apart: 7, of which 4 were waited for; matrix products, arithmetic and copies ran while one was open for 2% of the time, Pallas kernels for 8%

profile of v9, /device:TPU:1, one launch (start us, length us, event | category | flops | bytes accessed | tf_op | source)
XLA Modules:
  0.0 150.8 jit_solution(4096821482723658414)
XLA Ops:
  7.2 0.9 copy.10
  8.1 0.7 copy.9
  8.8 18.2 %all-to-all-start = ((bf16[16,16,256]{2,1,0:T(8,128)(2,1)}), bf16[16,16,256]{2,1,0:T(8,128)(2,1)S(1)}, u32[]{:S(2)}, u32[]{:S(2)}) async-start(bf16[16,16,256]{2,1,0:T(8,128)(2,1)} %copy.9), calls=%async_computation | async-start | bytes 262144 | tf_op jit(solution)/shard_map/all_to_all | solution.py:159
  27.0 0.0 reduce-scatter.2.cloned.1.call-start
  27.0 2.0 %collective-permute-start.1 = (bf16[8,768,256]{2,1,0:T(8,128)(2,1)}, bf16[8,768,256]{2,1,0:T(8,128)(2,1)}, u32[]{:S(2)}, u32[]{:S(2)}) collective-permute-start(bf16[8,768,256]{2,1,0:T(8,128)(2,1)} %w_ref.3), channel_id=1, source_target_pairs={{0,8},{8,0},{16,24},{24,16},{32,40},{40,32},{48,56},{56,48},{64,72... | collective-permute-start | bytes 9437192 | tf_op jit(solution)/shard_map/ppermute | solution.py:154
  29.1 0.7 convert_bitcast_fusion
  29.8 6.4 %all-to-all-done = bf16[16,16,256]{2,1,0:T(8,128)(2,1)S(1)} async-done(((bf16[16,16,256]{2,1,0:T(8,128)(2,1)}), bf16[16,16,256]{2,1,0:T(8,128)(2,1)S(1)}, u32[]{:S(2)}, u32[]{:S(2)}) %all-to-all-start) | async-done | bytes 131104 | tf_op jit(solution)/shard_map/all_to_all | solution.py:159
  36.2 0.7 pad_maximum_fusion
  36.9 0.1 broadcast_in_dim.12
  36.9 36.9 %all_to_all.15.meta_ref.tok_ref = bf16[8,272,256]{2,1,0:T(8,128)(2,1)S(1)} all-to-all(bf16[8,272,256]{2,1,0:T(8,128)(2,1)S(1)} %broadcast_in_dim.12), channel_id=1, replica_groups=mesh['dp'=8,'tensor'=16,'expert'=8] {'expert'}, dimensions={0} | all-to-all | bytes 2228224 | tf_op jit(solution)/shard_map/all_to_all | solution.py:162
  73.9 2.3 %collective-permute-start = (bf16[8,272,256]{2,1,0:T(8,128)(2,1)S(1)}, bf16[8,272,256]{2,1,0:T(8,128)(2,1)S(1)}, u32[]{:S(2)}, u32[]{:S(2)}) collective-permute-start(bf16[8,272,256]{2,1,0:T(8,128)(2,1)S(1)} %all_to_all.15.meta_ref.tok_ref), channel_id=1, source_target_pairs={{0,8},{8,0},{16,24},{24,16},{32,40},{40,32},{48,56},{56,48},{64,72... | collective-permute-start | bytes 3342344 | tf_op jit(solution)/shard_map/ppermute | solution.py:185
  76.2 0.1 pad_add_fusion.place
  76.3 1.2 pick.1
  77.6 0.0 collective-permute-done.1.w_other_ref
  77.6 1.0 collective-permute-done.other_ref
  78.6 0.0 copy-done
  78.6 5.5 %hidden_part.2 = (bf16[4,6,24,768]{3,2,1,0:T(8,128)(2,1)S(1)}, bf16[4,6,24,768]{3,2,1,0:T(8,128)(2,1)}) custom-call(s32[3]{0:T(128)S(1)} %pad_add_fusion.place, bf16[8,272,256]{2,1,0:T(8,128)(2,1)S(1)} %all_to_all.15.meta_ref.tok_ref, bf16[8,272,256]{2,1,0:T(8,128)(2,1)S(1)} %collective-permute-done.other_ref, ...), custom_call_target="tpu_custom_call" | custom-call | flops 1610612736 | bytes 3145728 | tf_op jit(solution)/shard_map/hidden_part/pallas_call | solution.py:195
  84.1 1.0 copy-done.2
  85.1 2.0 %collective-permute-start.2 = (bf16[4,6,24,768]{3,2,1,0:T(8,128)(2,1)}, bf16[4,6,24,768]{3,2,1,0:T(8,128)(2,1)}, u32[]{:S(2)}, u32[]{:S(2)}) collective-permute-start(bf16[4,6,24,768]{3,2,1,0:T(8,128)(2,1)} %get-tuple-element.17), channel_id=1, source_target_pairs={{0,16},{8,24},{16,0},{24,8},{32,48},{40,56},{48,32},{56,40},{64,80... | collective-permute-start | bytes 2654216 | tf_op jit(solution)/shard_map/ppermute | solution.py:222
  87.1 5.5 %weight_part.1 = bf16[8,8,96,256]{3,2,1,0:T(8,128)(2,1)} custom-call(bf16[8,272,256]{2,1,0:T(8,128)(2,1)S(1)} %all_to_all.15.meta_ref.tok_ref, bf16[8,384,256]{2,1,0:T(8,128)(2,1)S(1)} %get-tuple-element.18.hot_ref, bf16[8,384,768]{2,1,0:T(8,128)(2,1)} %bitcast.23), custom_call_target="tpu_custom_call" | custom-call | flops 1610612736 | bytes 3145728 | tf_op jit(solution)/shard_map/weight_part/pallas_call | solution.py:224
  92.6 0.0 reduce-scatter.2.cloned.1.call-update
  92.6 0.0 copy-start.1
  92.6 1.9 %copy-done.1 = bf16[8,768,256]{2,1,0:T(8,128)(2,1)S(1)} copy-done((bf16[8,768,256]{2,1,0:T(8,128)(2,1)S(1)}, bf16[8,768,256]{2,1,0:T(8,128)(2,1)}, u32[]{:S(2)}) %copy-start.1) | copy-done | bytes 3145752
  94.5 2.7 %hidden_part.3 = (bf16[4,2,24,768]{3,2,1,0:T(8,128)(2,1)S(1)}, bf16[4,2,24,768]{3,2,1,0:T(8,128)(2,1)S(1)}) custom-call(s32[3]{0:T(128)S(1)} %pad_add_fusion.place, bf16[8,272,256]{2,1,0:T(8,128)(2,1)S(1)} %all_to_all.15.meta_ref.tok_ref, bf16[8,272,256]{2,1,0:T(8,128)(2,1)S(1)} %collective-permute-done.other_ref, ...), custom_call_target="tpu_custom_call" | custom-call | flops 1610612736 | bytes 3145728 | tf_op jit(solution)/shard_map/hidden_part/pallas_call | solution.py:195
  97.2 2.4 %collective-permute-start.3 = (bf16[4,2,24,768]{3,2,1,0:T(8,128)(2,1)S(1)}, bf16[4,2,24,768]{3,2,1,0:T(8,128)(2,1)S(1)}, u32[]{:S(2)}, u32[]{:S(2)}) collective-permute-start(bf16[4,2,24,768]{3,2,1,0:T(8,128)(2,1)S(1)} %get-tuple-element.21), channel_id=1, source_target_pairs={{0,112},{8,120},{16,32},{24,40},{32,16},{40,24},{48,64},{56,72},{6... | collective-permute-start | bytes 884744 | tf_op jit(solution)/shard_map/ppermute | solution.py:238
  99.6 8.7 %collective-permute-done.3.far_ref = bf16[4,2,24,768]{3,2,1,0:T(8,128)(2,1)S(1)} collective-permute-done((bf16[4,2,24,768]{3,2,1,0:T(8,128)(2,1)S(1)}, bf16[4,2,24,768]{3,2,1,0:T(8,128)(2,1)S(1)}, u32[]{:S(2)}, u32[]{:S(2)}) %collective-permute-start.3) | collective-permute-done | bytes 294944 | tf_op jit(solution)/shard_map/ppermute | solution.py:238
  108.3 0.0 collective-permute-done.2.near_ref
  108.3 2.2 %pair_sum.1 = bf16[4,8,24,768]{3,2,1,0:T(8,128)(2,1)} custom-call(bf16[4,6,24,768]{3,2,1,0:T(8,128)(2,1)S(1)} %copy-done.3, bf16[4,2,24,768]{3,2,1,0:T(8,128)(2,1)S(1)} %get-tuple-element.20.keep_b_ref, bf16[4,6,24,768]{3,2,1,0:T(8,128)(2,1)} %collective-permute-done.2.near_ref, bf16[4,2,24,768]{3,2,1,0:T(8,128)(2,1)S(1)} %collective-permute-done.3.far_ref), custom_call_target="tpu_custom_call" | custom-call | flops 41999998976 | tf_op jit(solution)/shard_map/pair_sum/pallas_call | solution.py:240
  110.5 3.5 %all-to-all-start.2 = ((bf16[4,8,24,768]{3,2,1,0:T(8,128)(2,1)}), bf16[4,8,24,768]{3,2,1,0:T(8,128)(2,1)S(1)}, u32[]{:S(2)}, u32[]{:S(2)}) async-start(bf16[4,8,24,768]{3,2,1,0:T(8,128)(2,1)} %pair_sum.1), calls=%async_computation.2 | async-start | bytes 2359296 | tf_op jit(solution)/shard_map/all_to_all | solution.py:253
  114.1 1.0 dynamic-slice_bitcast_fusion.hidden_ref
  115.1 27.9 %all-to-all-done.2.parts_ref = bf16[4,8,24,768]{3,2,1,0:T(8,128)(2,1)S(1)} async-done(((bf16[4,8,24,768]{3,2,1,0:T(8,128)(2,1)}), bf16[4,8,24,768]{3,2,1,0:T(8,128)(2,1)S(1)}, u32[]{:S(2)}, u32[]{:S(2)}) %all-to-all-start.2) | async-done | bytes 1179680 | tf_op jit(solution)/shard_map/all_to_all | solution.py:253
  142.9 1.0 finish.1
  (5 shorter events, 0.0 us)
Async XLA Ops:
  8.8 27.4 %all-to-all-start = ((bf16[16,16,256]{2,1,0:T(8,128)(2,1)}), bf16[16,16,256]{2,1,0:T(8,128)(2,1)S(1)}, u32[]{:S(2)}, u32[]{:S(2)}) async-start(bf16[16,16,256]{2,1,0:T(8,128)(2,1)} %copy.9), calls=%async_computation | async-start | bytes 262144 | tf_op jit(solution)/shard_map/all_to_all | solution.py:159
  27.0 117.0 %reduce-scatter.2.cloned.1.call-start = ((), (), s32[]{:S(2)}) async-start(), calls=%async_computation.4 | async-start | bytes 3538944 | tf_op jit(solution)/shard_map/reduce_scatter | solution.py:235
  27.0 50.5 %collective-permute-start.1 = (bf16[8,768,256]{2,1,0:T(8,128)(2,1)}, bf16[8,768,256]{2,1,0:T(8,128)(2,1)}, u32[]{:S(2)}, u32[]{:S(2)}) collective-permute-start(bf16[8,768,256]{2,1,0:T(8,128)(2,1)} %w_ref.3), channel_id=1, source_target_pairs={{0,8},{8,0},{16,24},{24,16},{32,40},{40,32},{48,56},{56,48},{64,72... | collective-permute-start | bytes 9437192 | tf_op jit(solution)/shard_map/ppermute | solution.py:154
  73.9 4.7 %collective-permute-start = (bf16[8,272,256]{2,1,0:T(8,128)(2,1)S(1)}, bf16[8,272,256]{2,1,0:T(8,128)(2,1)S(1)}, u32[]{:S(2)}, u32[]{:S(2)}) collective-permute-start(bf16[8,272,256]{2,1,0:T(8,128)(2,1)S(1)} %all_to_all.15.meta_ref.tok_ref), channel_id=1, source_target_pairs={{0,8},{8,0},{16,24},{24,16},{32,40},{40,32},{48,56},{56,48},{64,72... | collective-permute-start | bytes 3342344 | tf_op jit(solution)/shard_map/ppermute | solution.py:185
  76.3 2.3 %copy-start = (bf16[8,768,256]{2,1,0:T(8,128)(2,1)S(1)}, bf16[8,768,256]{2,1,0:T(8,128)(2,1)}, u32[]{:S(2)}) copy-start(bf16[8,768,256]{2,1,0:T(8,128)(2,1)} %w_ref.3) | copy-start | bytes 9437188
  84.1 1.0 copy-start.2
  85.1 23.3 %collective-permute-start.2 = (bf16[4,6,24,768]{3,2,1,0:T(8,128)(2,1)}, bf16[4,6,24,768]{3,2,1,0:T(8,128)(2,1)}, u32[]{:S(2)}, u32[]{:S(2)}) collective-permute-start(bf16[4,6,24,768]{3,2,1,0:T(8,128)(2,1)} %get-tuple-element.17), channel_id=1, source_target_pairs={{0,16},{8,24},{16,0},{24,8},{32,48},{40,56},{48,32},{56,40},{64,80... | collective-permute-start | bytes 2654216 | tf_op jit(solution)/shard_map/ppermute | solution.py:222
  92.6 1.9 %copy-start.1 = (bf16[8,768,256]{2,1,0:T(8,128)(2,1)S(1)}, bf16[8,768,256]{2,1,0:T(8,128)(2,1)}, u32[]{:S(2)}) copy-start(bf16[8,768,256]{2,1,0:T(8,128)(2,1)} %w_ref.3) | copy-start | bytes 9437188
  94.5 13.8 %copy-start.3 = (bf16[4,6,24,768]{3,2,1,0:T(8,128)(2,1)S(1)}, bf16[4,6,24,768]{3,2,1,0:T(8,128)(2,1)}, u32[]{:S(2)}) copy-start(bf16[4,6,24,768]{3,2,1,0:T(8,128)(2,1)} %copy-done.2) | copy-start | bytes 2654212
  97.2 11.1 %collective-permute-start.3 = (bf16[4,2,24,768]{3,2,1,0:T(8,128)(2,1)S(1)}, bf16[4,2,24,768]{3,2,1,0:T(8,128)(2,1)S(1)}, u32[]{:S(2)}, u32[]{:S(2)}) collective-permute-start(bf16[4,2,24,768]{3,2,1,0:T(8,128)(2,1)S(1)} %get-tuple-element.21), channel_id=1, source_target_pairs={{0,112},{8,120},{16,32},{24,40},{32,16},{40,24},{48,64},{56,72},{6... | collective-permute-start | bytes 884744 | tf_op jit(solution)/shard_map/ppermute | solution.py:238
  110.5 32.4 %all-to-all-start.2 = ((bf16[4,8,24,768]{3,2,1,0:T(8,128)(2,1)}), bf16[4,8,24,768]{3,2,1,0:T(8,128)(2,1)S(1)}, u32[]{:S(2)}, u32[]{:S(2)}) async-start(bf16[4,8,24,768]{3,2,1,0:T(8,128)(2,1)} %pair_sum.1), calls=%async_computation.2 | async-start | bytes 2359296 | tf_op jit(solution)/shard_map/all_to_all | solution.py:253
Sparse Core Ops, SparseCore 0:
  92.7 41.8 reduce-scatter.1

commit v10 on v9

--- a/solution.py
+++ b/solution.py
@@ -208,7 +208,7 @@
                 out_specs=(pl.BlockSpec((pairs, per, half, width), lambda x, p: (0, x, 0, 0)),) * 2,
                 scratch_shapes=[pltpu.VMEM((count, slots // 2, block), F32)] * 2,
             ),
-            compiler_params=pltpu.CompilerParams(vmem_limit_bytes=32 * 1024 * 1024),
+            compiler_params=pltpu.CompilerParams(vmem_limit_bytes=48 * 1024 * 1024),
             cost_estimate=cost,
             name="hidden_part",
         )(place, tok, other, hot, w_down, w_other)

time: 153 us -> 152 us (level)
  local copies, waits for them, and re-layouts: 5.55 us -> 3.67 us
    unnamed x9 -> x5, local copies, waits for them, and re-layouts: 3.78 us -> 1.91 us
  transfers between devices with their start and end apart: 7 -> 7, of which waited for: 4 -> 5; matrix products, arithmetic and copies ran while one was open for 2% -> 2% of each run, Pallas kernels for 8% -> 9%
where the time goes in v10:
time: 152 us; the launch traced here: 151 us
  waiting for transfers between devices  45.4 us (30%)
  blocking collectives  36.9 us (24%)
  starting transfers between devices  30.5 us (20%)
  Pallas kernels  18.9 us (12%)
  between operations  14.1 us (9%)
  local copies, waits for them, and re-layouts  3.67 us (2%)
    all_to_all x1, blocking collectives, local(): tok = lax.all_to_all(packed, 'expert', 0, 0, tiled=True)  36.9 us
    all_to_all x1, waiting for transfers between devices, local(): lax.all_to_all(parts, 'tensor', 0, 0, tiled=True, axis_index_groups=same_...  27.7 us
    all_to_all x1, starting transfers between devices, local(): lax.all_to_all(send, 'tensor', 0, 0, tiled=True).reshape(tokens, block)  18.2 us
    pallas_call x2, Pallas kernels, hidden_parts(): pl.pallas_call(functools.partial(part_kernel, low=low, half=half), out_sh...  8.96 us
    ppermute x1, waiting for transfers between devices, local(): far_back = lax.ppermute(far, 'tensor', swap(1))  8.7 us
    all_to_all x1, waiting for transfers between devices, local(): lax.all_to_all(send, 'tensor', 0, 0, tiled=True).reshape(tokens, block)  6.4 us
    pallas_call x1, Pallas kernels, local(): pl.pallas_call(weight_kernel, out_shape=jax.ShapeDtypeStruct((n_dp, exper...  5.5 us
    all_to_all x1, starting transfers between devices, local(): lax.all_to_all(parts, 'tensor', 0, 0, tiled=True, axis_index_groups=same_...  3.53 us
  transfers between devices with their start and end apart: 7, of which 5 were waited for; matrix products, arithmetic and copies ran while one was open for 2% of the time, Pallas kernels for 9%

profile of v10, /device:TPU:1, one launch (start us, length us, event | category | flops | bytes accessed | tf_op | source)
XLA Modules:
  0.0 151.0 jit_solution(17103230536669988864)
XLA Ops:
  7.2 0.9 copy.10
  8.1 0.7 copy.9
  8.8 18.2 %all-to-all-start = ((bf16[16,16,256]{2,1,0:T(8,128)(2,1)}), bf16[16,16,256]{2,1,0:T(8,128)(2,1)S(1)}, u32[]{:S(2)}, u32[]{:S(2)}) async-start(bf16[16,16,256]{2,1,0:T(8,128)(2,1)} %copy.9), calls=%async_computation | async-start | bytes 262144 | tf_op jit(solution)/shard_map/all_to_all | solution.py:159
  27.0 0.0 reduce-scatter.2.cloned.1.call-start
  27.0 2.0 %collective-permute-start.1 = (bf16[8,768,256]{2,1,0:T(8,128)(2,1)}, bf16[8,768,256]{2,1,0:T(8,128)(2,1)}, u32[]{:S(2)}, u32[]{:S(2)}) collective-permute-start(bf16[8,768,256]{2,1,0:T(8,128)(2,1)} %w_ref.3), channel_id=1, source_target_pairs={{0,8},{8,0},{16,24},{24,16},{32,40},{40,32},{48,56},{56,48},{64,72... | collective-permute-start | bytes 9437192 | tf_op jit(solution)/shard_map/ppermute | solution.py:154
  29.1 0.7 convert_bitcast_fusion
  29.8 6.4 %all-to-all-done = bf16[16,16,256]{2,1,0:T(8,128)(2,1)S(1)} async-done(((bf16[16,16,256]{2,1,0:T(8,128)(2,1)}), bf16[16,16,256]{2,1,0:T(8,128)(2,1)S(1)}, u32[]{:S(2)}, u32[]{:S(2)}) %all-to-all-start) | async-done | bytes 131104 | tf_op jit(solution)/shard_map/all_to_all | solution.py:159
  36.2 0.7 pad_maximum_fusion
  36.9 0.1 broadcast_in_dim.12
  36.9 36.9 %all_to_all.15.meta_ref.tok_ref = bf16[8,272,256]{2,1,0:T(8,128)(2,1)S(1)} all-to-all(bf16[8,272,256]{2,1,0:T(8,128)(2,1)S(1)} %broadcast_in_dim.12), channel_id=1, replica_groups=mesh['dp'=8,'tensor'=16,'expert'=8] {'expert'}, dimensions={0} | all-to-all | bytes 2228224 | tf_op jit(solution)/shard_map/all_to_all | solution.py:162
  73.9 2.3 %collective-permute-start = (bf16[8,272,256]{2,1,0:T(8,128)(2,1)S(1)}, bf16[8,272,256]{2,1,0:T(8,128)(2,1)S(1)}, u32[]{:S(2)}, u32[]{:S(2)}) collective-permute-start(bf16[8,272,256]{2,1,0:T(8,128)(2,1)S(1)} %all_to_all.15.meta_ref.tok_ref), channel_id=1, source_target_pairs={{0,8},{8,0},{16,24},{24,16},{32,40},{40,32},{48,56},{56,48},{64,72... | collective-permute-start | bytes 3342344 | tf_op jit(solution)/shard_map/ppermute | solution.py:185
  76.2 0.1 pad_add_fusion.place
  76.3 1.2 pick.1
  77.6 0.0 collective-permute-done.1.w_other_ref
  77.6 1.0 collective-permute-done.other_ref
  78.6 6.0 %hidden_part.2 = (bf16[4,6,24,768]{3,2,1,0:T(8,128)(2,1)S(1)}, bf16[4,6,24,768]{3,2,1,0:T(8,128)(2,1)}) custom-call(s32[3]{0:T(128)S(1)} %pad_add_fusion.place, bf16[8,272,256]{2,1,0:T(8,128)(2,1)S(1)} %all_to_all.15.meta_ref.tok_ref, bf16[8,272,256]{2,1,0:T(8,128)(2,1)S(1)} %collective-permute-done.other_ref, ...), custom_call_target="tpu_custom_call" | custom-call | flops 1610612736 | bytes 3145728 | tf_op jit(solution)/shard_map/hidden_part/pallas_call | solution.py:195
  84.6 0.0 copy-start
  84.6 1.0 copy-done
  85.6 2.0 %collective-permute-start.2 = (bf16[4,6,24,768]{3,2,1,0:T(8,128)(2,1)}, bf16[4,6,24,768]{3,2,1,0:T(8,128)(2,1)}, u32[]{:S(2)}, u32[]{:S(2)}) collective-permute-start(bf16[4,6,24,768]{3,2,1,0:T(8,128)(2,1)} %get-tuple-element.17), channel_id=1, source_target_pairs={{0,16},{8,24},{16,0},{24,8},{32,48},{40,56},{48,32},{56,40},{64,80... | collective-permute-start | bytes 2654216 | tf_op jit(solution)/shard_map/ppermute | solution.py:222
  87.5 5.5 %weight_part.1 = bf16[8,8,96,256]{3,2,1,0:T(8,128)(2,1)} custom-call(bf16[8,272,256]{2,1,0:T(8,128)(2,1)S(1)} %all_to_all.15.meta_ref.tok_ref, bf16[8,384,256]{2,1,0:T(8,128)(2,1)S(1)} %get-tuple-element.18.hot_ref, bf16[8,384,768]{2,1,0:T(8,128)(2,1)} %bitcast.23), custom_call_target="tpu_custom_call" | custom-call | flops 1610612736 | bytes 3145728 | tf_op jit(solution)/shard_map/weight_part/pallas_call | solution.py:224
  93.0 0.0 reduce-scatter.2.cloned.1.call-update
  93.1 0.0 copy-start.1
  93.1 3.0 %hidden_part.3 = (bf16[4,2,24,768]{3,2,1,0:T(8,128)(2,1)S(1)}, bf16[4,2,24,768]{3,2,1,0:T(8,128)(2,1)S(1)}) custom-call(s32[3]{0:T(128)S(1)} %pad_add_fusion.place, bf16[8,272,256]{2,1,0:T(8,128)(2,1)S(1)} %all_to_all.15.meta_ref.tok_ref, bf16[8,272,256]{2,1,0:T(8,128)(2,1)S(1)} %collective-permute-done.other_ref, ...), custom_call_target="tpu_custom_call" | custom-call | flops 1610612736 | bytes 3145728 | tf_op jit(solution)/shard_map/hidden_part/pallas_call | solution.py:195
  96.0 2.4 %collective-permute-start.3 = (bf16[4,2,24,768]{3,2,1,0:T(8,128)(2,1)S(1)}, bf16[4,2,24,768]{3,2,1,0:T(8,128)(2,1)S(1)}, u32[]{:S(2)}, u32[]{:S(2)}) collective-permute-start(bf16[4,2,24,768]{3,2,1,0:T(8,128)(2,1)S(1)} %get-tuple-element.21), channel_id=1, source_target_pairs={{0,112},{8,120},{16,32},{24,40},{32,16},{40,24},{48,64},{56,72},{6... | collective-permute-start | bytes 884744 | tf_op jit(solution)/shard_map/ppermute | solution.py:238
  98.4 8.7 %collective-permute-done.3.far_ref = bf16[4,2,24,768]{3,2,1,0:T(8,128)(2,1)S(1)} collective-permute-done((bf16[4,2,24,768]{3,2,1,0:T(8,128)(2,1)S(1)}, bf16[4,2,24,768]{3,2,1,0:T(8,128)(2,1)S(1)}, u32[]{:S(2)}, u32[]{:S(2)}) %collective-permute-start.3) | collective-permute-done | bytes 294944 | tf_op jit(solution)/shard_map/ppermute | solution.py:238
  107.1 1.5 collective-permute-done.2.near_ref
  108.6 0.0 copy-done.1
  108.6 2.2 %pair_sum.1 = bf16[4,8,24,768]{3,2,1,0:T(8,128)(2,1)} custom-call(bf16[4,6,24,768]{3,2,1,0:T(8,128)(2,1)S(1)} %copy-done.1, bf16[4,2,24,768]{3,2,1,0:T(8,128)(2,1)S(1)} %get-tuple-element.20.keep_b_ref, bf16[4,6,24,768]{3,2,1,0:T(8,128)(2,1)} %collective-permute-done.2.near_ref, bf16[4,2,24,768]{3,2,1,0:T(8,128)(2,1)S(1)} %collective-permute-done.3.far_ref), custom_call_target="tpu_custom_call" | custom-call | flops 41999998976 | tf_op jit(solution)/shard_map/pair_sum/pallas_call | solution.py:240
  110.8 3.5 %all-to-all-start.2 = ((bf16[4,8,24,768]{3,2,1,0:T(8,128)(2,1)}), bf16[4,8,24,768]{3,2,1,0:T(8,128)(2,1)S(1)}, u32[]{:S(2)}, u32[]{:S(2)}) async-start(bf16[4,8,24,768]{3,2,1,0:T(8,128)(2,1)} %pair_sum.1), calls=%async_computation.2 | async-start | bytes 2359296 | tf_op jit(solution)/shard_map/all_to_all | solution.py:253
  114.3 1.0 dynamic-slice_bitcast_fusion.hidden_ref
  115.3 27.7 %all-to-all-done.2.parts_ref = bf16[4,8,24,768]{3,2,1,0:T(8,128)(2,1)S(1)} async-done(((bf16[4,8,24,768]{3,2,1,0:T(8,128)(2,1)}), bf16[4,8,24,768]{3,2,1,0:T(8,128)(2,1)S(1)}, u32[]{:S(2)}, u32[]{:S(2)}) %all-to-all-start.2) | async-done | bytes 1179680 | tf_op jit(solution)/shard_map/all_to_all | solution.py:253
  143.1 1.0 finish.1
  (1 shorter events, 0.0 us)
Async XLA Ops:
  8.8 27.4 %all-to-all-start = ((bf16[16,16,256]{2,1,0:T(8,128)(2,1)}), bf16[16,16,256]{2,1,0:T(8,128)(2,1)S(1)}, u32[]{:S(2)}, u32[]{:S(2)}) async-start(bf16[16,16,256]{2,1,0:T(8,128)(2,1)} %copy.9), calls=%async_computation | async-start | bytes 262144 | tf_op jit(solution)/shard_map/all_to_all | solution.py:159
  27.0 117.1 %reduce-scatter.2.cloned.1.call-start = ((), (), s32[]{:S(2)}) async-start(), calls=%async_computation.4 | async-start | bytes 3538944 | tf_op jit(solution)/shard_map/reduce_scatter | solution.py:235
  27.0 50.5 %collective-permute-start.1 = (bf16[8,768,256]{2,1,0:T(8,128)(2,1)}, bf16[8,768,256]{2,1,0:T(8,128)(2,1)}, u32[]{:S(2)}, u32[]{:S(2)}) collective-permute-start(bf16[8,768,256]{2,1,0:T(8,128)(2,1)} %w_ref.3), channel_id=1, source_target_pairs={{0,8},{8,0},{16,24},{24,16},{32,40},{40,32},{48,56},{56,48},{64,72... | collective-permute-start | bytes 9437192 | tf_op jit(solution)/shard_map/ppermute | solution.py:154
  73.9 4.7 %collective-permute-start = (bf16[8,272,256]{2,1,0:T(8,128)(2,1)S(1)}, bf16[8,272,256]{2,1,0:T(8,128)(2,1)S(1)}, u32[]{:S(2)}, u32[]{:S(2)}) collective-permute-start(bf16[8,272,256]{2,1,0:T(8,128)(2,1)S(1)} %all_to_all.15.meta_ref.tok_ref), channel_id=1, source_target_pairs={{0,8},{8,0},{16,24},{24,16},{32,40},{40,32},{48,56},{56,48},{64,72... | collective-permute-start | bytes 3342344 | tf_op jit(solution)/shard_map/ppermute | solution.py:185
  84.6 1.0 copy-start
  85.6 23.1 %collective-permute-start.2 = (bf16[4,6,24,768]{3,2,1,0:T(8,128)(2,1)}, bf16[4,6,24,768]{3,2,1,0:T(8,128)(2,1)}, u32[]{:S(2)}, u32[]{:S(2)}) collective-permute-start(bf16[4,6,24,768]{3,2,1,0:T(8,128)(2,1)} %get-tuple-element.17), channel_id=1, source_target_pairs={{0,16},{8,24},{16,0},{24,8},{32,48},{40,56},{48,32},{56,40},{64,80... | collective-permute-start | bytes 2654216 | tf_op jit(solution)/shard_map/ppermute | solution.py:222
  93.1 15.5 %copy-start.1 = (bf16[4,6,24,768]{3,2,1,0:T(8,128)(2,1)S(1)}, bf16[4,6,24,768]{3,2,1,0:T(8,128)(2,1)}, u32[]{:S(2)}) copy-start(bf16[4,6,24,768]{3,2,1,0:T(8,128)(2,1)} %copy-done) | copy-start | bytes 2654212
  96.0 11.1 %collective-permute-start.3 = (bf16[4,2,24,768]{3,2,1,0:T(8,128)(2,1)S(1)}, bf16[4,2,24,768]{3,2,1,0:T(8,128)(2,1)S(1)}, u32[]{:S(2)}, u32[]{:S(2)}) collective-permute-start(bf16[4,2,24,768]{3,2,1,0:T(8,128)(2,1)S(1)} %get-tuple-element.21), channel_id=1, source_target_pairs={{0,112},{8,120},{16,32},{24,40},{32,16},{40,24},{48,64},{56,72},{6... | collective-permute-start | bytes 884744 | tf_op jit(solution)/shard_map/ppermute | solution.py:238
  110.8 32.3 %all-to-all-start.2 = ((bf16[4,8,24,768]{3,2,1,0:T(8,128)(2,1)}), bf16[4,8,24,768]{3,2,1,0:T(8,128)(2,1)S(1)}, u32[]{:S(2)}, u32[]{:S(2)}) async-start(bf16[4,8,24,768]{3,2,1,0:T(8,128)(2,1)} %pair_sum.1), calls=%async_computation.2 | async-start | bytes 2359296 | tf_op jit(solution)/shard_map/all_to_all | solution.py:253
Sparse Core Ops, SparseCore 0:
  93.2 41.8 reduce-scatter.1
